TPU v7x, 256 devices: a whole 4x4x8 slice. The times are simulated.
256 devices in a mesh: seq: 64 (over z, y, core), batch: 4 (over x).
Axes of the slice: x: 4, y: 4, z: 8, core: 2. Of those that a mesh axis runs over, the one named last changes fastest.
Arguments:
- convolution_input: bfloat16 [4, 32768, 768], P('batch', 'seq'), may hold values from -16 to 16
- interval_index: int32 [4, 32768], P('batch', 'seq'), may hold values from 0 to 3, never falling along the last dimension, each value on 1 to 16384 neighbouring positions
- owner_lists: int32 [4, 16384, 1], P('batch', 'seq'), may hold values from 0 to 63; in each aligned block of 256 rows (0 to 255, 256 to 511, ..., all dimensions but the last counted through in order) at most 8 rows name the same one
- dilated_kernel_weight: bfloat16 [768, 3, 768], replicated, may hold values from -0.125 to 0.125
- proj_weight: bfloat16 [768, 1536], replicated, may hold values from -0.21875 to 0.21875
- owner_grads: bfloat16 [4, 64, 64, 8, 1536], P('batch', 'seq'), may hold values from -6 to 6
Outputs:
- owner_rows: bfloat16 [4, 64, 64, 8, 1536], P('batch', 'seq')
- input_grad: bfloat16 [4, 32768, 768], P('batch', 'seq')
- conv_grad: float32 [768, 3, 768], P('seq')
Inputs may be any that keep to these rules, and one draw needn't show every extreme that they name: `interval_index`: positions of one interval are contiguous, ids never fall along a row. `owner_lists`: among the 256 token rows of one device, at most 8 name the same owner, and 8 is reached.
All inputs are finite; a program needn't handle non-finite values.
Results may differ from a plain program's by a relative error of at most 0.018.
Values may be sent and summed in bfloat16 or wider, within the bound.
No kernel may reach another device: no remote copies, remote signals or barrier semaphores. Data moves between devices by JAX's collectives and lax.ppermute only.
A program may use at most 128 MiB of HBM per device.

v0:
```python
import jax
import jax.numpy as jnp
from jax import lax
from jax.sharding import PartitionSpec as P

DILATION_STEP = 32


def with_halo(array, sides, width):
    for axis, dim in sides:
        size, length = (lax.axis_size(axis), array.shape[dim])
        up = [(i, (i + 1) % size) for i in range(size - 1)]
        down = [(j, i) for i, j in up]
        last = lax.slice_in_dim(array, length - width, length, axis=dim)
        initial = lax.slice_in_dim(array, 0, width, axis=dim)
        before = lax.ppermute(last, axis, up)
        after = lax.ppermute(initial, axis, down)
        array = jnp.concatenate([before, array, after], axis=dim)
    return array


def gelu_exact(value):
    return 0.5 * value * (1.0 + jax.scipy.special.erf(value * 0.7071067811865476))


def gelu_slope(value):
    return (
        0.5 * (1.0 + jax.scipy.special.erf(value * 0.7071067811865476))
        + value * jnp.exp(-0.5 * value * value) * 0.3989422804014327
    )


def body(
    convolution_input, interval_index, owner_lists, dilated_kernel_weight, proj_weight, owner_grads
):
    group_rows, count_of_rows, channels = convolution_input.shape
    owner_total = lax.axis_size("seq")
    capacity = owner_grads.shape[3]
    tap_shifts = (-DILATION_STEP, 0, DILATION_STEP)
    input_with_margin, segment_with_margin = (
        with_halo(convolution_input, (("seq", 1),), DILATION_STEP),
        with_halo(interval_index, (("seq", 1),), DILATION_STEP),
    )
    same_segment = [
        segment_with_margin[
            :, DILATION_STEP + tap_shift : DILATION_STEP + tap_shift + count_of_rows
        ]
        == interval_index
        for tap_shift in tap_shifts
    ]
    tap_products = jnp.einsum(
        "btc,cd->btd",
        input_with_margin,
        dilated_kernel_weight.reshape(channels, 3 * channels),
        preferred_element_type=jnp.float32,
    )
    preact = jnp.zeros((group_rows, count_of_rows, channels), jnp.float32)
    for kernel_tap_index in range(3):
        tap_shift = tap_shifts[kernel_tap_index]
        window_slice = tap_products[
            :,
            DILATION_STEP + tap_shift : DILATION_STEP + tap_shift + count_of_rows,
            kernel_tap_index * channels : (kernel_tap_index + 1) * channels,
        ]
        preact = preact + jnp.where(
            same_segment[kernel_tap_index][..., None], window_slice, jnp.float32(0.0)
        )
    hidden = (convolution_input.astype(jnp.float32) + gelu_exact(preact)).astype(jnp.bfloat16)
    pooled = (
        jnp.sum(
            hidden.reshape(group_rows, count_of_rows // 2, 2, channels).astype(jnp.float32), axis=2
        )
        * 0.5
    ).astype(jnp.bfloat16)
    owners = owner_lists[..., 0]
    onehot = (owners[..., None] == jnp.arange(owner_total, dtype=jnp.int32)).astype(jnp.int32)
    slot_rank = jnp.sum((jnp.cumsum(onehot, axis=1) - onehot) * onehot, axis=-1)
    slots = owners * capacity + slot_rank
    local_grads = owner_grads[:, 0]
    projected = jnp.einsum(
        "btc,ce->bte", pooled, proj_weight, preferred_element_type=jnp.float32
    ).astype(jnp.bfloat16)

    def place_one(slot_row, value_row):
        return (
            jnp.zeros((owner_total * capacity, value_row.shape[-1]), jnp.bfloat16)
            .at[slot_row]
            .set(value_row)
        )

    placed = jax.vmap(place_one)(slots, projected)
    received = lax.all_to_all(
        placed.reshape(group_rows, owner_total, capacity, projected.shape[-1]),
        "seq",
        split_axis=1,
        concat_axis=1,
        tiled=True,
    )
    returned = lax.all_to_all(local_grads, "seq", split_axis=1, concat_axis=1, tiled=True)
    flat_rows = returned.reshape(group_rows, owner_total * capacity, returned.shape[-1])
    token_grad = jnp.einsum(
        "bte,ce->btc",
        jnp.take_along_axis(flat_rows, slots[..., None], axis=1),
        proj_weight,
        preferred_element_type=jnp.float32,
    ).astype(jnp.bfloat16)
    owner_rows = received[:, None]
    hidden_grad = jnp.repeat(token_grad.astype(jnp.float32) * 0.5, 2, axis=1)
    preactivation_gradient = (hidden_grad * gelu_slope(preact)).astype(jnp.bfloat16)
    gradient_with_margin = with_halo(preactivation_gradient, (("seq", 1),), DILATION_STEP)
    spread_gradient = jnp.einsum(
        "btd,ckd->btkc",
        gradient_with_margin,
        dilated_kernel_weight,
        preferred_element_type=jnp.float32,
    )
    input_grad = hidden_grad
    for kernel_tap_index in range(3):
        tap_shift = tap_shifts[kernel_tap_index]
        shifted_rows = spread_gradient[
            :,
            DILATION_STEP - tap_shift : DILATION_STEP - tap_shift + count_of_rows,
            kernel_tap_index,
        ]
        input_grad = input_grad + jnp.where(
            same_segment[2 - kernel_tap_index][..., None], shifted_rows, jnp.float32(0.0)
        )
    masked_grads = [
        jnp.where(
            same_segment[kernel_tap_index][..., None],
            preactivation_gradient,
            jnp.zeros_like(preactivation_gradient),
        )
        for kernel_tap_index in range(3)
    ]
    kernel_taps = []
    for kernel_tap_index in range(3):
        tap_shift = tap_shifts[kernel_tap_index]
        kernel_taps.append(
            jnp.einsum(
                "btc,btd->cd",
                input_with_margin[
                    :, DILATION_STEP + tap_shift : DILATION_STEP + tap_shift + count_of_rows
                ],
                masked_grads[kernel_tap_index],
                preferred_element_type=jnp.float32,
            )
        )
    local_total = jnp.stack(kernel_taps, axis=1)
    grad_share = lax.psum_scatter(local_total, "seq", scatter_dimension=0, tiled=True)
    conv_grad = lax.psum(grad_share.astype(jnp.bfloat16), "batch").astype(jnp.float32)
    return (owner_rows, input_grad.astype(jnp.bfloat16), conv_grad)


def solution(mesh):
    placed = (
        P("batch", "seq", None),
        P("batch", "seq"),
        P("batch", "seq", None),
        P(),
        P(),
        P("batch", "seq", None, None, None),
    )
    return jax.shard_map(
        body,
        mesh=mesh,
        in_specs=placed,
        out_specs=(
            P("batch", "seq", None, None, None),
            P("batch", "seq", None),
            P("seq", None, None),
        ),
        check_vma=False,
    )
```

profile of v0, /device:TPU:6, one launch (start us, length us, event | category | flops | bytes accessed | tf_op | source)
XLA Modules:
  0.0 442.2 jit_solution(17469007772250384659)
XLA Ops:
  0.7 12.6 %all-to-all-start.1 = ((bf16[1,64,8,1536]{3,2,0,1:T(8,128)(2,1)}), bf16[1,64,8,1536]{3,2,0,1:T(8,128)(2,1)}, u32[]{:S(2)}, u32[]{:S(2)}) async-start(bf16[1,64,8,1536]{3,2,0,1:T(8,128)(2,1)} %bitcast.97), calls=%async_computation.1 | async-start | bytes 3145728 | tf_op jit(solution)/shard_map/all_to_all | solution.py:99
  14.6 3.0 collective-permute-start.1
  17.7 3.1 collective-permute-start
  23.3 6.1 %copy.20 = bf16[768,3,768]{0,2,1:T(8,128)(2,1)} copy(bf16[768,3,768]{2,0,1:T(8,128)(2,1)} %param.9) | data formatting | bytes 7077888 | tf_op args[3]
  31.1 6.6 %convolution_bitcast_fusion = f32[1,576,2304]{2,1,0:T(8,128)} fusion(bf16[768,2304]{0,1:T(8,128)(2,1)} %bitcast.96, bf16[1,32,768]{2,1,0:T(8,128)(2,1)S(1)} %collective-permute-done.2, bf16[1,512,768]{2,1,0:T(8,128)(2,1)S(1)} %copy-done.5, bf16[1,32,768]{2,1,0:T(8,128)(2,1)S(1)} %collective-permute-done.1), kind=kOutput, calls=%fused_computation.3 | convolution fusion | flops 2041085952 | bytes 9732096 | tf_op jit(solution)/shard_map/btc,cd->btd/dot_general | solution.py:51
  37.7 15.6 %all-to-all-done.1 = bf16[1,64,8,1536]{3,2,0,1:T(8,128)(2,1)} async-done(((bf16[1,64,8,1536]{3,2,0,1:T(8,128)(2,1)}), bf16[1,64,8,1536]{3,2,0,1:T(8,128)(2,1)}, u32[]{:S(2)}, u32[]{:S(2)}) %all-to-all-start.1) | async-done | bytes 1572896 | tf_op jit(solution)/shard_map/all_to_all | solution.py:99
  53.3 4.5 %gather_fusion = bf16[256,1536]{1,0:T(8,128)(2,1)} fusion(bf16[512,1536]{1,0:T(8,128)(2,1)} %bitcast.16, s32[1024]{0:T(1024)S(1)} %pad_clamp_fusion), kind=kCustom, calls=%fused_computation | custom fusion | bytes 1573888 | tf_op jit(solution)/shard_map/jit(take_along_axis)/gather | solution.py:103
  57.8 2.0 fusion.14
  59.7 1.7 broadcast_in_dim.87
  61.4 3.1 broadcast_in_dim.88
  64.6 3.4 fusion.5
  68.0 2.2 convolution_bitcast_fusion.3
  71.7 3.0 reshape.383
  74.8 3.3 reduce_sum.22
  78.1 1.7 convolution_convert_fusion
  79.7 3.7 scatter_custom_fusion
  83.4 12.5 %all-to-all-start = ((bf16[1,64,8,1536]{3,2,0,1:T(8,128)(2,1)}), bf16[1,64,8,1536]{3,2,0,1:T(8,128)(2,1)}, u32[]{:S(2)}, u32[]{:S(2)}) async-start(bf16[1,64,8,1536]{3,2,0,1:T(8,128)(2,1)} %bitcast.95), calls=%async_computation | async-start | bytes 3145728 | tf_op jit(solution)/shard_map/all_to_all | solution.py:92
  97.3 3.8 collective-permute-start.4
  101.1 2.0 convolution_bitcast_fusion.2
  104.8 3.4 pad_maximum_fusion
  108.1 309.2 %all-reduce.2 = bf16[768,3,768]{2,0,1:T(8,128)(2,1)} all-reduce(f32[768,3,768]{2,0,1:T(8,128)} %pad_maximum_fusion), channel_id=2, replica_groups=mesh['seq'=64,'batch'=4] {'seq'}, use_global_device_ids=true, to_apply=%region_5.6.clone | all-reduce | flops 1769472 | bytes 10616832
  418.2 14.8 %psum.7 = bf16[12,3,768]{2,0,1:T(8,128)(2,1)S(1)} all-reduce(bf16[12,3,768]{2,0,1:T(8,128)(2,1)S(1)} %dynamic-slice_convert_fusion), channel_id=1, replica_groups=mesh['seq'=64,'batch'=4] {'batch'}, use_global_device_ids=true, to_apply=%region_6.7 | all-reduce | flops 27648 | bytes 110592 | tf_op jit(solution)/shard_map/psum | solution.py:151
  433.8 4.4 %convolution_bitcast_fusion.1 = f32[1,576,3,768]{3,1,2,0:T(8,128)S(1)} fusion(bf16[768,3,768]{2,0,1:T(8,128)(2,1)} %param.9, bf16[1,32,768]{2,1,0:T(8,128)(2,1)} %collective-permute-done.5, bf16[1,512,768]{2,1,0:T(8,128)(2,1)S(1)} %copy-done.4, bf16[1,32,768]{2,1,0:T(8,128)(2,1)} %collective-permute-done.4), kind=kOutput, calls=%fused_computation.5 | convolution fusion | flops 2041085952 | bytes 9732096 | tf_op jit(solution)/shard_map/btd,ckd->btkc/dot_general | solution.py:111
  439.5 2.7 copy.29
  (54 shorter events, 12.1 us)
Async XLA Ops:
  0.6 57.2 %copy-start = (bf16[768,1536]{1,0:T(8,128)(2,1)S(1)}, bf16[768,1536]{1,0:T(8,128)(2,1)}, u32[]{:S(2)}) copy-start(bf16[768,1536]{1,0:T(8,128)(2,1)} %param.10) | copy-start | bytes 7077892
  0.6 12.7 %copy-start.5 = (bf16[1,512,768]{2,1,0:T(8,128)(2,1)S(1)}, bf16[1,512,768]{2,1,0:T(8,128)(2,1)}, u32[]{:S(2)}) copy-start(bf16[1,512,768]{2,1,0:T(8,128)(2,1)} %param.6) | copy-start | bytes 2359300
  0.7 17.0 %copy-start.8 = (s32[1,512]{1,0:T(1,128)S(1)}, s32[1,512]{1,0:T(1,128)}, u32[]{:S(2)}) copy-start(s32[1,512]{1,0:T(1,128)} %param.7) | copy-start | bytes 6148
  0.7 21.5 %copy-start.7 = (s32[1,256,1]{1,2,0:T(1,128)S(1)}, s32[1,256,1]{1,2,0:T(1,128)}, u32[]{:S(2)}) copy-start(s32[1,256,1]{1,2,0:T(1,128)} %param.8) | copy-start | bytes 3076
  0.7 52.6 %all-to-all-start.1 = ((bf16[1,64,8,1536]{3,2,0,1:T(8,128)(2,1)}), bf16[1,64,8,1536]{3,2,0,1:T(8,128)(2,1)}, u32[]{:S(2)}, u32[]{:S(2)}) async-start(bf16[1,64,8,1536]{3,2,0,1:T(8,128)(2,1)} %bitcast.97), calls=%async_computation.1 | async-start | bytes 3145728 | tf_op jit(solution)/shard_map/all_to_all | solution.py:99
  13.3 17.8 %collective-permute-start.2 = (bf16[1,32,768]{2,1,0:T(8,128)(2,1)S(1)}, bf16[1,32,768]{2,1,0:T(8,128)(2,1)S(1)}, u32[]{:S(2)}, u32[]{:S(2)}) collective-permute-start(bf16[1,32,768]{2,1,0:T(8,128)(2,1)S(1)} %get-tuple-element.21), channel_id=1, source_target_pairs={{4,0},{8,4},{12,8},{16,12},{20,16},{24,20},{28,24},{32,28},{36,32}... | collective-permute-start | bytes 147464 | tf_op jit(solution)/shard_map/ppermute | solution.py:17
  14.6 16.5 %collective-permute-start.1 = (bf16[1,32,768]{2,1,0:T(8,128)(2,1)S(1)}, bf16[1,32,768]{2,1,0:T(8,128)(2,1)S(1)}, u32[]{:S(2)}, u32[]{:S(2)}) collective-permute-start(bf16[1,32,768]{2,1,0:T(8,128)(2,1)S(1)} %get-tuple-element.20), channel_id=1, source_target_pairs={{0,4},{4,8},{8,12},{12,16},{16,20},{20,24},{24,28},{28,32},{32,36}... | collective-permute-start | bytes 147464 | tf_op jit(solution)/shard_map/ppermute | solution.py:16
  17.7 13.2 %collective-permute-start = (s32[1,32]{1,0:T(1,128)S(1)}, s32[1,32]{1,0:T(1,128)S(1)}, u32[]{:S(2)}, u32[]{:S(2)}) collective-permute-start(s32[1,32]{1,0:T(1,128)S(1)} %get-tuple-element.23), channel_id=1, source_target_pairs={{0,4},{4,8},{8,12},{12,16},{16,20},{20,24},{24,28},{28,32},{32,36}... | collective-permute-start | bytes 392 | tf_op jit(solution)/shard_map/ppermute | solution.py:16
  20.9 10.1 %collective-permute-start.3 = (s32[1,32]{1,0:T(1,128)S(1)}, s32[1,32]{1,0:T(1,128)S(1)}, u32[]{:S(2)}, u32[]{:S(2)}) collective-permute-start(s32[1,32]{1,0:T(1,128)S(1)} %get-tuple-element.22), channel_id=1, source_target_pairs={{4,0},{8,4},{12,8},{16,12},{20,16},{24,20},{28,24},{32,28},{36,32}... | collective-permute-start | bytes 392 | tf_op jit(solution)/shard_map/ppermute | solution.py:17
  23.3 6.1 %copy-start.9 = (u32[256]{0:T(256)S(1)}, u32[256]{0:T(256)}, u32[]{:S(2)}) copy-start(u32[256]{0:T(256)} %constant.51) | copy-start | bytes 3076
  67.9 2.3 copy-start.3
  83.4 17.7 %copy-start.4 = (bf16[1,512,768]{2,1,0:T(8,128)(2,1)S(1)}, bf16[1,512,768]{2,1,0:T(8,128)(2,1)}, u32[]{:S(2)}) copy-start(bf16[1,512,768]{2,1,0:T(8,128)(2,1)} %copy-done.3) | copy-start | bytes 2359300
  83.4 356.1 %all-to-all-start = ((bf16[1,64,8,1536]{3,2,0,1:T(8,128)(2,1)}), bf16[1,64,8,1536]{3,2,0,1:T(8,128)(2,1)}, u32[]{:S(2)}, u32[]{:S(2)}) async-start(bf16[1,64,8,1536]{3,2,0,1:T(8,128)(2,1)} %bitcast.95), calls=%async_computation | async-start | bytes 3145728 | tf_op jit(solution)/shard_map/all_to_all | solution.py:92
  96.0 337.8 %collective-permute-start.5 = (bf16[1,32,768]{2,1,0:T(8,128)(2,1)S(1)}, bf16[1,32,768]{2,1,0:T(8,128)(2,1)}, u32[]{:S(2)}, u32[]{:S(2)}) collective-permute-start(bf16[1,32,768]{2,1,0:T(8,128)(2,1)S(1)} %get-tuple-element.19), channel_id=1, source_target_pairs={{4,0},{8,4},{12,8},{16,12},{20,16},{24,20},{28,24},{32,28},{36,32}... | collective-permute-start | bytes 147464 | tf_op jit(solution)/shard_map/ppermute | solution.py:17
  97.3 5.8 %copy-start.6 = (bf16[1,512,768]{2,1,0:T(8,128)(2,1)S(1)}, bf16[1,512,768]{2,1,0:T(8,128)(2,1)}, u32[]{:S(2)}) copy-start(bf16[1,512,768]{2,1,0:T(8,128)(2,1)} %param.6) | copy-start | bytes 2359300
  97.3 336.5 %collective-permute-start.4 = (bf16[1,32,768]{2,1,0:T(8,128)(2,1)S(1)}, bf16[1,32,768]{2,1,0:T(8,128)(2,1)}, u32[]{:S(2)}, u32[]{:S(2)}) collective-permute-start(bf16[1,32,768]{2,1,0:T(8,128)(2,1)S(1)} %get-tuple-element.18), channel_id=1, source_target_pairs={{0,4},{4,8},{8,12},{12,16},{16,20},{20,24},{24,28},{28,32},{32,36}... | collective-permute-start | bytes 147464 | tf_op jit(solution)/shard_map/ppermute | solution.py:16
  103.1 1.7 copy-start.2
  433.8 4.4 %copy-start.1 = (f32[1,512,768]{2,1,0:T(8,128)S(1)}, f32[1,512,768]{2,1,0:T(8,128)}, u32[]{:S(2)}) copy-start(f32[1,512,768]{2,1,0:T(8,128)} %broadcast_in_dim.88) | copy-start | bytes 4718596
where the time goes:
time: 446 us; the launch traced here: 442 us
  blocking collectives  324 us (73%)
  starting transfers between devices  39 us (9%)
  local copies, waits for them, and re-layouts  28.4 us (6%)
  matrix products  19.7 us (4%)
  waiting for transfers between devices  15.6 us (3%)
  other arithmetic  13.8 us (3%)
    unnamed x1, blocking collectives  309 us
    all_to_all x1, waiting for transfers between devices, body(): lax.all_to_all(local_grads, 'seq', split_axis=1, concat_axis=1, tiled=True)  15.6 us
    psum x1, blocking collectives, body(): lax.psum(grad_share.astype(jnp.bfloat16), 'batch').astype(jnp.float32)  14.8 us
    all_to_all x1, starting transfers between devices, body(): lax.all_to_all(local_grads, 'seq', split_axis=1, concat_axis=1, tiled=True)  12.6 us
    all_to_all x1, starting transfers between devices, body(): lax.all_to_all(placed.reshape(group_rows, owner_total, capacity, projecte...  12.5 us
    unnamed x24, local copies, waits for them, and re-layouts  10.9 us
    ppermute x3, starting transfers between devices, with_halo(): before = lax.ppermute(last, axis, up)  9.93 us
  transfers between devices with their start and end apart: 8, of which 1 were waited for; matrix products, arithmetic and copies ran while one was open for 6% of the time, Pallas kernels for 0%

commit v1 on v0

v1 whole, which is shorter than its diff:
```python
import jax
import jax.numpy as jnp
import numpy as np
from jax import lax
from jax.sharding import Mesh, PartitionSpec as P

DIL = 32
SEQ = ("z", "y", "core")
BF = jnp.bfloat16
F32 = jnp.float32


def gelu_exact(value):
    return 0.5 * value * (1.0 + jax.scipy.special.erf(value * 0.7071067811865476))


def gelu_slope(value):
    return (
        0.5 * (1.0 + jax.scipy.special.erf(value * 0.7071067811865476))
        + value * jnp.exp(-0.5 * value * value) * 0.3989422804014327
    )


def seq_shift(array, sizes, step):
    count = int(np.prod(sizes))
    if step > 0:
        pairs = [(i, i + 1) for i in range(count - 1)]
    else:
        pairs = [(i + 1, i) for i in range(count - 1)]
    return lax.ppermute(array, SEQ, pairs)


def exchange_sum(parts, axis):
    moved = lax.all_to_all(parts, axis, 0, 0, tiled=True)
    return jnp.sum(moved.astype(F32), axis=0)


def body(x, ids, owners, weight, proj, grads):
    nz, ny, nc, nx = (lax.axis_size(a) for a in ("z", "y", "core", "batch"))
    x, ids, owners, grads = x[0], ids[0], owners[0, :, 0], grads[0, 0]
    rows, ch = x.shape
    tokens = owners.shape[0]
    devs, cap, wide = grads.shape
    slots_n = devs * cap
    core = lax.axis_index("core")
    sizes = (nz, ny, nc)
    back = jnp.dot(grads.reshape(slots_n, wide), proj.T, preferred_element_type=F32).astype(BF)
    returned = lax.all_to_all(back, SEQ, 0, 0, tiled=True)
    x_ext = jnp.concatenate(
        [seq_shift(x[-DIL:], sizes, 1), x, seq_shift(x[:DIL], sizes, -1)], axis=0
    )
    seq_idx = lax.axis_index(SEQ)
    before = jnp.where(seq_idx == 0, -1, seq_shift(ids[-DIL:], sizes, 1))
    after = jnp.where(seq_idx == devs - 1, -1, seq_shift(ids[:DIL], sizes, -1))
    ids_ext = jnp.concatenate([before, ids, after])
    same = [ids_ext[o : o + rows] == ids for o in (0, DIL, 2 * DIL)]
    w3 = weight.transpose(1, 0, 2)
    zero = jnp.zeros((), BF)
    taps = [jnp.where(same[k][:, None], x_ext[k * DIL : k * DIL + rows], zero) for k in range(3)]
    preact = jnp.dot(
        jnp.concatenate(taps, axis=1), w3.reshape(3 * ch, ch), preferred_element_type=F32
    )
    hidden = (x.astype(F32) + gelu_exact(preact)).astype(BF)
    earlier = jnp.arange(tokens)[None, :] < jnp.arange(tokens)[:, None]
    rank = jnp.sum(((owners[:, None] == owners[None, :]) & earlier).astype(jnp.int32), axis=1)
    slot = owners * cap + rank
    pick = (slot[:, None] == jnp.arange(slots_n)[None, :]).astype(BF)
    pair = jnp.where(
        (jnp.arange(rows)[None, :] // 2) == jnp.arange(tokens)[:, None], 0.5, 0.0
    ).astype(BF)
    pooled = jnp.dot(pair, hidden, preferred_element_type=F32).astype(BF)
    placed = jnp.dot(pick.T, pooled, preferred_element_type=F32).astype(BF)
    received = lax.all_to_all(placed, SEQ, 0, 0, tiled=True)
    owner_rows = jnp.dot(received, proj, preferred_element_type=F32).astype(BF)
    token_grad = jnp.dot(pick, returned, preferred_element_type=F32).astype(BF)
    hidden_grad = jnp.dot(pair.T, token_grad, preferred_element_type=F32)
    pre_grad = (hidden_grad * gelu_slope(preact)).astype(BF)
    g_ext = jnp.concatenate(
        [seq_shift(pre_grad[-DIL:], sizes, 1), pre_grad, seq_shift(pre_grad[:DIL], sizes, -1)],
        axis=0,
    )
    g_taps = [
        jnp.where(same[2 - k][:, None], g_ext[(2 - k) * DIL : (2 - k) * DIL + rows], zero)
        for k in range(3)
    ]
    input_grad = hidden_grad
    for k in range(3):
        input_grad = input_grad + jnp.dot(g_taps[k], w3[k].T, preferred_element_type=F32)
    own = ch // devs
    rest = own // nx
    order = np.arange(ch).reshape(nz, ny, nc, nx, rest).transpose(2, 3, 1, 0, 4).reshape(ch)
    perm = jnp.asarray(np.eye(ch, dtype=np.float32)[:, order], BF)
    parts = [
        lax.dot_general(
            jnp.dot(taps[k], perm, preferred_element_type=F32).astype(BF),
            pre_grad,
            (((0,), (0,)), ((), ())),
            preferred_element_type=F32,
        )
        for k in range(3)
    ]
    half = ch // 2
    total = jnp.stack(parts, axis=0).reshape(3, nc, half, ch)
    mine = lax.dynamic_index_in_dim(total, core, 1, False)
    other = lax.dynamic_index_in_dim(total, 1 - core, 1, False).astype(BF)
    chip = (mine + lax.ppermute(other, "core", [(0, 1), (1, 0)]).astype(F32)).astype(BF)
    chip = chip.reshape(3, nx, half // nx, ch).transpose(1, 0, 2, 3)
    by_x = exchange_sum(chip, "batch").astype(BF)
    by_x = by_x.reshape(3, ny, half // nx // ny, ch).transpose(1, 0, 2, 3)
    by_y = exchange_sum(by_x, "y").astype(BF)
    by_y = by_y.reshape(3, nz, rest, ch).transpose(1, 0, 2, 3)
    by_z = exchange_sum(by_y, "z").astype(BF)
    everyone = lax.all_gather(by_z, "batch", axis=0, tiled=False)
    conv_grad = everyone.transpose(0, 2, 1, 3).reshape(own, 3, ch).astype(F32)
    return (
        owner_rows.reshape(1, 1, devs, cap, wide),
        input_grad.astype(BF)[None],
        conv_grad,
    )


def solution(mesh):
    fine = Mesh(mesh.devices.reshape(8, 4, 2, 4), ("z", "y", "core", "batch"))
    return jax.shard_map(
        body,
        mesh=fine,
        in_specs=(
            P("batch", SEQ, None),
            P("batch", SEQ),
            P("batch", SEQ, None),
            P(),
            P(),
            P("batch", SEQ, None, None, None),
        ),
        out_specs=(
            P("batch", SEQ, None, None, None),
            P("batch", SEQ, None),
            P(SEQ, None, None),
        ),
        check_vma=False,
    )
```

time: 446 us -> 186 us (0.42)
  blocking collectives: 324 us -> 37.6 us
  waiting for transfers between devices: 15.6 us -> 39.3 us
  matrix products: 19.7 us -> 41.8 us
  local copies, waits for them, and re-layouts: 28.4 us -> 10.5 us
  starting transfers between devices: 39 us -> 45.5 us
  other arithmetic: 13.8 us -> 9.18 us
    unnamed x1 -> x0, blocking collectives: 309 us -> none
    all_to_all x0 -> x1, blocking collectives: none -> 25.7 us  [exchange_sum(): moved = lax.all_to_all(parts, axis, 0, 0, tiled=True)]
    dot_general x7 -> x11, matrix products: 19.7 us -> 41.8 us  [the longest x3 14.3 us: body(): lax.dot_general(jnp.dot(taps[k], perm, preferred_element_type=F32).astype...]
    all_to_all x2 -> x4, waiting for transfers between devices: 15.6 us -> 35.3 us  [the longest x1 16 us: body(): returned = lax.all_to_all(back, SEQ, 0, 0, tiled=True)]
    psum x1 -> x0, blocking collectives: 14.8 us -> none  [body(): lax.psum(grad_share.astype(jnp.bfloat16), 'batch').astype(jnp.float32)]
    all_gather x0 -> x1, blocking collectives: none -> 11.9 us  [body(): everyone = lax.all_gather(by_z, 'batch', axis=0, tiled=False)]
    all_to_all x2 -> x4, starting transfers between devices: 25.2 us -> 33 us  [the longest x1 14.9 us: body(): returned = lax.all_to_all(back, SEQ, 0, 0, tiled=True)]
    unnamed x24 -> x18, local copies, waits for them, and re-layouts: 10.9 us -> 4.09 us
  transfers between devices with their start and end apart: 8 -> 11, of which waited for: 1 -> 5; matrix products, arithmetic and copies ran while one was open for 6% -> 14% of each run, Pallas kernels for 0% -> 0%
where the time goes in v1:
time: 186 us; the launch traced here: 185 us
  starting transfers between devices  45.5 us (24%)
  matrix products  41.8 us (22%)
  waiting for transfers between devices  39.3 us (21%)
  blocking collectives  37.6 us (20%)
  local copies, waits for them, and re-layouts  10.5 us (6%)
  other arithmetic  9.18 us (5%)
    all_to_all x1, blocking collectives, exchange_sum(): moved = lax.all_to_all(parts, axis, 0, 0, tiled=True)  25.7 us
    all_to_all x1, waiting for transfers between devices, body(): returned = lax.all_to_all(back, SEQ, 0, 0, tiled=True)  16 us
    all_to_all x1, starting transfers between devices, body(): returned = lax.all_to_all(back, SEQ, 0, 0, tiled=True)  14.9 us
    dot_general x3, matrix products, body(): lax.dot_general(jnp.dot(taps[k], perm, preferred_element_type=F32).astype...  14.3 us
    all_to_all x2, starting transfers between devices, exchange_sum(): moved = lax.all_to_all(parts, axis, 0, 0, tiled=True)  12.5 us
    ppermute x6, starting transfers between devices, seq_shift(): return lax.ppermute(array, SEQ, pairs)  12.5 us
    all_gather x1, blocking collectives, body(): everyone = lax.all_gather(by_z, 'batch', axis=0, tiled=False)  11.9 us
    all_to_all x2, waiting for transfers between devices, exchange_sum(): moved = lax.all_to_all(parts, axis, 0, 0, tiled=True)  9.87 us
  transfers between devices with their start and end apart: 11, of which 5 were waited for; matrix products, arithmetic and copies ran while one was open for 14% of the time, Pallas kernels for 0%

profile of v1, /device:TPU:6, one launch (start us, length us, event | category | flops | bytes accessed | tf_op | source)
XLA Modules:
  0.0 184.7 jit_solution(17263649449852176419)
XLA Ops:
  4.1 3.8 %collective-permute-start = (s32[32]{0:T(128)S(1)}, s32[32]{0:T(128)S(1)}, u32[]{:S(2)}, u32[]{:S(2)}) collective-permute-start(s32[32]{0:T(128)S(1)} %get-tuple-element.13), channel_id=1, source_target_pairs={{0,4},{4,8},{8,12},{12,16},{16,20},{20,24},{24,28},{28,32},{32,36}... | collective-permute-start | bytes 392 | tf_op jit(solution)/shard_map/ppermute | solution.py:30
  10.5 3.7 %fusion.20 = bf16[64,8,768]{2,1,0:T(8,128)(2,1)} fusion(bf16[768,1536]{1,0:T(8,128)(2,1)S(1)} %copy-done, bf16[1,1,64,8,1536]{4,3,2,1,0:T(8,128)(2,1)} %param.12), kind=kOutput, calls=%fused_computation.30 | convolution fusion | flops 1208352768 | bytes 4718592 | tf_op jit(solution)/shard_map/dot_general | solution.py:47
  14.2 14.9 %all-to-all-start.1 = ((bf16[64,8,768]{2,1,0:T(8,128)(2,1)}), bf16[64,8,768]{2,1,0:T(8,128)(2,1)}, u32[]{:S(2)}, u32[]{:S(2)}) async-start(bf16[64,8,768]{2,1,0:T(8,128)(2,1)} %fusion.20), calls=%async_computation.1 | async-start | bytes 1572864 | tf_op jit(solution)/shard_map/all_to_all | solution.py:48
  31.2 5.1 %fusion.2 = f32[512,768]{1,0:T(8,128)} fusion(bf16[2304,768]{1,0:T(8,128)(2,1)} %bitcast.102, bf16[512,768]{1,0:T(8,128)(2,1)S(1)} %get-tuple-element.6, bf16[512,768]{1,0:T(8,128)(2,1)S(1)} %bitcast.100, bf16[512,768]{1,0:T(8,128)(2,1)S(1)} %get-tuple-element.5), kind=kOutput, calls=%fused_computation.7 | convolution fusion | flops 1819017216 | bytes 7471104 | tf_op jit(solution)/shard_map/dot_general | solution.py:60
  36.4 16.0 %all-to-all-done.1 = bf16[64,8,768]{2,1,0:T(8,128)(2,1)} async-done(((bf16[64,8,768]{2,1,0:T(8,128)(2,1)}), bf16[64,8,768]{2,1,0:T(8,128)(2,1)}, u32[]{:S(2)}, u32[]{:S(2)}) %all-to-all-start.1) | async-done | bytes 786464 | tf_op jit(solution)/shard_map/all_to_all | solution.py:48
  52.3 4.1 %fusion.14 = (bf16[512,768]{1,0:T(8,128)(2,1)}, f32[512,768]{1,0:T(8,128)}) fusion(f32[512,768]{1,0:T(8,128)} %fusion.2, bf16[64,8,768]{2,1,0:T(8,128)(2,1)} %all-to-all-done.1, s32[256]{0:T(256)S(1)} %multiply_add_fusion, s32[512]{0:T(512)S(1)} %add_select_fusion), kind=kOutput, calls=%fused_computation.19 | convolution fusion | flops 407306240 | bytes 4721664 | tf_op jit(solution)/shard_map/dot_general | solution.py:76
  56.4 4.9 %fusion.27 = f32[768,768]{1,0:T(8,128)} fusion(bf16[512,768]{1,0:T(8,128)(2,1)} %get-tuple-element.15, bf16[512,768]{1,0:T(8,128)(2,1)} %copy-done.6, bf16[768,768]{1,0:T(8,128)(2,1)} %constant.69.clone), kind=kOutput, calls=%fused_computation.35 | convolution fusion | flops 1208352768 | bytes 5111808 | tf_op jit(solution)/shard_map/dot_general | solution.py:94
  61.3 4.4 %fusion.26 = f32[768,768]{1,0:T(8,128)} fusion(bf16[512,768]{1,0:T(8,128)(2,1)} %get-tuple-element.15, bf16[768,768]{1,0:T(8,128)(2,1)} %constant.69.clone, bf16[1,512,768]{2,1,0:T(8,128)(2,1)S(1)} %copy-done.3), kind=kOutput, calls=%fused_computation.34 | convolution fusion | flops 1208352768 | bytes 5111808 | tf_op jit(solution)/shard_map/dot_general | solution.py:94
  65.7 4.9 %fusion.25 = f32[768,768]{1,0:T(8,128)} fusion(bf16[512,768]{1,0:T(8,128)(2,1)} %get-tuple-element.15, bf16[512,768]{1,0:T(8,128)(2,1)} %copy-done.5, bf16[768,768]{1,0:T(8,128)(2,1)} %constant.69.clone), kind=kOutput, calls=%fused_computation.33 | convolution fusion | flops 1208352768 | bytes 5111808 | tf_op jit(solution)/shard_map/dot_general | solution.py:94
  70.6 3.5 %pad_maximum_fusion = f32[3,2,384,768]{3,2,0,1:T(8,128)S(1)} fusion(f32[1,2,384,768]{3,2,0,1:T(8,128)} %bitcast.95, f32[1,2,384,768]{3,2,0,1:T(8,128)} %bitcast.96, f32[1,2,384,768]{3,2,0,1:T(8,128)} %bitcast.97), kind=kLoop, calls=%fused_computation | loop fusion | flops 3538944 | bytes 14155776 | tf_op jit(solution)/shard_map/stack | solution.py:103
  78.4 4.0 %collective-permute-done.6 = bf16[3,384,768]{2,1,0:T(8,128)(2,1)} collective-permute-done((bf16[3,384,768]{2,1,0:T(8,128)(2,1)}, bf16[3,384,768]{2,1,0:T(8,128)(2,1)}, u32[]{:S(2)}, u32[]{:S(2)}) %collective-permute-start.6) | collective-permute-done | bytes 1769504 | tf_op jit(solution)/shard_map/ppermute | solution.py:106
  82.5 2.9 %fusion = bf16[3,384,768]{2,1,0:T(8,128)(2,1)S(1)} fusion(bf16[3,384,768]{2,1,0:T(8,128)(2,1)} %collective-permute-done.6, f32[3,2,384,768]{3,2,0,1:T(8,128)} %copy-done.1, s32[]{:T(128)S(6)} %select_n.64), kind=kLoop, calls=%fused_computation.2 | loop fusion | flops 2654208 | bytes 7077892 | tf_op jit(solution)/shard_map/convert_element_type | solution.py:106
  85.5 25.7 %all_to_all.39 = bf16[4,3,96,768]{3,2,1,0:T(8,128)(2,1)} all-to-all(bf16[4,3,96,768]{3,2,1,0:T(8,128)(2,1)S(1)} %copy.23), channel_id=1, replica_groups=mesh['z'=8,'y'=4,'core'=2,'batch'=4] {'batch'}, dimensions={0} | all-to-all | bytes 3538944 | tf_op jit(solution)/shard_map/all_to_all | solution.py:34
  113.9 4.3 %all-to-all-start.3 = ((bf16[4,3,24,768]{3,2,1,0:T(8,128)(2,1)}), bf16[4,3,24,768]{3,2,1,0:T(8,128)(2,1)S(1)}, u32[]{:S(2)}, u32[]{:S(2)}) async-start(bf16[4,3,24,768]{3,2,1,0:T(8,128)(2,1)} %copy.24), calls=%async_computation.3 | async-start | bytes 884736 | tf_op jit(solution)/shard_map/all_to_all | solution.py:34
  118.2 3.5 %fusion.23 = bf16[64,8,768]{2,1,0:T(8,128)(2,1)} fusion(f32[512,768]{1,0:T(8,128)} %fusion.2, s32[512]{0:T(512)S(1)} %add_select_fusion, s32[256]{0:T(256)S(1)} %multiply_add_fusion, bf16[1,512,768]{2,1,0:T(8,128)(2,1)} %param.7), kind=kOutput, calls=%fused_computation.31 | convolution fusion | flops 406519808 | bytes 3148800 | tf_op jit(solution)/shard_map/dot_general | solution.py:72
  121.6 4.3 %all-to-all-done.3 = bf16[4,3,24,768]{3,2,1,0:T(8,128)(2,1)S(1)} async-done(((bf16[4,3,24,768]{3,2,1,0:T(8,128)(2,1)}), bf16[4,3,24,768]{3,2,1,0:T(8,128)(2,1)S(1)}, u32[]{:S(2)}, u32[]{:S(2)}) %all-to-all-start.3) | async-done | bytes 442400 | tf_op jit(solution)/shard_map/all_to_all | solution.py:34
  125.9 5.5 %all-to-all-start = ((bf16[64,8,768]{2,1,0:T(8,128)(2,1)}), bf16[64,8,768]{2,1,0:T(8,128)(2,1)}, u32[]{:S(2)}, u32[]{:S(2)}) async-start(bf16[64,8,768]{2,1,0:T(8,128)(2,1)} %fusion.23), calls=%async_computation | async-start | bytes 1572864 | tf_op jit(solution)/shard_map/all_to_all | solution.py:73
  135.9 3.2 %collective-permute-start.5 = (bf16[32,768]{1,0:T(8,128)(2,1)S(1)}, bf16[32,768]{1,0:T(8,128)(2,1)S(1)}, u32[]{:S(2)}, u32[]{:S(2)}) collective-permute-start(bf16[32,768]{1,0:T(8,128)(2,1)S(1)} %get-tuple-element.3), channel_id=1, source_target_pairs={{0,4},{4,8},{8,12},{12,16},{16,20},{20,24},{24,28},{28,32},{32,36}... | collective-permute-start | bytes 147464 | tf_op jit(solution)/shard_map/ppermute | solution.py:30
  141.2 3.0 %fusion.24 = bf16[1,512,768]{2,1,0:T(8,128)(2,1)} fusion(f32[512,768]{1,0:T(8,128)S(1)} %fusion.29, f32[512,768]{1,0:T(8,128)S(1)} %copy-done.2, f32[512,768]{1,0:T(8,128)S(1)} %fusion.30, bf16[3,768,768]{2,1,0:T(8,128)(2,1)} %bitcast.105, bf16[512,768]{1,0:T(8,128)(2,1)S(1)} %copy-done.4, bf16[32,768]{1,0:T(8,128)(2,1)S(1)} %collective-permute-done.5, ...), kind=kOutput, calls=%fused_computation.32 | convolution fusion | flops 607518720 | bytes 7520768 | tf_op jit(solution)/shard_map/dot_general | solution.py:88
  145.1 9.4 %all-to-all-done = bf16[64,8,768]{2,1,0:T(8,128)(2,1)} async-done(((bf16[64,8,768]{2,1,0:T(8,128)(2,1)}), bf16[64,8,768]{2,1,0:T(8,128)(2,1)}, u32[]{:S(2)}, u32[]{:S(2)}) %all-to-all-start) | async-done | bytes 786464 | tf_op jit(solution)/shard_map/all_to_all | solution.py:73
  154.5 8.3 %all-to-all-start.4 = ((bf16[8,3,3,768]{3,2,1,0:T(4,128)(2,1)}), bf16[8,3,3,768]{3,2,1,0:T(4,128)(2,1)S(1)}, u32[]{:S(2)}, u32[]{:S(2)}) async-start(bf16[8,3,3,768]{3,2,1,0:T(4,128)(2,1)} %copy.25), calls=%async_computation.4 | async-start | bytes 294912 | tf_op jit(solution)/shard_map/all_to_all | solution.py:34
  162.8 3.7 %fusion.1 = bf16[1,1,64,8,1536]{4,3,2,1,0:T(8,128)(2,1)} fusion(bf16[768,1536]{1,0:T(8,128)(2,1)S(1)} %copy-done, bf16[64,8,768]{2,1,0:T(8,128)(2,1)} %all-to-all-done), kind=kOutput, calls=%fused_computation.5 | convolution fusion | flops 1208745984 | bytes 4718592 | tf_op jit(solution)/shard_map/dot_general | solution.py:74
  166.5 5.6 %all-to-all-done.4 = bf16[8,3,3,768]{3,2,1,0:T(4,128)(2,1)S(1)} async-done(((bf16[8,3,3,768]{3,2,1,0:T(4,128)(2,1)}), bf16[8,3,3,768]{3,2,1,0:T(4,128)(2,1)S(1)}, u32[]{:S(2)}, u32[]{:S(2)}) %all-to-all-start.4) | async-done | bytes 110624 | tf_op jit(solution)/shard_map/all_to_all | solution.py:34
  172.1 11.9 %all-gather = bf16[12,3,768]{2,1,0:T(4,128)(2,1)S(1)} all-gather(bf16[3,3,768]{2,1,0:T(4,128)(2,1)S(1)} %reduce_sum.48), channel_id=2, replica_groups=mesh['z'=8,'y'=4,'core'=2,'batch'=4] {'batch'}, dimensions={0}, use_global_device_ids=true | all-gather | bytes 69120 | tf_op jit(solution)/shard_map/all_gather | solution.py:113
  (52 shorter events, 23.3 us)
Async XLA Ops:
  0.6 9.8 %copy-start = (bf16[768,1536]{1,0:T(8,128)(2,1)S(1)}, bf16[768,1536]{1,0:T(8,128)(2,1)}, u32[]{:S(2)}) copy-start(bf16[768,1536]{1,0:T(8,128)(2,1)} %param.11) | copy-start | bytes 7077892
  1.6 28.0 %collective-permute-start.1 = (bf16[32,768]{1,0:T(8,128)(2,1)S(1)}, bf16[32,768]{1,0:T(8,128)(2,1)S(1)}, u32[]{:S(2)}, u32[]{:S(2)}) collective-permute-start(bf16[32,768]{1,0:T(8,128)(2,1)S(1)} %get-tuple-element.7), channel_id=1, source_target_pairs={{0,4},{4,8},{8,12},{12,16},{16,20},{20,24},{24,28},{28,32},{32,36}... | collective-permute-start | bytes 147464 | tf_op jit(solution)/shard_map/ppermute | solution.py:30
  4.1 25.3 %collective-permute-start = (s32[32]{0:T(128)S(1)}, s32[32]{0:T(128)S(1)}, u32[]{:S(2)}, u32[]{:S(2)}) collective-permute-start(s32[32]{0:T(128)S(1)} %get-tuple-element.13), channel_id=1, source_target_pairs={{0,4},{4,8},{8,12},{12,16},{16,20},{20,24},{24,28},{28,32},{32,36}... | collective-permute-start | bytes 392 | tf_op jit(solution)/shard_map/ppermute | solution.py:30
  7.9 21.5 %collective-permute-start.2 = (s32[32]{0:T(128)S(1)}, s32[32]{0:T(128)S(1)}, u32[]{:S(2)}, u32[]{:S(2)}) collective-permute-start(s32[32]{0:T(128)S(1)} %get-tuple-element.14), channel_id=1, source_target_pairs={{4,0},{8,4},{12,8},{16,12},{20,16},{24,20},{28,24},{32,28},{36,32}... | collective-permute-start | bytes 392 | tf_op jit(solution)/shard_map/ppermute | solution.py:30
  9.2 20.4 %collective-permute-start.3 = (bf16[32,768]{1,0:T(8,128)(2,1)S(1)}, bf16[32,768]{1,0:T(8,128)(2,1)S(1)}, u32[]{:S(2)}, u32[]{:S(2)}) collective-permute-start(bf16[32,768]{1,0:T(8,128)(2,1)S(1)} %get-tuple-element.8), channel_id=1, source_target_pairs={{4,0},{8,4},{12,8},{16,12},{20,16},{24,20},{28,24},{32,28},{36,32}... | collective-permute-start | bytes 147464 | tf_op jit(solution)/shard_map/ppermute | solution.py:30
  14.2 15.0 %copy-start.8 = (s32[1,256,1]{1,2,0:T(1,128)S(1)}, s32[1,256,1]{1,2,0:T(1,128)}, u32[]{:S(2)}) copy-start(s32[1,256,1]{1,2,0:T(1,128)} %param.9) | copy-start | bytes 3076
  14.2 15.2 %copy-start.7 = (s32[1,512]{1,0:T(1,128)S(1)}, s32[1,512]{1,0:T(1,128)}, u32[]{:S(2)}) copy-start(s32[1,512]{1,0:T(1,128)} %param.8) | copy-start | bytes 6148
  14.2 15.4 %copy-start.3 = (bf16[1,512,768]{2,1,0:T(8,128)(2,1)S(1)}, bf16[1,512,768]{2,1,0:T(8,128)(2,1)}, u32[]{:S(2)}) copy-start(bf16[1,512,768]{2,1,0:T(8,128)(2,1)} %param.7) | copy-start | bytes 2359300
  14.2 38.1 %all-to-all-start.1 = ((bf16[64,8,768]{2,1,0:T(8,128)(2,1)}), bf16[64,8,768]{2,1,0:T(8,128)(2,1)}, u32[]{:S(2)}, u32[]{:S(2)}) async-start(bf16[64,8,768]{2,1,0:T(8,128)(2,1)} %fusion.20), calls=%async_computation.1 | async-start | bytes 1572864 | tf_op jit(solution)/shard_map/all_to_all | solution.py:48
  30.0 0.9 copy-start.5
  30.0 1.2 copy-start.6
  74.2 2.9 %copy-start.1 = (f32[3,2,384,768]{3,2,0,1:T(8,128)}, f32[3,2,384,768]{3,2,0,1:T(8,128)S(1)}, u32[]{:S(2)}) copy-start(f32[3,2,384,768]{3,2,0,1:T(8,128)S(1)} %pad_maximum_fusion) | copy-start | bytes 21233668
  78.4 4.0 %collective-permute-start.6 = (bf16[3,384,768]{2,1,0:T(8,128)(2,1)}, bf16[3,384,768]{2,1,0:T(8,128)(2,1)}, u32[]{:S(2)}, u32[]{:S(2)}) collective-permute-start(bf16[3,384,768]{2,1,0:T(8,128)(2,1)} %fusion.8), channel_id=1, source_target_pairs={{0,4},{4,0},{1,5},{5,1},{2,6},{6,2},{3,7},{7,3},{8,12},{12,8},{9,1... | collective-permute-start | bytes 5308424 | tf_op jit(solution)/shard_map/ppermute | solution.py:106
  113.9 12.0 %all-to-all-start.3 = ((bf16[4,3,24,768]{3,2,1,0:T(8,128)(2,1)}), bf16[4,3,24,768]{3,2,1,0:T(8,128)(2,1)S(1)}, u32[]{:S(2)}, u32[]{:S(2)}) async-start(bf16[4,3,24,768]{3,2,1,0:T(8,128)(2,1)} %copy.24), calls=%async_computation.3 | async-start | bytes 884736 | tf_op jit(solution)/shard_map/all_to_all | solution.py:34
  125.9 28.6 %all-to-all-start = ((bf16[64,8,768]{2,1,0:T(8,128)(2,1)}), bf16[64,8,768]{2,1,0:T(8,128)(2,1)}, u32[]{:S(2)}, u32[]{:S(2)}) async-start(bf16[64,8,768]{2,1,0:T(8,128)(2,1)} %fusion.23), calls=%async_computation | async-start | bytes 1572864 | tf_op jit(solution)/shard_map/all_to_all | solution.py:73
  132.2 6.9 %collective-permute-start.4 = (bf16[32,768]{1,0:T(8,128)(2,1)S(1)}, bf16[32,768]{1,0:T(8,128)(2,1)S(1)}, u32[]{:S(2)}, u32[]{:S(2)}) collective-permute-start(bf16[32,768]{1,0:T(8,128)(2,1)S(1)} %get-tuple-element.4), channel_id=1, source_target_pairs={{4,0},{8,4},{12,8},{16,12},{20,16},{24,20},{28,24},{32,28},{36,32}... | collective-permute-start | bytes 147464 | tf_op jit(solution)/shard_map/ppermute | solution.py:30
  133.5 5.6 %copy-start.4 = (bf16[512,768]{1,0:T(8,128)(2,1)S(1)}, bf16[512,768]{1,0:T(8,128)(2,1)}, u32[]{:S(2)}) copy-start(bf16[512,768]{1,0:T(8,128)(2,1)} %get-tuple-element.15) | copy-start | bytes 2359300
  135.9 5.3 %copy-start.2 = (f32[512,768]{1,0:T(8,128)S(1)}, f32[512,768]{1,0:T(8,128)}, u32[]{:S(2)}) copy-start(f32[512,768]{1,0:T(8,128)} %get-tuple-element.16) | copy-start | bytes 4718596
  135.9 5.3 %collective-permute-start.5 = (bf16[32,768]{1,0:T(8,128)(2,1)S(1)}, bf16[32,768]{1,0:T(8,128)(2,1)S(1)}, u32[]{:S(2)}, u32[]{:S(2)}) collective-permute-start(bf16[32,768]{1,0:T(8,128)(2,1)S(1)} %get-tuple-element.3), channel_id=1, source_target_pairs={{0,4},{4,8},{8,12},{12,16},{16,20},{20,24},{24,28},{28,32},{32,36}... | collective-permute-start | bytes 147464 | tf_op jit(solution)/shard_map/ppermute | solution.py:30
  154.5 17.5 %all-to-all-start.4 = ((bf16[8,3,3,768]{3,2,1,0:T(4,128)(2,1)}), bf16[8,3,3,768]{3,2,1,0:T(4,128)(2,1)S(1)}, u32[]{:S(2)}, u32[]{:S(2)}) async-start(bf16[8,3,3,768]{3,2,1,0:T(4,128)(2,1)} %copy.25), calls=%async_computation.4 | async-start | bytes 294912 | tf_op jit(solution)/shard_map/all_to_all | solution.py:34

commit v2 on v1

v2 whole, which is shorter than its diff:
```python
import functools

import jax
import jax.numpy as jnp
import numpy as np
from jax import lax
from jax.experimental import pallas as pl
from jax.experimental.pallas import tpu as pltpu
from jax.sharding import Mesh, PartitionSpec as P

DIL = 32
SEQ = ("z", "y", "core")
BF = jnp.bfloat16
F32 = jnp.float32
I32 = jnp.int32
LANES = 128
CHUNK = 256
NZ, NY, NC, NX = 8, 4, 2, 4
ROWS, TOKENS, SLOTS, CH, WIDE, CAP = 512, 256, 512, 768, 1536, 8
HALF = CH // 2
OWN = CH // (NZ * NY * NC)
REST = OWN // NX
PIECE = NZ * REST
VMEM = 60 * 1024 * 1024
SMEM_SPEC = pl.BlockSpec(memory_space=pltpu.SMEM)


def nt_dot(a, b):
    return lax.dot_general(a, b, (((1,), (1,)), ((), ())), preferred_element_type=F32)


def tn_dot(a, b):
    return lax.dot_general(a, b, (((0,), (0,)), ((), ())), preferred_element_type=F32)


def dot(a, b):
    return jnp.dot(a, b, preferred_element_type=F32)


def whole(shape):
    return pl.BlockSpec(shape, lambda j: (0,) * len(shape))


def iota(shape, dim):
    return lax.broadcasted_iota(I32, shape, dim)


def channel_order(core, x_me, y_me):
    q = iota((CH, LANES), 0)
    other = (q >= HALF).astype(I32)
    left = q - HALF * other
    parts = []
    size = HALF
    for count in (NY, NX, NZ):
        size //= count
        digit = jnp.zeros_like(q)
        for i in range(1, count):
            digit += (left >= size * i).astype(I32)
        left = left - size * digit
        parts.append(digit)
    y, x, z = parts
    half = core + other - 2 * core * other
    y, x = y + y_me, x + x_me
    y = jnp.where(y >= NY, y - NY, y)
    x = jnp.where(x >= NX, x - NX, x)
    return z * (NY * NC * OWN) + y * (NC * OWN) + half * OWN + x * REST + left


def forward_kernel(
    place_ref, x_ref, peer_ref, out_ref, ids_ref, own_ref, w_ref,
    slope_ref, placed_ref, xt_mine_ref, xt_peer_ref, pick_ref, mask_ref,
    taps, perm, pick_t, pair,
):
    j = pl.program_id(0)
    core = place_ref[0]

    @pl.when(j == 0)
    def _():
        first = core == 0
        before = jnp.where(first, out_ref[...], peer_ref[...])
        after = jnp.where(first, peer_ref[...], out_ref[...])
        ids_col = jnp.transpose(
            jnp.broadcast_to(ids_ref[...].astype(F32), (LANES, ROWS)), (1, 0)
        )
        ids_ext = jnp.concatenate(
            [before[:, CH:].astype(F32), ids_col, after[:, CH:].astype(F32)], axis=0
        )
        x_ext = jnp.concatenate([before[:, :CH], x_ref[...], after[:, :CH]], axis=0)
        taps[1] = x_ref[...]
        for i, k in ((0, 0), (1, 2)):
            same = jnp.where(ids_ext[k * DIL : k * DIL + ROWS] == ids_col, 1.0, 0.0).astype(BF)
            mask_ref[i] = same
            for c in range(0, CH, LANES):
                taps[k, :, c : c + LANES] = x_ext[k * DIL : k * DIL + ROWS, c : c + LANES] * same
        order = channel_order(core, place_ref[1], place_ref[2])
        for c in range(0, CH, LANES):
            perm[:, c : c + LANES] = jnp.where(
                order == iota((CH, LANES), 1) + c, 1.0, 0.0
            ).astype(BF)
        own_row = own_ref[...].astype(F32)
        row_b = jnp.broadcast_to(own_row, (TOKENS, TOKENS))
        col_b = jnp.transpose(row_b, (1, 0))
        src, dst = iota((TOKENS, TOKENS), 0), iota((TOKENS, TOKENS), 1)
        earlier = jnp.where((row_b == col_b) & (src < dst), 1.0, 0.0)
        slot_row = (own_row * CAP + jnp.sum(earlier, axis=0, keepdims=True)).astype(I32)
        pick_t[...] = jnp.where(iota((SLOTS, TOKENS), 0) == slot_row, 1.0, 0.0).astype(BF)
        two = 2 * iota((TOKENS, ROWS), 0)
        pos = iota((TOKENS, ROWS), 1)
        pair[...] = jnp.where((pos == two) | (pos == two + 1), 0.5, 0.0).astype(BF)
        pick_ref[...] = lax.dot_general(
            pair[...], pick_t[...], (((0,), (1,)), ((), ())), preferred_element_type=F32
        ).astype(BF)

    preact = dot(taps[0], w_ref[0]) + dot(taps[1], w_ref[1]) + dot(taps[2], w_ref[2])
    cdf = 0.5 * (1.0 + lax.erf(preact * 0.7071067811865476))
    slope_ref[...] = cdf + preact * jnp.exp(-0.5 * preact * preact) * 0.3989422804014327
    x_own = x_ref[:, pl.ds(pl.multiple_of(j * CHUNK, CHUNK), CHUNK)].astype(F32)
    hidden = (x_own + preact * cdf).astype(BF)
    pooled = dot(pair[...], hidden).astype(BF)
    placed_ref[...] = dot(pick_t[...], pooled).astype(BF)
    turned = nt_dot(perm[...], taps[j]).astype(BF)
    xt_mine_ref[0] = turned[:HALF]
    xt_peer_ref[0] = turned[HALF:]


def forward(place, x, peer, out, ids, own, w3):
    col = lambda j: (0, j)
    tap = lambda j: (j, 0, 0)
    halo = (DIL, CH + LANES)
    return pl.pallas_call(
        forward_kernel,
        grid=(3,),
        in_specs=[
            SMEM_SPEC, whole((ROWS, CH)), whole(halo), whole(halo), whole((1, ROWS)),
            whole((1, TOKENS)), pl.BlockSpec((3, CH, CHUNK), lambda j: (0, 0, j)),
        ],
        out_specs=[
            pl.BlockSpec((ROWS, CHUNK), col), pl.BlockSpec((SLOTS, CHUNK), col),
            pl.BlockSpec((1, HALF, ROWS), tap), pl.BlockSpec((1, HALF, ROWS), tap),
            whole((ROWS, SLOTS)), whole((2, ROWS, LANES)),
        ],
        out_shape=[
            jax.ShapeDtypeStruct((ROWS, CH), F32), jax.ShapeDtypeStruct((SLOTS, CH), BF),
            jax.ShapeDtypeStruct((3, HALF, ROWS), BF), jax.ShapeDtypeStruct((3, HALF, ROWS), BF),
            jax.ShapeDtypeStruct((ROWS, SLOTS), BF), jax.ShapeDtypeStruct((2, ROWS, LANES), BF),
        ],
        scratch_shapes=[
            pltpu.VMEM((3, ROWS, CH), BF), pltpu.VMEM((CH, CH), BF), pltpu.VMEM((SLOTS, TOKENS), BF),
            pltpu.VMEM((TOKENS, ROWS), BF),
        ],
        compiler_params=pltpu.CompilerParams(vmem_limit_bytes=VMEM),
        name="forward",
    )(place, x, peer, out, ids, own, w3)


def grad_kernel(ret_ref, pick_ref, slope_ref, g_ref):
    g_ref[...] = (dot(pick_ref[...], ret_ref[...]) * slope_ref[...]).astype(BF)


def gradient(returned, pick, slope):
    col = lambda j: (0, j)
    return pl.pallas_call(
        grad_kernel,
        grid=(CH // CHUNK,),
        in_specs=[
            pl.BlockSpec((SLOTS, CHUNK), col), whole((ROWS, SLOTS)), pl.BlockSpec((ROWS, CHUNK), col),
        ],
        out_specs=pl.BlockSpec((ROWS, CHUNK), col),
        out_shape=jax.ShapeDtypeStruct((ROWS, CH), BF),
        compiler_params=pltpu.CompilerParams(vmem_limit_bytes=VMEM),
        name="gradient",
    )(returned, pick, slope)


def wgrad_kernel(mine_ref, peer_ref, g_ref, gp_ref, *refs):
    total = dot(mine_ref[0], g_ref[...]) + dot(peer_ref[0], gp_ref[...])
    for i in range(NY):
        for d in range(NX):
            low = (i * NX + d) * PIECE
            block = total[low : low + PIECE].astype(BF)
            refs[d][0, i] = block[:, :HALF]
            refs[NX + i][0, d] = block[:, HALF:]


def wgrad(mine, peer, g, gp):
    tap = lambda j: (j, 0, 0)
    out = jax.ShapeDtypeStruct((3, NY, PIECE, HALF), BF)
    spec = pl.BlockSpec((1, NY, PIECE, HALF), lambda j: (j, 0, 0, 0))
    outs = pl.pallas_call(
        wgrad_kernel,
        grid=(3,),
        in_specs=[
            pl.BlockSpec((1, HALF, ROWS), tap), pl.BlockSpec((1, HALF, ROWS), tap),
            whole((ROWS, CH)), whole((ROWS, CH)),
        ],
        out_specs=[spec] * (NX + NY),
        out_shape=[out] * (NX + NY),
        compiler_params=pltpu.CompilerParams(vmem_limit_bytes=VMEM),
        name="wgrad",
    )(mine, peer, g, gp)
    return outs[:NX], outs[NX:]


def sum_kernel(*refs):
    for side in (0, 1):
        ins = refs[4 * side : 4 * side + 4]
        for d in range(4):
            total = ins[0][0, d].astype(F32)
            for ref in ins[1:]:
                total += ref[0, d].astype(F32)
            refs[8 + 4 * side + d][0] = total.astype(BF)


def sum_parts(a_parts, b_parts):
    ins = pl.BlockSpec((1, 4, PIECE, HALF), lambda j: (j, 0, 0, 0))
    outs = pl.BlockSpec((1, PIECE, HALF), lambda j: (j, 0, 0))
    got = pl.pallas_call(
        sum_kernel,
        grid=(3,),
        in_specs=[ins] * 8,
        out_specs=[outs] * 8,
        out_shape=[jax.ShapeDtypeStruct((3, PIECE, HALF), BF)] * 8,
        compiler_params=pltpu.CompilerParams(vmem_limit_bytes=VMEM),
        name="sum_parts",
    )(*a_parts, *b_parts)
    return got[:4], got[4:]


def dgrad_kernel(place_ref, g_ref, gp_ref, out_ref, mask_ref, pick_ref, ret_ref, w_ref, o_ref, taps):
    @pl.when(pl.program_id(0) == 0)
    def _():
        first = place_ref[0] == 0
        before = jnp.where(first, out_ref[...], gp_ref[ROWS - DIL :])
        after = jnp.where(first, gp_ref[:DIL], out_ref[...])
        g_ext = jnp.concatenate([before, g_ref[...], after], axis=0)
        for i, k in ((0, 2), (1, 0)):
            low = (2 - k) * DIL
            for c in range(0, CH, LANES):
                taps[i, :, c : c + LANES] = g_ext[low : low + ROWS, c : c + LANES] * mask_ref[i]

    total = dot(pick_ref[...], ret_ref[...])
    total += nt_dot(taps[1], w_ref[0])
    total += nt_dot(g_ref[...], w_ref[1])
    total += nt_dot(taps[0], w_ref[2])
    o_ref[...] = total.astype(BF)


def dgrad(place, g, gp, out, masks, pick, returned, w3):
    col = lambda j: (0, j)
    return pl.pallas_call(
        dgrad_kernel,
        grid=(CH // CHUNK,),
        in_specs=[
            SMEM_SPEC, whole((ROWS, CH)), whole((ROWS, CH)), whole((DIL, CH)),
            whole((2, ROWS, LANES)), whole((ROWS, SLOTS)), pl.BlockSpec((SLOTS, CHUNK), col),
            pl.BlockSpec((3, CHUNK, CH), lambda j: (0, j, 0)),
        ],
        out_specs=pl.BlockSpec((ROWS, CHUNK), col),
        out_shape=jax.ShapeDtypeStruct((ROWS, CH), BF),
        scratch_shapes=[pltpu.VMEM((2, ROWS, CH), BF)],
        compiler_params=pltpu.CompilerParams(vmem_limit_bytes=VMEM),
        name="dgrad",
    )(place, g, gp, out, masks, pick, returned, w3)


def to_peer(array):
    return lax.ppermute(array, "core", [(0, 1), (1, 0)])


def to_next_chip(array):
    last = NZ * NY * NC
    pairs = [(i, i - 1) for i in range(2, last, 2)] + [(i, i + 1) for i in range(1, last - 1, 2)]
    return lax.ppermute(array, SEQ, pairs)


def spread(pieces, axis):
    count = len(pieces)
    got = [pieces[0]]
    for d in range(1, count):
        pairs = [(i, (i + d) % count) for i in range(count)]
        got.append(lax.ppermute(pieces[d], axis, pairs))
    return got


def gather_x(array):
    me = lax.axis_index("batch")
    stacked = jnp.stack(spread([array] * NX, "batch"), axis=0)
    return [
        lax.dynamic_index_in_dim(stacked, (me - i + NX) % NX, 0, False) for i in range(NX)
    ]


def body(x, ids, owners, weight, proj, grads):
    x, ids, owners, grads = x[0], ids[0], owners[0, :, 0], grads[0, 0]
    core = lax.axis_index("core")
    first = core == 0
    place = jnp.stack([core, lax.axis_index("batch"), lax.axis_index("y")]).astype(I32)
    ids_b = ids.astype(BF)
    head = jnp.concatenate([x[:DIL], jnp.broadcast_to(ids_b[:DIL, None], (DIL, LANES))], axis=1)
    tail = jnp.concatenate([x[-DIL:], jnp.broadcast_to(ids_b[-DIL:, None], (DIL, LANES))], axis=1)
    peer_halo = to_peer(jnp.where(first, tail, head))
    out_halo = to_next_chip(jnp.where(first, head, tail))
    back = jnp.dot(grads.reshape(SLOTS, WIDE), proj.T, preferred_element_type=F32).astype(BF)
    back, peer_halo, out_halo = lax.optimization_barrier((back, peer_halo, out_halo))
    returned = lax.all_to_all(back, SEQ, 0, 0, tiled=True)
    w3 = weight.transpose(1, 0, 2)
    slope, placed, xt_mine, xt_peer, pick, masks = forward(
        place, x, peer_halo, out_halo, ids[None], owners[None], w3
    )
    xt_from = to_peer(xt_peer)
    received = lax.all_to_all(placed, SEQ, 0, 0, tiled=True)
    g = gradient(returned, pick, slope)
    g_peer = to_peer(g)
    g_out = to_next_chip(jnp.where(first, g[:DIL], g[-DIL:]))
    a_parts, b_parts = wgrad(xt_mine, xt_from, g, g_peer)
    a_parts, b_parts = spread(a_parts, "batch"), spread(b_parts, "y")
    input_grad = dgrad(place, g, g_peer, g_out, masks, pick, returned, w3)
    a_next, b_next = sum_parts(a_parts, b_parts)
    a_next, b_next, received, input_grad = lax.optimization_barrier(
        (a_next, b_next, received, input_grad)
    )
    owner_rows = jnp.dot(received, proj, preferred_element_type=F32).astype(BF)
    a_next, b_next = spread(a_next, "y"), spread(b_next, "batch")
    by_xy = jnp.concatenate(
        [sum(part.astype(F32) for part in parts) for parts in (a_next, b_next)], axis=-1
    ).astype(BF)
    by_xy = by_xy.reshape(3, NZ, REST, CH).transpose(1, 0, 2, 3)
    by_xy, owner_rows = lax.optimization_barrier((by_xy, owner_rows))
    by_z = lax.all_to_all(by_xy, "z", 0, 0, tiled=True)
    by_z = jnp.sum(by_z.astype(F32), axis=0).astype(BF)
    every = jnp.concatenate(gather_x(by_z), axis=1)
    conv_grad = every.transpose(1, 0, 2).astype(F32)
    return (
        owner_rows.reshape(1, 1, NZ * NY * NC, CAP, WIDE),
        input_grad[None],
        conv_grad,
    )


def solution(mesh):
    fine = Mesh(mesh.devices.reshape(NZ, NY, NC, NX), ("z", "y", "core", "batch"))
    return jax.shard_map(
        body,
        mesh=fine,
        in_specs=(
            P("batch", SEQ, None),
            P("batch", SEQ),
            P("batch", SEQ, None),
            P(),
            P(),
            P("batch", SEQ, None, None, None),
        ),
        out_specs=(
            P("batch", SEQ, None, None, None),
            P("batch", SEQ, None),
            P(SEQ, None, None),
        ),
        check_vma=False,
    )
```

time: 186 us -> 134 us (0.72)
  matrix products: 41.8 us -> 7.37 us
  Pallas kernels: 0 us -> 31.5 us
  blocking collectives: 37.6 us -> 15.8 us
  waiting for transfers between devices: 39.3 us -> 24.1 us
  local copies, waits for them, and re-layouts: 10.5 us -> 3.78 us
  other arithmetic: 9.18 us -> 2.51 us
    dot_general x10 -> x1, matrix products: 38.1 us -> 3.71 us  [body(): jnp.dot(grads.reshape(SLOTS, WIDE), proj.T, preferred_element_type=F32)]
    pallas_call x0 -> x5, Pallas kernels: none -> 31.5 us  [the longest x1 12.9 us: forward(): pl.pallas_call(forward_kernel, grid=(3,), in_specs=[SMEM_SPEC, whole((ROW...]
    all_to_all x2 -> x0, starting transfers between devices: 12.5 us -> none  [exchange_sum(): moved = lax.all_to_all(parts, axis, 0, 0, tiled=True)]
    all_gather x1 -> x0, blocking collectives: 11.9 us -> none  [body(): everyone = lax.all_gather(by_z, 'batch', axis=0, tiled=False)]
    ppermute x7 -> x20, starting transfers between devices: 12.5 us -> 23.9 us  [the longest x15 22.4 us: spread(): got.append(lax.ppermute(pieces[d], axis, pairs))]
    ppermute x7 -> x20, waiting for transfers between devices: 4.05 us -> 14.5 us  [the longest x15 12 us: spread(): got.append(lax.ppermute(pieces[d], axis, pairs))]
    all_to_all x1, blocking collectives: 25.7 us -> 15.8 us  [body(): by_z = lax.all_to_all(by_xy, 'z', 0, 0, tiled=True)]
    all_to_all x2 -> x0, waiting for transfers between devices: 9.87 us -> none  [exchange_sum(): moved = lax.all_to_all(parts, axis, 0, 0, tiled=True)]
  transfers between devices with their start and end apart: 11 -> 22, of which waited for: 5 -> 9; matrix products, arithmetic and copies ran while one was open for 14% -> 7% of each run, Pallas kernels for 0% -> 24%
where the time goes in v2:
time: 134 us; the launch traced here: 131 us
  starting transfers between devices  45 us (34%)
  Pallas kernels  31.5 us (24%)
  waiting for transfers between devices  24.1 us (18%)
  blocking collectives  15.8 us (12%)
  matrix products  7.37 us (6%)
  local copies, waits for them, and re-layouts  3.78 us (3%)
  other arithmetic  2.51 us (2%)
    ppermute x15, starting transfers between devices, spread(): got.append(lax.ppermute(pieces[d], axis, pairs))  22.4 us
    all_to_all x1, blocking collectives, body(): by_z = lax.all_to_all(by_xy, 'z', 0, 0, tiled=True)  15.8 us
    all_to_all x1, starting transfers between devices, body(): returned = lax.all_to_all(back, SEQ, 0, 0, tiled=True)  15.2 us
    pallas_call x1, Pallas kernels, forward(): pl.pallas_call(forward_kernel, grid=(3,), in_specs=[SMEM_SPEC, whole((ROW...  12.9 us
    ppermute x15, waiting for transfers between devices, spread(): got.append(lax.ppermute(pieces[d], axis, pairs))  12 us
    all_to_all x1, waiting for transfers between devices, body(): returned = lax.all_to_all(back, SEQ, 0, 0, tiled=True)  9.64 us
    pallas_call x1, Pallas kernels, dgrad(): pl.pallas_call(dgrad_kernel, grid=(CH // CHUNK,), in_specs=[SMEM_SPEC, wh...  6.34 us
    all_to_all x1, starting transfers between devices, body(): received = lax.all_to_all(placed, SEQ, 0, 0, tiled=True)  5.95 us
  transfers between devices with their start and end apart: 22, of which 9 were waited for; matrix products, arithmetic and copies ran while one was open for 7% of the time, Pallas kernels for 24%

profile of v2, /device:TPU:6, one launch (start us, length us, event | category | flops | bytes accessed | tf_op | source)
XLA Modules:
  0.0 131.0 jit_solution(14991766649010418893)
XLA Ops:
  3.4 3.7 %fusion.2 = bf16[512,768]{1,0:T(8,128)(2,1)} fusion(bf16[768,1536]{1,0:T(8,128)(2,1)S(1)} %copy-done, bf16[1,1,64,8,1536]{4,3,2,1,0:T(8,128)(2,1)} %param.11), kind=kOutput, calls=%fused_computation.3 | convolution fusion | flops 1208352768 | bytes 4718592 | tf_op jit(solution)/shard_map/dot_general | solution.py:303
  7.1 15.2 %all-to-all-start = ((bf16[64,8,768]{2,1,0:T(8,128)(2,1)}), bf16[64,8,768]{2,1,0:T(8,128)(2,1)S(1)}, u32[]{:S(2)}, u32[]{:S(2)}) async-start(bf16[64,8,768]{2,1,0:T(8,128)(2,1)} %bitcast.50), calls=%async_computation | async-start | bytes 1572864 | tf_op jit(solution)/shard_map/all_to_all | solution.py:305
  23.0 12.9 %forward.1 = (f32[512,768]{1,0:T(8,128)}, bf16[512,768]{1,0:T(8,128)(2,1)}, bf16[3,384,512]{2,1,0:T(8,128)(2,1)}, bf16[3,384,512]{2,1,0:T(8,128)(2,1)}, bf16[512...) custom-call(s32[3]{0:T(128)} %pad_add_fusion.place_ref, bf16[512,768]{1,0:T(8,128)(2,1)} %bitcast.48, ...), custom_call_target="tpu_custom_call" | custom-call | tf_op jit(solution)/shard_map/forward/pallas_call | solution.py:130
  35.9 9.6 %all-to-all-done = bf16[64,8,768]{2,1,0:T(8,128)(2,1)S(1)} async-done(((bf16[64,8,768]{2,1,0:T(8,128)(2,1)}), bf16[64,8,768]{2,1,0:T(8,128)(2,1)S(1)}, u32[]{:S(2)}, u32[]{:S(2)}) %all-to-all-start) | async-done | bytes 786464 | tf_op jit(solution)/shard_map/all_to_all | solution.py:305
  45.6 6.0 %all-to-all-start.1 = ((bf16[64,8,768]{2,1,0:T(8,128)(2,1)}), bf16[64,8,768]{2,1,0:T(8,128)(2,1)}, u32[]{:S(2)}, u32[]{:S(2)}) async-start(bf16[64,8,768]{2,1,0:T(8,128)(2,1)} %bitcast.49), calls=%async_computation.1 | async-start | bytes 1572864 | tf_op jit(solution)/shard_map/all_to_all | solution.py:311
  51.6 3.9 %gradient.1.g_ref = bf16[512,768]{1,0:T(8,128)(2,1)} custom-call(bf16[512,768]{1,0:T(8,128)(2,1)} %bitcast.46, bf16[512,512]{1,0:T(8,128)(2,1)} %get-tuple-element.45.pick_ref, f32[512,768]{1,0:T(8,128)} %get-tuple-element.46.slope_ref), custom_call_target="tpu_custom_call" | custom-call | tf_op jit(solution)/shard_map/gradient/pallas_call | solution.py:162
  55.5 2.5 %collective-permute-done.3.gp_ref = bf16[512,768]{1,0:T(8,128)(2,1)S(1)} collective-permute-done((bf16[512,768]{1,0:T(8,128)(2,1)}, bf16[512,768]{1,0:T(8,128)(2,1)S(1)}, u32[]{:S(2)}, u32[]{:S(2)}) %collective-permute-start.3) | collective-permute-done | bytes 786464 | tf_op jit(solution)/shard_map/ppermute | solution.py:267
  58.8 5.2 %wgrad.1 = (bf16[3,4,24,384]{3,2,1,0:T(8,128)(2,1)}, bf16[3,4,24,384]{3,2,1,0:T(8,128)(2,1)}, bf16[3,4,24,384]{3,2,1,0:T(8,128)(2,1)}, bf16[3,4,24,384]{3,2,1,0:...) custom-call(bf16[3,384,512]{2,1,0:T(8,128)(2,1)} %get-tuple-element., ...), custom_call_target="tpu_custom_call" | custom-call | tf_op jit(solution)/shard_map/wgrad/pallas_call | solution.py:189
  66.1 2.5 %collective-permute-start.5 = (bf16[3,4,24,384]{3,2,1,0:T(8,128)(2,1)}, bf16[3,4,24,384]{3,2,1,0:T(8,128)(2,1)S(1)}, u32[]{:S(2)}, u32[]{:S(2)}) collective-permute-start(bf16[3,4,24,384]{3,2,1,0:T(8,128)(2,1)} %get-tuple-element.49), channel_id=1, source_target_pairs={{0,2},{1,3},{2,0},{3,1},{4,6},{5,7},{6,4},{7,5},{8,10},{9,11},{10,... | collective-permute-start | bytes 663560 | tf_op jit(solution)/shard_map/ppermute | solution.py:281
  68.6 2.7 %collective-permute-start.7 = (bf16[3,4,24,384]{3,2,1,0:T(8,128)(2,1)}, bf16[3,4,24,384]{3,2,1,0:T(8,128)(2,1)S(1)}, u32[]{:S(2)}, u32[]{:S(2)}) collective-permute-start(bf16[3,4,24,384]{3,2,1,0:T(8,128)(2,1)} %get-tuple-element.52), channel_id=1, source_target_pairs={{0,8},{8,16},{16,24},{24,0},{1,9},{9,17},{17,25},{25,1},{2,10},{10... | collective-permute-start | bytes 663560 | tf_op jit(solution)/shard_map/ppermute | solution.py:281
  71.4 3.0 %collective-permute-start.8 = (bf16[3,4,24,384]{3,2,1,0:T(8,128)(2,1)}, bf16[3,4,24,384]{3,2,1,0:T(8,128)(2,1)S(1)}, u32[]{:S(2)}, u32[]{:S(2)}) collective-permute-start(bf16[3,4,24,384]{3,2,1,0:T(8,128)(2,1)} %get-tuple-element.53), channel_id=1, source_target_pairs={{0,16},{8,24},{16,0},{24,8},{1,17},{9,25},{17,1},{25,9},{2,18},{10... | collective-permute-start | bytes 663560 | tf_op jit(solution)/shard_map/ppermute | solution.py:281
  74.4 1.2 collective-permute-start.9
  75.5 6.3 %dgrad.1 = bf16[512,768]{1,0:T(8,128)(2,1)} custom-call(s32[3]{0:T(128)} %pad_add_fusion.place_ref, bf16[512,768]{1,0:T(8,128)(2,1)} %gradient.1.g_ref, bf16[512,768]{1,0:T(8,128)(2,1)} %copy-done.2, bf16[32,768]{1,0:T(8,128)(2,1)} %copy-done.13, bf16[2,512,128]{2,1,0:T(8,128)(2,1)} %get-tuple-element.64.mask_ref, ...), custom_call_target="tpu_custom_call" | custom-call | tf_op jit(solution)/shard_map/dgrad/pallas_call | solution.py:250
  82.0 3.6 %collective-permute-done.8.refs_6_ = bf16[3,4,24,384]{3,2,1,0:T(8,128)(2,1)S(1)} collective-permute-done((bf16[3,4,24,384]{3,2,1,0:T(8,128)(2,1)}, bf16[3,4,24,384]{3,2,1,0:T(8,128)(2,1)S(1)}, u32[]{:S(2)}, u32[]{:S(2)}) %collective-permute-start.8) | collective-permute-done | bytes 221216 | tf_op jit(solution)/shard_map/ppermute | solution.py:281
  86.3 3.1 %sum_parts.1 = (bf16[3,24,384]{2,1,0:T(8,128)(2,1)}, bf16[3,24,384]{2,1,0:T(8,128)(2,1)}, bf16[3,24,384]{2,1,0:T(8,128)(2,1)}, bf16[3,24,384]{2,1,0:T(8,128)(2,1...) custom-call(bf16[3,4,24,384]{3,2,1,0:T(8,128)(2,1)} %get-tuple-eleme, ...), custom_call_target="tpu_custom_call" | custom-call | tf_op jit(solution)/shard_map/sum_parts/pallas_call | solution.py:217
  89.5 1.7 %collective-permute-start.11 = (bf16[3,24,384]{2,1,0:T(8,128)(2,1)}, bf16[3,24,384]{2,1,0:T(8,128)(2,1)S(1)}, u32[]{:S(2)}, u32[]{:S(2)}) collective-permute-start(bf16[3,24,384]{2,1,0:T(8,128)(2,1)} %get-tuple-element.66), channel_id=1, source_target_pairs={{0,8},{8,16},{16,24},{24,0},{1,9},{9,17},{17,25},{25,1},{2,10},{10... | collective-permute-start | bytes 165896 | tf_op jit(solution)/shard_map/ppermute | solution.py:281
  91.2 2.6 %collective-permute-start.12 = (bf16[3,24,384]{2,1,0:T(8,128)(2,1)}, bf16[3,24,384]{2,1,0:T(8,128)(2,1)S(1)}, u32[]{:S(2)}, u32[]{:S(2)}) collective-permute-start(bf16[3,24,384]{2,1,0:T(8,128)(2,1)} %get-tuple-element.67), channel_id=1, source_target_pairs={{0,16},{8,24},{16,0},{24,8},{1,17},{9,25},{17,1},{25,9},{2,18},{10... | collective-permute-start | bytes 165896 | tf_op jit(solution)/shard_map/ppermute | solution.py:281
  94.5 3.7 %convolution_convert_fusion = bf16[512,1536]{1,0:T(8,128)(2,1)} fusion(bf16[512,768]{1,0:T(8,128)(2,1)} %bitcast.14, bf16[768,1536]{1,0:T(8,128)(2,1)S(1)} %copy-done), kind=kOutput, calls=%fused_computation | convolution fusion | flops 1208745984 | bytes 4718592 | tf_op jit(solution)/shard_map/dot_general | solution.py:322
  98.2 3.0 %collective-permute-start.14 = (bf16[3,24,384]{2,1,0:T(8,128)(2,1)S(1)}, bf16[3,24,384]{2,1,0:T(8,128)(2,1)S(1)}, u32[]{:S(2)}, u32[]{:S(2)}) collective-permute-start(bf16[3,24,384]{2,1,0:T(8,128)(2,1)S(1)} %copy-done.16), channel_id=1, source_target_pairs={{0,1},{1,2},{2,3},{3,0},{4,5},{5,6},{6,7},{7,4},{8,9},{9,10},{10,1... | collective-permute-start | bytes 165896 | tf_op jit(solution)/shard_map/ppermute | solution.py:281
  101.5 1.2 collective-permute-start.16
  103.0 3.9 %collective-permute-done.15 = bf16[3,24,384]{2,1,0:T(8,128)(2,1)S(1)} collective-permute-done((bf16[3,24,384]{2,1,0:T(8,128)(2,1)S(1)}, bf16[3,24,384]{2,1,0:T(8,128)(2,1)S(1)}, u32[]{:S(2)}, u32[]{:S(2)}) %collective-permute-start.15) | collective-permute-done | bytes 55328 | tf_op jit(solution)/shard_map/ppermute | solution.py:281
  107.6 15.8 %all_to_all.28 = bf16[8,3,3,768]{3,2,1,0:T(4,128)(2,1)S(1)} all-to-all(bf16[8,3,3,768]{3,2,1,0:T(4,128)(2,1)S(1)} %copy.11), channel_id=1, replica_groups=mesh['z'=8,'y'=4,'core'=2,'batch'=4] {'z'}, dimensions={0} | all-to-all | bytes 221184 | tf_op jit(solution)/shard_map/all_to_all | solution.py:329
  125.2 1.3 %collective-permute-start.19 = (bf16[3,3,768]{2,1,0:T(4,128)(2,1)S(1)}, bf16[3,3,768]{2,1,0:T(4,128)(2,1)S(1)}, u32[]{:S(2)}, u32[]{:S(2)}) collective-permute-start(bf16[3,3,768]{2,1,0:T(4,128)(2,1)S(1)} %reduce_sum.12), channel_id=1, source_target_pairs={{0,3},{1,0},{2,1},{3,2},{4,7},{5,4},{6,5},{7,6},{8,11},{9,8},{10,9... | collective-permute-start | bytes 41480 | tf_op jit(solution)/shard_map/ppermute | solution.py:281
  127.4 2.1 %collective-permute-done.18 = bf16[3,3,768]{2,1,0:T(4,128)(2,1)S(1)} collective-permute-done((bf16[3,3,768]{2,1,0:T(4,128)(2,1)S(1)}, bf16[3,3,768]{2,1,0:T(4,128)(2,1)S(1)}, u32[]{:S(2)}, u32[]{:S(2)}) %collective-permute-start.18) | collective-permute-done | bytes 13856 | tf_op jit(solution)/shard_map/ppermute | solution.py:281
  (81 shorter events, 13.3 us)
Async XLA Ops:
  2.6 4.5 %collective-permute-start = (bf16[32,896]{1,0:T(8,128)(2,1)S(1)}, bf16[32,896]{1,0:T(8,128)(2,1)S(1)}, u32[]{:S(2)}, u32[]{:S(2)}) collective-permute-start(bf16[32,896]{1,0:T(8,128)(2,1)S(1)} %get-tuple-element.83), channel_id=1, source_target_pairs={{0,4},{4,0},{1,5},{5,1},{2,6},{6,2},{3,7},{7,3},{8,12},{12,8},{9,1... | collective-permute-start | bytes 172040 | tf_op jit(solution)/shard_map/ppermute | solution.py:267
  2.7 4.4 %collective-permute-start.1 = (bf16[32,896]{1,0:T(8,128)(2,1)S(1)}, bf16[32,896]{1,0:T(8,128)(2,1)S(1)}, u32[]{:S(2)}, u32[]{:S(2)}) collective-permute-start(bf16[32,896]{1,0:T(8,128)(2,1)S(1)} %get-tuple-element.82), channel_id=1, source_target_pairs={{8,4},{16,12},{24,20},{32,28},{40,36},{48,44},{56,52},{64,60},{72,... | collective-permute-start | bytes 172040 | tf_op jit(solution)/shard_map/ppermute | solution.py:273
  7.1 15.9 %copy-start.9 = (bf16[32,896]{1,0:T(8,128)(2,1)}, bf16[32,896]{1,0:T(8,128)(2,1)S(1)}, u32[]{:S(2)}) copy-start(bf16[32,896]{1,0:T(8,128)(2,1)S(1)} %collective-permute-done.peer_ref) | copy-start | bytes 172036
  7.1 38.5 %all-to-all-start = ((bf16[64,8,768]{2,1,0:T(8,128)(2,1)}), bf16[64,8,768]{2,1,0:T(8,128)(2,1)S(1)}, u32[]{:S(2)}, u32[]{:S(2)}) async-start(bf16[64,8,768]{2,1,0:T(8,128)(2,1)} %bitcast.50), calls=%async_computation | async-start | bytes 1572864 | tf_op jit(solution)/shard_map/all_to_all | solution.py:305
  35.9 19.6 %collective-permute-start.2 = (bf16[3,384,512]{2,1,0:T(8,128)(2,1)}, bf16[3,384,512]{2,1,0:T(8,128)(2,1)}, u32[]{:S(2)}, u32[]{:S(2)}) collective-permute-start(bf16[3,384,512]{2,1,0:T(8,128)(2,1)} %get-tuple-element.43), channel_id=1, source_target_pairs={{0,4},{4,0},{1,5},{5,1},{2,6},{6,2},{3,7},{7,3},{8,12},{12,8},{9,1... | collective-permute-start | bytes 3538952 | tf_op jit(solution)/shard_map/ppermute | solution.py:267
  45.6 43.9 %all-to-all-start.1 = ((bf16[64,8,768]{2,1,0:T(8,128)(2,1)}), bf16[64,8,768]{2,1,0:T(8,128)(2,1)}, u32[]{:S(2)}, u32[]{:S(2)}) async-start(bf16[64,8,768]{2,1,0:T(8,128)(2,1)} %bitcast.49), calls=%async_computation.1 | async-start | bytes 1572864 | tf_op jit(solution)/shard_map/all_to_all | solution.py:311
  55.5 2.5 %collective-permute-start.3 = (bf16[512,768]{1,0:T(8,128)(2,1)}, bf16[512,768]{1,0:T(8,128)(2,1)S(1)}, u32[]{:S(2)}, u32[]{:S(2)}) collective-permute-start(bf16[512,768]{1,0:T(8,128)(2,1)} %gradient.1.g_ref), channel_id=1, source_target_pairs={{0,4},{4,0},{1,5},{5,1},{2,6},{6,2},{3,7},{7,3},{8,12},{12,8},{9,1... | collective-permute-start | bytes 2359304 | tf_op jit(solution)/shard_map/ppermute | solution.py:267
  64.1 10.3 %collective-permute-start.4 = (bf16[3,4,24,384]{3,2,1,0:T(8,128)(2,1)}, bf16[3,4,24,384]{3,2,1,0:T(8,128)(2,1)S(1)}, u32[]{:S(2)}, u32[]{:S(2)}) collective-permute-start(bf16[3,4,24,384]{3,2,1,0:T(8,128)(2,1)} %get-tuple-element.48), channel_id=1, source_target_pairs={{0,1},{1,2},{2,3},{3,0},{4,5},{5,6},{6,7},{7,4},{8,9},{9,10},{10,1... | collective-permute-start | bytes 663560 | tf_op jit(solution)/shard_map/ppermute | solution.py:281
  65.4 5.9 %collective-permute-start.10 = (bf16[32,768]{1,0:T(8,128)(2,1)S(1)}, bf16[32,768]{1,0:T(8,128)(2,1)S(1)}, u32[]{:S(2)}, u32[]{:S(2)}) collective-permute-start(bf16[32,768]{1,0:T(8,128)(2,1)S(1)} %slice_select_fusion), channel_id=1, source_target_pairs={{8,4},{16,12},{24,20},{32,28},{40,36},{48,44},{56,52},{64,60},{72,... | collective-permute-start | bytes 147464 | tf_op jit(solution)/shard_map/ppermute | solution.py:273
  66.1 15.8 %collective-permute-start.5 = (bf16[3,4,24,384]{3,2,1,0:T(8,128)(2,1)}, bf16[3,4,24,384]{3,2,1,0:T(8,128)(2,1)S(1)}, u32[]{:S(2)}, u32[]{:S(2)}) collective-permute-start(bf16[3,4,24,384]{3,2,1,0:T(8,128)(2,1)} %get-tuple-element.49), channel_id=1, source_target_pairs={{0,2},{1,3},{2,0},{3,1},{4,6},{5,7},{6,4},{7,5},{8,10},{9,11},{10,... | collective-permute-start | bytes 663560 | tf_op jit(solution)/shard_map/ppermute | solution.py:281
  68.6 13.3 %collective-permute-start.6 = (bf16[3,4,24,384]{3,2,1,0:T(8,128)(2,1)}, bf16[3,4,24,384]{3,2,1,0:T(8,128)(2,1)S(1)}, u32[]{:S(2)}, u32[]{:S(2)}) collective-permute-start(bf16[3,4,24,384]{3,2,1,0:T(8,128)(2,1)} %get-tuple-element.50), channel_id=1, source_target_pairs={{0,3},{1,0},{2,1},{3,2},{4,7},{5,4},{6,5},{7,6},{8,11},{9,8},{10,9... | collective-permute-start | bytes 663560 | tf_op jit(solution)/shard_map/ppermute | solution.py:281
  68.6 13.3 %collective-permute-start.7 = (bf16[3,4,24,384]{3,2,1,0:T(8,128)(2,1)}, bf16[3,4,24,384]{3,2,1,0:T(8,128)(2,1)S(1)}, u32[]{:S(2)}, u32[]{:S(2)}) collective-permute-start(bf16[3,4,24,384]{3,2,1,0:T(8,128)(2,1)} %get-tuple-element.52), channel_id=1, source_target_pairs={{0,8},{8,16},{16,24},{24,0},{1,9},{9,17},{17,25},{25,1},{2,10},{10... | collective-permute-start | bytes 663560 | tf_op jit(solution)/shard_map/ppermute | solution.py:281
  71.4 14.2 %collective-permute-start.8 = (bf16[3,4,24,384]{3,2,1,0:T(8,128)(2,1)}, bf16[3,4,24,384]{3,2,1,0:T(8,128)(2,1)S(1)}, u32[]{:S(2)}, u32[]{:S(2)}) collective-permute-start(bf16[3,4,24,384]{3,2,1,0:T(8,128)(2,1)} %get-tuple-element.53), channel_id=1, source_target_pairs={{0,16},{8,24},{16,0},{24,8},{1,17},{9,25},{17,1},{25,9},{2,18},{10... | collective-permute-start | bytes 663560 | tf_op jit(solution)/shard_map/ppermute | solution.py:281
  74.4 11.2 %collective-permute-start.9 = (bf16[3,4,24,384]{3,2,1,0:T(8,128)(2,1)}, bf16[3,4,24,384]{3,2,1,0:T(8,128)(2,1)S(1)}, u32[]{:S(2)}, u32[]{:S(2)}) collective-permute-start(bf16[3,4,24,384]{3,2,1,0:T(8,128)(2,1)} %get-tuple-element.54), channel_id=1, source_target_pairs={{0,24},{8,0},{16,8},{24,16},{1,25},{9,1},{17,9},{25,17},{2,26},{10... | collective-permute-start | bytes 663560 | tf_op jit(solution)/shard_map/ppermute | solution.py:281
  89.5 17.9 %copy-start.11 = (bf16[3,24,384]{2,1,0:T(8,128)(2,1)S(1)}, bf16[3,24,384]{2,1,0:T(8,128)(2,1)}, u32[]{:S(2)}) copy-start(bf16[3,24,384]{2,1,0:T(8,128)(2,1)} %get-tuple-element.69) | copy-start | bytes 165892
  89.5 12.0 %collective-permute-start.11 = (bf16[3,24,384]{2,1,0:T(8,128)(2,1)}, bf16[3,24,384]{2,1,0:T(8,128)(2,1)S(1)}, u32[]{:S(2)}, u32[]{:S(2)}) collective-permute-start(bf16[3,24,384]{2,1,0:T(8,128)(2,1)} %get-tuple-element.66), channel_id=1, source_target_pairs={{0,8},{8,16},{16,24},{24,0},{1,9},{9,17},{17,25},{25,1},{2,10},{10... | collective-permute-start | bytes 165896 | tf_op jit(solution)/shard_map/ppermute | solution.py:281
  91.2 11.5 %collective-permute-start.12 = (bf16[3,24,384]{2,1,0:T(8,128)(2,1)}, bf16[3,24,384]{2,1,0:T(8,128)(2,1)S(1)}, u32[]{:S(2)}, u32[]{:S(2)}) collective-permute-start(bf16[3,24,384]{2,1,0:T(8,128)(2,1)} %get-tuple-element.67), channel_id=1, source_target_pairs={{0,16},{8,24},{16,0},{24,8},{1,17},{9,25},{17,1},{25,9},{2,18},{10... | collective-permute-start | bytes 165896 | tf_op jit(solution)/shard_map/ppermute | solution.py:281
  93.8 8.8 %collective-permute-start.13 = (bf16[3,24,384]{2,1,0:T(8,128)(2,1)}, bf16[3,24,384]{2,1,0:T(8,128)(2,1)S(1)}, u32[]{:S(2)}, u32[]{:S(2)}) collective-permute-start(bf16[3,24,384]{2,1,0:T(8,128)(2,1)} %get-tuple-element.68), channel_id=1, source_target_pairs={{0,24},{8,0},{16,8},{24,16},{1,25},{9,1},{17,9},{25,17},{2,26},{10... | collective-permute-start | bytes 165896 | tf_op jit(solution)/shard_map/ppermute | solution.py:281
  98.2 4.8 %collective-permute-start.14 = (bf16[3,24,384]{2,1,0:T(8,128)(2,1)S(1)}, bf16[3,24,384]{2,1,0:T(8,128)(2,1)S(1)}, u32[]{:S(2)}, u32[]{:S(2)}) collective-permute-start(bf16[3,24,384]{2,1,0:T(8,128)(2,1)S(1)} %copy-done.16), channel_id=1, source_target_pairs={{0,1},{1,2},{2,3},{3,0},{4,5},{5,6},{6,7},{7,4},{8,9},{9,10},{10,1... | collective-permute-start | bytes 165896 | tf_op jit(solution)/shard_map/ppermute | solution.py:281
  101.2 5.7 %collective-permute-start.15 = (bf16[3,24,384]{2,1,0:T(8,128)(2,1)S(1)}, bf16[3,24,384]{2,1,0:T(8,128)(2,1)S(1)}, u32[]{:S(2)}, u32[]{:S(2)}) collective-permute-start(bf16[3,24,384]{2,1,0:T(8,128)(2,1)S(1)} %copy-done.15), channel_id=1, source_target_pairs={{0,2},{1,3},{2,0},{3,1},{4,6},{5,7},{6,4},{7,5},{8,10},{9,11},{10,... | collective-permute-start | bytes 165896 | tf_op jit(solution)/shard_map/ppermute | solution.py:281
  101.5 6.0 %collective-permute-start.16 = (bf16[3,24,384]{2,1,0:T(8,128)(2,1)S(1)}, bf16[3,24,384]{2,1,0:T(8,128)(2,1)S(1)}, u32[]{:S(2)}, u32[]{:S(2)}) collective-permute-start(bf16[3,24,384]{2,1,0:T(8,128)(2,1)S(1)} %copy-done.14), channel_id=1, source_target_pairs={{0,3},{1,0},{2,1},{3,2},{4,7},{5,4},{6,5},{7,6},{8,11},{9,8},{10,9... | collective-permute-start | bytes 165896 | tf_op jit(solution)/shard_map/ppermute | solution.py:281
  123.5 3.8 %collective-permute-start.17 = (bf16[3,3,768]{2,1,0:T(4,128)(2,1)S(1)}, bf16[3,3,768]{2,1,0:T(4,128)(2,1)S(1)}, u32[]{:S(2)}, u32[]{:S(2)}) collective-permute-start(bf16[3,3,768]{2,1,0:T(4,128)(2,1)S(1)} %reduce_sum.12), channel_id=1, source_target_pairs={{0,1},{1,2},{2,3},{3,0},{4,5},{5,6},{6,7},{7,4},{8,9},{9,10},{10,1... | collective-permute-start | bytes 41480 | tf_op jit(solution)/shard_map/ppermute | solution.py:281
  124.2 5.3 %collective-permute-start.18 = (bf16[3,3,768]{2,1,0:T(4,128)(2,1)S(1)}, bf16[3,3,768]{2,1,0:T(4,128)(2,1)S(1)}, u32[]{:S(2)}, u32[]{:S(2)}) collective-permute-start(bf16[3,3,768]{2,1,0:T(4,128)(2,1)S(1)} %reduce_sum.12), channel_id=1, source_target_pairs={{0,2},{1,3},{2,0},{3,1},{4,6},{5,7},{6,4},{7,5},{8,10},{9,11},{10,... | collective-permute-start | bytes 41480 | tf_op jit(solution)/shard_map/ppermute | solution.py:281
  125.2 5.0 %collective-permute-start.19 = (bf16[3,3,768]{2,1,0:T(4,128)(2,1)S(1)}, bf16[3,3,768]{2,1,0:T(4,128)(2,1)S(1)}, u32[]{:S(2)}, u32[]{:S(2)}) collective-permute-start(bf16[3,3,768]{2,1,0:T(4,128)(2,1)S(1)} %reduce_sum.12), channel_id=1, source_target_pairs={{0,3},{1,0},{2,1},{3,2},{4,7},{5,4},{6,5},{7,6},{8,11},{9,8},{10,9... | collective-permute-start | bytes 41480 | tf_op jit(solution)/shard_map/ppermute | solution.py:281
  (15 other events, 95.2 us)

commit v3 on v2

--- a/solution.py
+++ b/solution.py
@@ -21,7 +21,8 @@
 OWN = CH // (NZ * NY * NC)
 REST = OWN // NX
 PIECE = NZ * REST
-VMEM = 60 * 1024 * 1024
+PART = NY * PIECE
+VMEM = 20 * 1024 * 1024
 SMEM_SPEC = pl.BlockSpec(memory_space=pltpu.SMEM)
 
 
@@ -51,14 +52,14 @@
     left = q - HALF * other
     parts = []
     size = HALF
-    for count in (NY, NX, NZ):
+    for count in (NX, NY, NZ):
         size //= count
         digit = jnp.zeros_like(q)
         for i in range(1, count):
             digit += (left >= size * i).astype(I32)
         left = left - size * digit
         parts.append(digit)
-    y, x, z = parts
+    x, y, z = parts
     half = core + other - 2 * core * other
     y, x = y + y_me, x + x_me
     y = jnp.where(y >= NY, y - NY, y)
@@ -113,7 +114,8 @@
 
     preact = dot(taps[0], w_ref[0]) + dot(taps[1], w_ref[1]) + dot(taps[2], w_ref[2])
     cdf = 0.5 * (1.0 + lax.erf(preact * 0.7071067811865476))
-    slope_ref[...] = cdf + preact * jnp.exp(-0.5 * preact * preact) * 0.3989422804014327
+    bell = jnp.exp(-0.5 * preact * preact) * 0.3989422804014327
+    slope_ref[...] = (cdf + preact * bell).astype(BF)
     x_own = x_ref[:, pl.ds(pl.multiple_of(j * CHUNK, CHUNK), CHUNK)].astype(F32)
     hidden = (x_own + preact * cdf).astype(BF)
     pooled = dot(pair[...], hidden).astype(BF)
@@ -140,9 +142,10 @@
             whole((ROWS, SLOTS)), whole((2, ROWS, LANES)),
         ],
         out_shape=[
-            jax.ShapeDtypeStruct((ROWS, CH), F32), jax.ShapeDtypeStruct((SLOTS, CH), BF),
+            jax.ShapeDtypeStruct((ROWS, CH), BF), jax.ShapeDtypeStruct((SLOTS, CH), BF),
             jax.ShapeDtypeStruct((3, HALF, ROWS), BF), jax.ShapeDtypeStruct((3, HALF, ROWS), BF),
-            jax.ShapeDtypeStruct((ROWS, SLOTS), BF), jax.ShapeDtypeStruct((2, ROWS, LANES), BF),
+            jax.ShapeDtypeStruct((ROWS, SLOTS), BF),
+            jax.ShapeDtypeStruct((2, ROWS, LANES), BF),
         ],
         scratch_shapes=[
             pltpu.VMEM((3, ROWS, CH), BF), pltpu.VMEM((CH, CH), BF), pltpu.VMEM((SLOTS, TOKENS), BF),
@@ -153,77 +156,65 @@
     )(place, x, peer, out, ids, own, w3)
 
 
-def grad_kernel(ret_ref, pick_ref, slope_ref, g_ref):
-    g_ref[...] = (dot(pick_ref[...], ret_ref[...]) * slope_ref[...]).astype(BF)
-
-
-def gradient(returned, pick, slope):
+def grad_kernel(place_ref, ret_ref, pick_ref, slope_ref, g_ref, edge_ref):
+    g = (dot(pick_ref[...], ret_ref[...]) * slope_ref[...].astype(F32)).astype(BF)
+    g_ref[...] = g
+    edge_ref[...] = jnp.where(place_ref[0] == 0, g[:DIL], g[ROWS - DIL :])
+
+
+def gradient(place, returned, pick, slope):
     col = lambda j: (0, j)
     return pl.pallas_call(
         grad_kernel,
+        grid=(CH // HALF,),
+        in_specs=[
+            SMEM_SPEC, pl.BlockSpec((SLOTS, HALF), col), whole((ROWS, SLOTS)),
+            pl.BlockSpec((ROWS, HALF), col),
+        ],
+        out_specs=[pl.BlockSpec((ROWS, HALF), col), pl.BlockSpec((DIL, HALF), col)],
+        out_shape=[jax.ShapeDtypeStruct((ROWS, CH), BF), jax.ShapeDtypeStruct((DIL, CH), BF)],
+        compiler_params=pltpu.CompilerParams(vmem_limit_bytes=VMEM),
+        name="gradient",
+    )(place, returned, pick, slope)
+
+
+def wgrad_kernel(xt_ref, xtp_ref, g_ref, gp_ref, *outs):
+    for k in range(3):
+        total = dot(xt_ref[k], g_ref[...]) + dot(xtp_ref[k], gp_ref[...])
+        for d in range(NX):
+            outs[d][k] = total[d * PART : (d + 1) * PART].astype(BF)
+
+
+def wgrad(xt, xt_peer, g, gp):
+    cols = pl.BlockSpec((ROWS, CHUNK), lambda j: (0, j))
+    xts = whole((3, HALF, ROWS))
+    return pl.pallas_call(
+        wgrad_kernel,
         grid=(CH // CHUNK,),
-        in_specs=[
-            pl.BlockSpec((SLOTS, CHUNK), col), whole((ROWS, SLOTS)), pl.BlockSpec((ROWS, CHUNK), col),
-        ],
-        out_specs=pl.BlockSpec((ROWS, CHUNK), col),
-        out_shape=jax.ShapeDtypeStruct((ROWS, CH), BF),
-        compiler_params=pltpu.CompilerParams(vmem_limit_bytes=VMEM),
-        name="gradient",
-    )(returned, pick, slope)
-
-
-def wgrad_kernel(mine_ref, peer_ref, g_ref, gp_ref, *refs):
-    total = dot(mine_ref[0], g_ref[...]) + dot(peer_ref[0], gp_ref[...])
-    for i in range(NY):
-        for d in range(NX):
-            low = (i * NX + d) * PIECE
-            block = total[low : low + PIECE].astype(BF)
-            refs[d][0, i] = block[:, :HALF]
-            refs[NX + i][0, d] = block[:, HALF:]
-
-
-def wgrad(mine, peer, g, gp):
-    tap = lambda j: (j, 0, 0)
-    out = jax.ShapeDtypeStruct((3, NY, PIECE, HALF), BF)
-    spec = pl.BlockSpec((1, NY, PIECE, HALF), lambda j: (j, 0, 0, 0))
-    outs = pl.pallas_call(
-        wgrad_kernel,
-        grid=(3,),
-        in_specs=[
-            pl.BlockSpec((1, HALF, ROWS), tap), pl.BlockSpec((1, HALF, ROWS), tap),
-            whole((ROWS, CH)), whole((ROWS, CH)),
-        ],
-        out_specs=[spec] * (NX + NY),
-        out_shape=[out] * (NX + NY),
+        in_specs=[xts, xts, cols, cols],
+        out_specs=[pl.BlockSpec((3, PART, CHUNK), lambda j: (0, 0, j))] * NX,
+        out_shape=[jax.ShapeDtypeStruct((3, PART, CH), BF)] * NX,
         compiler_params=pltpu.CompilerParams(vmem_limit_bytes=VMEM),
         name="wgrad",
-    )(mine, peer, g, gp)
-    return outs[:NX], outs[NX:]
+    )(xt, xt_peer, g, gp)
 
 
 def sum_kernel(*refs):
-    for side in (0, 1):
-        ins = refs[4 * side : 4 * side + 4]
-        for d in range(4):
-            total = ins[0][0, d].astype(F32)
-            for ref in ins[1:]:
-                total += ref[0, d].astype(F32)
-            refs[8 + 4 * side + d][0] = total.astype(BF)
-
-
-def sum_parts(a_parts, b_parts):
-    ins = pl.BlockSpec((1, 4, PIECE, HALF), lambda j: (j, 0, 0, 0))
-    outs = pl.BlockSpec((1, PIECE, HALF), lambda j: (j, 0, 0))
-    got = pl.pallas_call(
+    ins, outs = refs[:NX], refs[NX:]
+    total = ins[0][...].astype(F32)
+    for ref in ins[1:]:
+        total += ref[...].astype(F32)
+    for d in range(NY):
+        outs[d][...] = total[:, d * PIECE : (d + 1) * PIECE].astype(BF)
+
+
+def sum_parts(parts):
+    return pl.pallas_call(
         sum_kernel,
-        grid=(3,),
-        in_specs=[ins] * 8,
-        out_specs=[outs] * 8,
-        out_shape=[jax.ShapeDtypeStruct((3, PIECE, HALF), BF)] * 8,
+        out_shape=[jax.ShapeDtypeStruct((3, PIECE, CH), BF)] * NY,
         compiler_params=pltpu.CompilerParams(vmem_limit_bytes=VMEM),
         name="sum_parts",
-    )(*a_parts, *b_parts)
-    return got[:4], got[4:]
+    )(*parts)
 
 
 def dgrad_kernel(place_ref, g_ref, gp_ref, out_ref, mask_ref, pick_ref, ret_ref, w_ref, o_ref, taps):
@@ -308,28 +299,25 @@
         place, x, peer_halo, out_halo, ids[None], owners[None], w3
     )
     xt_from = to_peer(xt_peer)
+    g, edge = gradient(place, returned, pick, slope)
+    g_peer = to_peer(g)
+    g_out = to_next_chip(edge)
+    placed, g = lax.optimization_barrier((placed, g))
     received = lax.all_to_all(placed, SEQ, 0, 0, tiled=True)
-    g = gradient(returned, pick, slope)
-    g_peer = to_peer(g)
-    g_out = to_next_chip(jnp.where(first, g[:DIL], g[-DIL:]))
-    a_parts, b_parts = wgrad(xt_mine, xt_from, g, g_peer)
-    a_parts, b_parts = spread(a_parts, "batch"), spread(b_parts, "y")
+    parts = spread(wgrad(xt_mine, xt_from, g, g_peer), "batch")
     input_grad = dgrad(place, g, g_peer, g_out, masks, pick, returned, w3)
-    a_next, b_next = sum_parts(a_parts, b_parts)
-    a_next, b_next, received, input_grad = lax.optimization_barrier(
-        (a_next, b_next, received, input_grad)
-    )
+    pieces = sum_parts(parts)
+    pieces, input_grad = lax.optimization_barrier((pieces, input_grad))
+    pieces = spread(pieces, "y")
+    by_xy = sum(part.astype(F32) for part in pieces).astype(BF)
+    by_xy = by_xy.reshape(3, NZ, REST, CH).transpose(1, 0, 2, 3)
+    by_xy, received = lax.optimization_barrier((by_xy, received))
     owner_rows = jnp.dot(received, proj, preferred_element_type=F32).astype(BF)
-    a_next, b_next = spread(a_next, "y"), spread(b_next, "batch")
-    by_xy = jnp.concatenate(
-        [sum(part.astype(F32) for part in parts) for parts in (a_next, b_next)], axis=-1
-    ).astype(BF)
-    by_xy = by_xy.reshape(3, NZ, REST, CH).transpose(1, 0, 2, 3)
-    by_xy, owner_rows = lax.optimization_barrier((by_xy, owner_rows))
     by_z = lax.all_to_all(by_xy, "z", 0, 0, tiled=True)
     by_z = jnp.sum(by_z.astype(F32), axis=0).astype(BF)
-    every = jnp.concatenate(gather_x(by_z), axis=1)
-    conv_grad = every.transpose(1, 0, 2).astype(F32)
+    copies = jnp.broadcast_to(by_z[None], (NX,) + by_z.shape)
+    every = lax.all_to_all(copies, "batch", 0, 0, tiled=True)
+    conv_grad = every.transpose(0, 2, 1, 3).reshape(OWN, 3, CH).astype(F32)
     return (
         owner_rows.reshape(1, 1, NZ * NY * NC, CAP, WIDE),
         input_grad[None],

time: 134 us -> 123 us (0.918)
  local copies, waits for them, and re-layouts: 3.78 us -> 13 us
  starting transfers between devices: 45 us -> 36 us
  Pallas kernels: 31.5 us -> 23.7 us
  waiting for transfers between devices: 24.1 us -> 21.8 us
    ppermute x15 -> x6, starting transfers between devices: 22.4 us -> 8.84 us  [spread(): got.append(lax.ppermute(pieces[d], axis, pairs))]
    unnamed x35 -> x28, local copies, waits for them, and re-layouts: 2.41 us -> 11.2 us
    pallas_call x3, Pallas kernels: 12.2 us -> 6.85 us  [the longest x1 4.3 us: wgrad(): pl.pallas_call(wgrad_kernel, grid=(CH // CHUNK,), in_specs=[xts, xts, col...]
    ppermute x15 -> x6, waiting for transfers between devices: 12 us -> 17 us  [spread(): got.append(lax.ppermute(pieces[d], axis, pairs))]
    all_to_all x1, waiting for transfers between devices: 9.64 us -> 4.85 us  [body(): returned = lax.all_to_all(back, SEQ, 0, 0, tiled=True)]
    all_to_all x0 -> x1, starting transfers between devices: none -> 4.5 us  [body(): every = lax.all_to_all(copies, 'batch', 0, 0, tiled=True)]
    all_to_all x1, starting transfers between devices: 15.2 us -> 12 us  [body(): returned = lax.all_to_all(back, SEQ, 0, 0, tiled=True)]
    ppermute x3, starting transfers between devices: 0.17 us -> 3.08 us  [to_peer(): return lax.ppermute(array, 'core', [(0, 1), (1, 0)])]
  transfers between devices with their start and end apart: 22 -> 14, of which waited for: 9 -> 6; matrix products, arithmetic and copies ran while one was open for 7% -> 6% of each run, Pallas kernels for 24% -> 20%
where the time goes in v3:
time: 123 us; the launch traced here: 120 us
  starting transfers between devices  36 us (29%)
  Pallas kernels  23.7 us (19%)
  waiting for transfers between devices  21.8 us (18%)
  blocking collectives  15.8 us (13%)
  local copies, waits for them, and re-layouts  13 us (11%)
  matrix products  7.36 us (6%)
  other arithmetic  1.75 us (1%)
    ppermute x6, waiting for transfers between devices, spread(): got.append(lax.ppermute(pieces[d], axis, pairs))  17 us
    all_to_all x1, blocking collectives, body(): by_z = lax.all_to_all(by_xy, 'z', 0, 0, tiled=True)  15.8 us
    all_to_all x1, starting transfers between devices, body(): returned = lax.all_to_all(back, SEQ, 0, 0, tiled=True)  12 us
    pallas_call x1, Pallas kernels, forward(): pl.pallas_call(forward_kernel, grid=(3,), in_specs=[SMEM_SPEC, whole((ROW...  11.5 us
    unnamed x28, local copies, waits for them, and re-layouts  11.2 us
    ppermute x6, starting transfers between devices, spread(): got.append(lax.ppermute(pieces[d], axis, pairs))  8.84 us
    all_to_all x1, starting transfers between devices, body(): received = lax.all_to_all(placed, SEQ, 0, 0, tiled=True)  6.13 us
    pallas_call x1, Pallas kernels, dgrad(): pl.pallas_call(dgrad_kernel, grid=(CH // CHUNK,), in_specs=[SMEM_SPEC, wh...  5.36 us
  transfers between devices with their start and end apart: 14, of which 6 were waited for; matrix products, arithmetic and copies ran while one was open for 6% of the time, Pallas kernels for 20%

profile of v3, /device:TPU:6, one launch (start us, length us, event | category | flops | bytes accessed | tf_op | source)
XLA Modules:
  0.0 120.4 jit_solution(1475964035500152569)
XLA Ops:
  3.2 3.0 %collective-permute-start = (bf16[32,896]{1,0:T(8,128)(2,1)S(1)}, bf16[32,896]{1,0:T(8,128)(2,1)S(1)}, u32[]{:S(2)}, u32[]{:S(2)}) collective-permute-start(bf16[32,896]{1,0:T(8,128)(2,1)S(1)} %get-tuple-element.62), channel_id=1, source_target_pairs={{0,4},{4,0},{1,5},{5,1},{2,6},{6,2},{3,7},{7,3},{8,12},{12,8},{9,1... | collective-permute-start | bytes 172040 | tf_op jit(solution)/shard_map/ppermute | solution.py:258
  6.3 3.7 %fusion.3 = bf16[512,768]{1,0:T(8,128)(2,1)} fusion(bf16[768,1536]{1,0:T(8,128)(2,1)S(1)} %copy-done, bf16[1,1,64,8,1536]{4,3,2,1,0:T(8,128)(2,1)} %param.11), kind=kOutput, calls=%fused_computation.4 | convolution fusion | flops 1208352768 | bytes 4718592 | tf_op jit(solution)/shard_map/dot_general | solution.py:294
  10.0 12.0 %all-to-all-start = ((bf16[64,8,768]{2,1,0:T(8,128)(2,1)}), bf16[64,8,768]{2,1,0:T(8,128)(2,1)S(1)}, u32[]{:S(2)}, u32[]{:S(2)}) async-start(bf16[64,8,768]{2,1,0:T(8,128)(2,1)} %bitcast.40), calls=%async_computation | async-start | bytes 1572864 | tf_op jit(solution)/shard_map/all_to_all | solution.py:296
  22.0 2.0 %copy-done.1 = bf16[768,3,768]{2,0,1:T(8,128)(2,1)S(1)} copy-done((bf16[768,3,768]{2,0,1:T(8,128)(2,1)S(1)}, bf16[768,3,768]{2,0,1:T(8,128)(2,1)}, u32[]{:S(2)}) %copy-start.1) | copy-done | bytes 3538968
  24.0 1.1 copy-done.8
  25.2 11.5 %forward.1 = (bf16[512,768]{1,0:T(8,128)(2,1)S(1)}, bf16[512,768]{1,0:T(8,128)(2,1)S(1)}, bf16[3,384,512]{2,1,0:T(8,128)(2,1)S(1)}, bf16[3,384,512]{2,1,0:T(8,12...) custom-call(s32[3]{0:T(128)S(1)} %pad_add_fusion.place_ref, bf16[512,768]{1,0:T(8,128)(2,1)S(1)} %bitcast.37, ...), custom_call_target="tpu_custom_call" | custom-call | tf_op jit(solution)/shard_map/forward/pallas_call | solution.py:132
  40.4 4.8 %all-to-all-done = bf16[64,8,768]{2,1,0:T(8,128)(2,1)S(1)} async-done(((bf16[64,8,768]{2,1,0:T(8,128)(2,1)}), bf16[64,8,768]{2,1,0:T(8,128)(2,1)S(1)}, u32[]{:S(2)}, u32[]{:S(2)}) %all-to-all-start) | async-done | bytes 786464 | tf_op jit(solution)/shard_map/all_to_all | solution.py:296
  46.3 1.1 copy-done.11
  47.4 2.3 %gradient.1 = (bf16[512,768]{1,0:T(8,128)(2,1)}, bf16[32,768]{1,0:T(8,128)(2,1)S(1)}) custom-call(s32[3]{0:T(128)S(1)} %pad_add_fusion.place_ref, bf16[512,768]{1,0:T(8,128)(2,1)S(1)} %bitcast.35, bf16[512,512]{1,0:T(8,128)(2,1)S(1)} %copy-done.4, bf16[512,768]{1,0:T(8,128)(2,1)S(1)} %copy-done.11), custom_call_target="tpu_custom_call" | custom-call | tf_op jit(solution)/shard_map/gradient/pallas_call | solution.py:167
  49.7 6.1 %all-to-all-start.1 = ((bf16[64,8,768]{2,1,0:T(8,128)(2,1)}), bf16[64,8,768]{2,1,0:T(8,128)(2,1)}, u32[]{:S(2)}, u32[]{:S(2)}) async-start(bf16[64,8,768]{2,1,0:T(8,128)(2,1)} %bitcast.38), calls=%async_computation.1 | async-start | bytes 1572864 | tf_op jit(solution)/shard_map/all_to_all | solution.py:306
  55.9 1.3 %copy-done.7 = bf16[3,384,512]{2,1,0:T(8,128)(2,1)S(1)} copy-done((bf16[3,384,512]{2,1,0:T(8,128)(2,1)S(1)}, bf16[3,384,512]{2,1,0:T(8,128)(2,1)}, u32[]{:S(2)}) %copy-start.7) | copy-done | bytes 1179672
  57.2 4.3 %wgrad.1 = (bf16[3,96,768]{2,1,0:T(8,128)(2,1)S(1)}, bf16[3,96,768]{2,1,0:T(8,128)(2,1)S(1)}, bf16[3,96,768]{2,1,0:T(8,128)(2,1)S(1)}, bf16[3,96,768]{2,1,0:T(8,128)(2,1)S(1)}) custom-call(bf16[3,384,512]{2,1,0:T(8,128)(2,1)S(1)} %copy-done.7, bf16[3,384,512]{2,1,0:T(8,128)(2,1)} %collective-permute-done.2.xtp_ref, ...), custom_call_target="tpu_custom_call" | custom-call | tf_op jit(solution)/shard_map/wgrad/pallas_call | solution.py:191
  62.0 2.4 %collective-permute-start.5 = (bf16[3,96,768]{2,1,0:T(8,128)(2,1)S(1)}, bf16[3,96,768]{2,1,0:T(8,128)(2,1)S(1)}, u32[]{:S(2)}, u32[]{:S(2)}) collective-permute-start(bf16[3,96,768]{2,1,0:T(8,128)(2,1)S(1)} %get-tuple-element.43), channel_id=1, source_target_pairs={{0,2},{1,3},{2,0},{3,1},{4,6},{5,7},{6,4},{7,5},{8,10},{9,11},{10,... | collective-permute-start | bytes 1327112 | tf_op jit(solution)/shard_map/ppermute | solution.py:272
  66.3 5.4 %dgrad.1 = bf16[512,768]{1,0:T(8,128)(2,1)} custom-call(s32[3]{0:T(128)S(1)} %pad_add_fusion.place_ref, bf16[512,768]{1,0:T(8,128)(2,1)} %get-tuple-element.40.g_ref, bf16[512,768]{1,0:T(8,128)(2,1)} %collective-permute-done.3.gp_ref, bf16[32,768]{1,0:T(8,128)(2,1)S(1)} %collective-permute-done.7.out_ref, ...), custom_call_target="tpu_custom_call" | custom-call | tf_op jit(solution)/shard_map/dgrad/pallas_call | solution.py:241
  71.7 2.9 %collective-permute-done.4.refs_1_ = bf16[3,96,768]{2,1,0:T(8,128)(2,1)S(1)} collective-permute-done((bf16[3,96,768]{2,1,0:T(8,128)(2,1)S(1)}, bf16[3,96,768]{2,1,0:T(8,128)(2,1)S(1)}, u32[]{:S(2)}, u32[]{:S(2)}) %collective-permute-start.4) | collective-permute-done | bytes 442400 | tf_op jit(solution)/shard_map/ppermute | solution.py:272
  74.6 2.1 %collective-permute-done.5.refs_2_ = bf16[3,96,768]{2,1,0:T(8,128)(2,1)S(1)} collective-permute-done((bf16[3,96,768]{2,1,0:T(8,128)(2,1)S(1)}, bf16[3,96,768]{2,1,0:T(8,128)(2,1)S(1)}, u32[]{:S(2)}, u32[]{:S(2)}) %collective-permute-start.5) | collective-permute-done | bytes 442400 | tf_op jit(solution)/shard_map/ppermute | solution.py:272
  76.7 8.1 %collective-permute-done.6.refs_3_ = bf16[3,96,768]{2,1,0:T(8,128)(2,1)S(1)} collective-permute-done((bf16[3,96,768]{2,1,0:T(8,128)(2,1)S(1)}, bf16[3,96,768]{2,1,0:T(8,128)(2,1)S(1)}, u32[]{:S(2)}, u32[]{:S(2)}) %collective-permute-start.6) | collective-permute-done | bytes 442400 | tf_op jit(solution)/shard_map/ppermute | solution.py:272
  85.0 1.7 %collective-permute-start.8 = (bf16[3,24,768]{2,1,0:T(8,128)(2,1)S(1)}, bf16[3,24,768]{2,1,0:T(8,128)(2,1)S(1)}, u32[]{:S(2)}, u32[]{:S(2)}) collective-permute-start(bf16[3,24,768]{2,1,0:T(8,128)(2,1)S(1)} %get-tuple-element.52), channel_id=1, source_target_pairs={{0,8},{8,16},{16,24},{24,0},{1,9},{9,17},{17,25},{25,1},{2,10},{10... | collective-permute-start | bytes 331784 | tf_op jit(solution)/shard_map/ppermute | solution.py:272
  86.8 2.7 %collective-permute-start.9 = (bf16[3,24,768]{2,1,0:T(8,128)(2,1)S(1)}, bf16[3,24,768]{2,1,0:T(8,128)(2,1)S(1)}, u32[]{:S(2)}, u32[]{:S(2)}) collective-permute-start(bf16[3,24,768]{2,1,0:T(8,128)(2,1)S(1)} %get-tuple-element.53), channel_id=1, source_target_pairs={{0,16},{8,24},{16,0},{24,8},{1,17},{9,25},{17,1},{25,9},{2,18},{10... | collective-permute-start | bytes 331784 | tf_op jit(solution)/shard_map/ppermute | solution.py:272
  89.5 1.5 %collective-permute-start.10 = (bf16[3,24,768]{2,1,0:T(8,128)(2,1)S(1)}, bf16[3,24,768]{2,1,0:T(8,128)(2,1)S(1)}, u32[]{:S(2)}, u32[]{:S(2)}) collective-permute-start(bf16[3,24,768]{2,1,0:T(8,128)(2,1)S(1)} %get-tuple-element.54), channel_id=1, source_target_pairs={{0,24},{8,0},{16,8},{24,16},{1,25},{9,1},{17,9},{25,17},{2,26},{10... | collective-permute-start | bytes 331784 | tf_op jit(solution)/shard_map/ppermute | solution.py:272
  91.3 3.5 %collective-permute-done.9 = bf16[3,24,768]{2,1,0:T(8,128)(2,1)S(1)} collective-permute-done((bf16[3,24,768]{2,1,0:T(8,128)(2,1)S(1)}, bf16[3,24,768]{2,1,0:T(8,128)(2,1)S(1)}, u32[]{:S(2)}, u32[]{:S(2)}) %collective-permute-start.9) | collective-permute-done | bytes 110624 | tf_op jit(solution)/shard_map/ppermute | solution.py:272
  95.0 15.8 %all_to_all.33 = bf16[8,3,3,768]{3,2,1,0:T(4,128)(2,1)S(1)} all-to-all(bf16[8,3,3,768]{3,2,1,0:T(4,128)(2,1)S(1)} %copy.9), channel_id=1, replica_groups=mesh['z'=8,'y'=4,'core'=2,'batch'=4] {'z'}, dimensions={0} | all-to-all | bytes 221184 | tf_op jit(solution)/shard_map/all_to_all | solution.py:316
  111.6 4.5 %all-to-all-start.3 = ((bf16[4,3,3,768]{3,1,2,0:T(4,128)(2,1)}), bf16[4,3,3,768]{3,1,2,0:T(4,128)(2,1)S(1)}, u32[]{:S(2)}, u32[]{:S(2)}) async-start(bf16[4,3,3,768]{3,1,2,0:T(4,128)(2,1)} %broadcast_in_dim.11), calls=%async_computation.3 | async-start | bytes 147456 | tf_op jit(solution)/shard_map/all_to_all | solution.py:319
  116.1 3.7 %fusion = bf16[1,1,64,8,1536]{4,3,2,1,0:T(8,128)(2,1)} fusion(bf16[512,768]{1,0:T(8,128)(2,1)} %bitcast.15, bf16[768,1536]{1,0:T(8,128)(2,1)S(1)} %copy-done), kind=kOutput, calls=%fused_computation.1 | convolution fusion | flops 1208745984 | bytes 4718592 | tf_op jit(solution)/shard_map/dot_general | solution.py:315
  (54 shorter events, 12.0 us)
Async XLA Ops:
  0.6 5.6 %copy-start = (bf16[768,1536]{1,0:T(8,128)(2,1)S(1)}, bf16[768,1536]{1,0:T(8,128)(2,1)}, u32[]{:S(2)}) copy-start(bf16[768,1536]{1,0:T(8,128)(2,1)} %param.10) | copy-start | bytes 7077892
  2.6 7.4 %collective-permute-start.1 = (bf16[32,896]{1,0:T(8,128)(2,1)S(1)}, bf16[32,896]{1,0:T(8,128)(2,1)S(1)}, u32[]{:S(2)}, u32[]{:S(2)}) collective-permute-start(bf16[32,896]{1,0:T(8,128)(2,1)S(1)} %get-tuple-element.61), channel_id=1, source_target_pairs={{8,4},{16,12},{24,20},{32,28},{40,36},{48,44},{56,52},{64,60},{72,... | collective-permute-start | bytes 172040 | tf_op jit(solution)/shard_map/ppermute | solution.py:264
  3.2 6.7 %collective-permute-start = (bf16[32,896]{1,0:T(8,128)(2,1)S(1)}, bf16[32,896]{1,0:T(8,128)(2,1)S(1)}, u32[]{:S(2)}, u32[]{:S(2)}) collective-permute-start(bf16[32,896]{1,0:T(8,128)(2,1)S(1)} %get-tuple-element.62), channel_id=1, source_target_pairs={{0,4},{4,0},{1,5},{5,1},{2,6},{6,2},{3,7},{7,3},{8,12},{12,8},{9,1... | collective-permute-start | bytes 172040 | tf_op jit(solution)/shard_map/ppermute | solution.py:258
  10.0 12.1 %copy-start.12 = (s32[1,512]{1,0:T(1,128)S(1)}, s32[1,512]{1,0:T(1,128)}, u32[]{:S(2)}) copy-start(s32[1,512]{1,0:T(1,128)} %ids_ref.1) | copy-start | bytes 6148
  10.0 12.1 %copy-start.13 = (s32[1,256,1]{1,2,0:T(1,128)S(1)}, s32[1,256,1]{1,2,0:T(1,128)}, u32[]{:S(2)}) copy-start(s32[1,256,1]{1,2,0:T(1,128)} %param.8) | copy-start | bytes 3076
  10.0 35.2 %all-to-all-start = ((bf16[64,8,768]{2,1,0:T(8,128)(2,1)}), bf16[64,8,768]{2,1,0:T(8,128)(2,1)S(1)}, u32[]{:S(2)}, u32[]{:S(2)}) async-start(bf16[64,8,768]{2,1,0:T(8,128)(2,1)} %bitcast.40), calls=%async_computation | async-start | bytes 1572864 | tf_op jit(solution)/shard_map/all_to_all | solution.py:296
  22.0 2.0 %copy-start.1 = (bf16[768,3,768]{2,0,1:T(8,128)(2,1)S(1)}, bf16[768,3,768]{2,0,1:T(8,128)(2,1)}, u32[]{:S(2)}) copy-start(bf16[768,3,768]{2,0,1:T(8,128)(2,1)} %param.9) | copy-start | bytes 10616836
  24.0 1.1 copy-start.8
  40.3 15.6 %collective-permute-start.2 = (bf16[3,384,512]{2,1,0:T(8,128)(2,1)}, bf16[3,384,512]{2,1,0:T(8,128)(2,1)}, u32[]{:S(2)}, u32[]{:S(2)}) collective-permute-start(bf16[3,384,512]{2,1,0:T(8,128)(2,1)} %get-tuple-element.34), channel_id=1, source_target_pairs={{0,4},{4,0},{1,5},{5,1},{2,6},{6,2},{3,7},{7,3},{8,12},{12,8},{9,1... | collective-permute-start | bytes 3538952 | tf_op jit(solution)/shard_map/ppermute | solution.py:258
  45.2 1.0 copy-start.4
  46.3 1.1 copy-start.11
  49.7 6.2 %collective-permute-start.3 = (bf16[512,768]{1,0:T(8,128)(2,1)}, bf16[512,768]{1,0:T(8,128)(2,1)}, u32[]{:S(2)}, u32[]{:S(2)}) collective-permute-start(bf16[512,768]{1,0:T(8,128)(2,1)} %get-tuple-element.40.g_ref), channel_id=1, source_target_pairs={{0,4},{4,0},{1,5},{5,1},{2,6},{6,2},{3,7},{7,3},{8,12},{12,8},{9,1... | collective-permute-start | bytes 2359304 | tf_op jit(solution)/shard_map/ppermute | solution.py:258
  49.7 45.2 %all-to-all-start.1 = ((bf16[64,8,768]{2,1,0:T(8,128)(2,1)}), bf16[64,8,768]{2,1,0:T(8,128)(2,1)}, u32[]{:S(2)}, u32[]{:S(2)}) async-start(bf16[64,8,768]{2,1,0:T(8,128)(2,1)} %bitcast.38), calls=%async_computation.1 | async-start | bytes 1572864 | tf_op jit(solution)/shard_map/all_to_all | solution.py:306
  55.9 1.3 %copy-start.7 = (bf16[3,384,512]{2,1,0:T(8,128)(2,1)S(1)}, bf16[3,384,512]{2,1,0:T(8,128)(2,1)}, u32[]{:S(2)}) copy-start(bf16[3,384,512]{2,1,0:T(8,128)(2,1)} %copy-done.6) | copy-start | bytes 3538948
  57.2 8.1 %copy-start.2 = (bf16[768,3,768]{2,0,1:T(8,128)(2,1)S(1)}, bf16[768,3,768]{2,0,1:T(8,128)(2,1)}, u32[]{:S(2)}) copy-start(bf16[768,3,768]{2,0,1:T(8,128)(2,1)} %param.9) | copy-start | bytes 10616836
  61.5 13.1 %collective-permute-start.4 = (bf16[3,96,768]{2,1,0:T(8,128)(2,1)S(1)}, bf16[3,96,768]{2,1,0:T(8,128)(2,1)S(1)}, u32[]{:S(2)}, u32[]{:S(2)}) collective-permute-start(bf16[3,96,768]{2,1,0:T(8,128)(2,1)S(1)} %get-tuple-element.42), channel_id=1, source_target_pairs={{0,1},{1,2},{2,3},{3,0},{4,5},{5,6},{6,7},{7,4},{8,9},{9,10},{10,1... | collective-permute-start | bytes 1327112 | tf_op jit(solution)/shard_map/ppermute | solution.py:272
  62.0 14.6 %collective-permute-start.5 = (bf16[3,96,768]{2,1,0:T(8,128)(2,1)S(1)}, bf16[3,96,768]{2,1,0:T(8,128)(2,1)S(1)}, u32[]{:S(2)}, u32[]{:S(2)}) collective-permute-start(bf16[3,96,768]{2,1,0:T(8,128)(2,1)S(1)} %get-tuple-element.43), channel_id=1, source_target_pairs={{0,2},{1,3},{2,0},{3,1},{4,6},{5,7},{6,4},{7,5},{8,10},{9,11},{10,... | collective-permute-start | bytes 1327112 | tf_op jit(solution)/shard_map/ppermute | solution.py:272
  64.4 20.4 %collective-permute-start.6 = (bf16[3,96,768]{2,1,0:T(8,128)(2,1)S(1)}, bf16[3,96,768]{2,1,0:T(8,128)(2,1)S(1)}, u32[]{:S(2)}, u32[]{:S(2)}) collective-permute-start(bf16[3,96,768]{2,1,0:T(8,128)(2,1)S(1)} %get-tuple-element.44), channel_id=1, source_target_pairs={{0,3},{1,0},{2,1},{3,2},{4,7},{5,4},{6,5},{7,6},{8,11},{9,8},{10,9... | collective-permute-start | bytes 1327112 | tf_op jit(solution)/shard_map/ppermute | solution.py:272
  64.4 0.8 collective-permute-start.7
  65.3 1.0 copy-start.5
  85.0 6.3 %collective-permute-start.8 = (bf16[3,24,768]{2,1,0:T(8,128)(2,1)S(1)}, bf16[3,24,768]{2,1,0:T(8,128)(2,1)S(1)}, u32[]{:S(2)}, u32[]{:S(2)}) collective-permute-start(bf16[3,24,768]{2,1,0:T(8,128)(2,1)S(1)} %get-tuple-element.52), channel_id=1, source_target_pairs={{0,8},{8,16},{16,24},{24,0},{1,9},{9,17},{17,25},{25,1},{2,10},{10... | collective-permute-start | bytes 331784 | tf_op jit(solution)/shard_map/ppermute | solution.py:272
  86.8 8.0 %collective-permute-start.9 = (bf16[3,24,768]{2,1,0:T(8,128)(2,1)S(1)}, bf16[3,24,768]{2,1,0:T(8,128)(2,1)S(1)}, u32[]{:S(2)}, u32[]{:S(2)}) collective-permute-start(bf16[3,24,768]{2,1,0:T(8,128)(2,1)S(1)} %get-tuple-element.53), channel_id=1, source_target_pairs={{0,16},{8,24},{16,0},{24,8},{1,17},{9,25},{17,1},{25,9},{2,18},{10... | collective-permute-start | bytes 331784 | tf_op jit(solution)/shard_map/ppermute | solution.py:272
  89.5 5.3 %collective-permute-start.10 = (bf16[3,24,768]{2,1,0:T(8,128)(2,1)S(1)}, bf16[3,24,768]{2,1,0:T(8,128)(2,1)S(1)}, u32[]{:S(2)}, u32[]{:S(2)}) collective-permute-start(bf16[3,24,768]{2,1,0:T(8,128)(2,1)S(1)} %get-tuple-element.54), channel_id=1, source_target_pairs={{0,24},{8,0},{16,8},{24,16},{1,25},{9,1},{17,9},{25,17},{2,26},{10... | collective-permute-start | bytes 331784 | tf_op jit(solution)/shard_map/ppermute | solution.py:272
  111.6 8.2 %all-to-all-start.3 = ((bf16[4,3,3,768]{3,1,2,0:T(4,128)(2,1)}), bf16[4,3,3,768]{3,1,2,0:T(4,128)(2,1)S(1)}, u32[]{:S(2)}, u32[]{:S(2)}) async-start(bf16[4,3,3,768]{3,1,2,0:T(4,128)(2,1)} %broadcast_in_dim.11), calls=%async_computation.3 | async-start | bytes 147456 | tf_op jit(solution)/shard_map/all_to_all | solution.py:319
  (4 other events, 3.6 us)

commit v4 on v3

--- a/solution.py
+++ b/solution.py
@@ -69,7 +69,7 @@
 
 def forward_kernel(
     place_ref, x_ref, peer_ref, out_ref, ids_ref, own_ref, w_ref,
-    slope_ref, placed_ref, xt_mine_ref, xt_peer_ref, pick_ref, mask_ref,
+    both_ref, placed_ref, xt_mine_ref, xt_peer_ref, mask_ref,
     taps, perm, pick_t, pair,
 ):
     j = pl.program_id(0)
@@ -108,15 +108,16 @@
         two = 2 * iota((TOKENS, ROWS), 0)
         pos = iota((TOKENS, ROWS), 1)
         pair[...] = jnp.where((pos == two) | (pos == two + 1), 0.5, 0.0).astype(BF)
-        pick_ref[...] = lax.dot_general(
+        both_ref[:, CH:] = lax.dot_general(
             pair[...], pick_t[...], (((0,), (1,)), ((), ())), preferred_element_type=F32
         ).astype(BF)
 
     preact = dot(taps[0], w_ref[0]) + dot(taps[1], w_ref[1]) + dot(taps[2], w_ref[2])
     cdf = 0.5 * (1.0 + lax.erf(preact * 0.7071067811865476))
     bell = jnp.exp(-0.5 * preact * preact) * 0.3989422804014327
-    slope_ref[...] = (cdf + preact * bell).astype(BF)
-    x_own = x_ref[:, pl.ds(pl.multiple_of(j * CHUNK, CHUNK), CHUNK)].astype(F32)
+    own_cols = pl.ds(pl.multiple_of(j * CHUNK, CHUNK), CHUNK)
+    both_ref[:, own_cols] = (cdf + preact * bell).astype(BF)
+    x_own = x_ref[:, own_cols].astype(F32)
     hidden = (x_own + preact * cdf).astype(BF)
     pooled = dot(pair[...], hidden).astype(BF)
     placed_ref[...] = dot(pick_t[...], pooled).astype(BF)
@@ -137,14 +138,13 @@
             whole((1, TOKENS)), pl.BlockSpec((3, CH, CHUNK), lambda j: (0, 0, j)),
         ],
         out_specs=[
-            pl.BlockSpec((ROWS, CHUNK), col), pl.BlockSpec((SLOTS, CHUNK), col),
+            whole((ROWS, CH + SLOTS)), pl.BlockSpec((SLOTS, CHUNK), col),
             pl.BlockSpec((1, HALF, ROWS), tap), pl.BlockSpec((1, HALF, ROWS), tap),
-            whole((ROWS, SLOTS)), whole((2, ROWS, LANES)),
+            whole((2, ROWS, LANES)),
         ],
         out_shape=[
-            jax.ShapeDtypeStruct((ROWS, CH), BF), jax.ShapeDtypeStruct((SLOTS, CH), BF),
+            jax.ShapeDtypeStruct((ROWS, CH + SLOTS), BF), jax.ShapeDtypeStruct((SLOTS, CH), BF),
             jax.ShapeDtypeStruct((3, HALF, ROWS), BF), jax.ShapeDtypeStruct((3, HALF, ROWS), BF),
-            jax.ShapeDtypeStruct((ROWS, SLOTS), BF),
             jax.ShapeDtypeStruct((2, ROWS, LANES), BF),
         ],
         scratch_shapes=[
@@ -156,26 +156,21 @@
     )(place, x, peer, out, ids, own, w3)
 
 
-def grad_kernel(place_ref, ret_ref, pick_ref, slope_ref, g_ref, edge_ref):
-    g = (dot(pick_ref[...], ret_ref[...]) * slope_ref[...].astype(F32)).astype(BF)
+def grad_kernel(place_ref, ret_ref, both_ref, g_ref, edge_ref):
+    g = dot(both_ref[:, CH:], ret_ref[...]) * both_ref[:, :CH].astype(F32)
+    g = g.astype(BF)
     g_ref[...] = g
     edge_ref[...] = jnp.where(place_ref[0] == 0, g[:DIL], g[ROWS - DIL :])
 
 
-def gradient(place, returned, pick, slope):
-    col = lambda j: (0, j)
+def gradient(place, returned, both):
     return pl.pallas_call(
         grad_kernel,
-        grid=(CH // HALF,),
-        in_specs=[
-            SMEM_SPEC, pl.BlockSpec((SLOTS, HALF), col), whole((ROWS, SLOTS)),
-            pl.BlockSpec((ROWS, HALF), col),
-        ],
-        out_specs=[pl.BlockSpec((ROWS, HALF), col), pl.BlockSpec((DIL, HALF), col)],
+        in_specs=[SMEM_SPEC] + [pl.BlockSpec(memory_space=pltpu.VMEM)] * 2,
         out_shape=[jax.ShapeDtypeStruct((ROWS, CH), BF), jax.ShapeDtypeStruct((DIL, CH), BF)],
         compiler_params=pltpu.CompilerParams(vmem_limit_bytes=VMEM),
         name="gradient",
-    )(place, returned, pick, slope)
+    )(place, returned, both)
 
 
 def wgrad_kernel(xt_ref, xtp_ref, g_ref, gp_ref, *outs):
@@ -217,7 +212,7 @@
     )(*parts)
 
 
-def dgrad_kernel(place_ref, g_ref, gp_ref, out_ref, mask_ref, pick_ref, ret_ref, w_ref, o_ref, taps):
+def dgrad_kernel(place_ref, g_ref, gp_ref, out_ref, mask_ref, both_ref, ret_ref, w_ref, o_ref, taps):
     @pl.when(pl.program_id(0) == 0)
     def _():
         first = place_ref[0] == 0
@@ -229,21 +224,21 @@
             for c in range(0, CH, LANES):
                 taps[i, :, c : c + LANES] = g_ext[low : low + ROWS, c : c + LANES] * mask_ref[i]
 
-    total = dot(pick_ref[...], ret_ref[...])
+    total = dot(both_ref[:, CH:], ret_ref[...])
     total += nt_dot(taps[1], w_ref[0])
     total += nt_dot(g_ref[...], w_ref[1])
     total += nt_dot(taps[0], w_ref[2])
     o_ref[...] = total.astype(BF)
 
 
-def dgrad(place, g, gp, out, masks, pick, returned, w3):
+def dgrad(place, g, gp, out, masks, both, returned, w3):
     col = lambda j: (0, j)
     return pl.pallas_call(
         dgrad_kernel,
         grid=(CH // CHUNK,),
         in_specs=[
             SMEM_SPEC, whole((ROWS, CH)), whole((ROWS, CH)), whole((DIL, CH)),
-            whole((2, ROWS, LANES)), whole((ROWS, SLOTS)), pl.BlockSpec((SLOTS, CHUNK), col),
+            whole((2, ROWS, LANES)), whole((ROWS, CH + SLOTS)), pl.BlockSpec((SLOTS, CHUNK), col),
             pl.BlockSpec((3, CHUNK, CH), lambda j: (0, j, 0)),
         ],
         out_specs=pl.BlockSpec((ROWS, CHUNK), col),
@@ -251,7 +246,7 @@
         scratch_shapes=[pltpu.VMEM((2, ROWS, CH), BF)],
         compiler_params=pltpu.CompilerParams(vmem_limit_bytes=VMEM),
         name="dgrad",
-    )(place, g, gp, out, masks, pick, returned, w3)
+    )(place, g, gp, out, masks, both, returned, w3)
 
 
 def to_peer(array):
@@ -295,17 +290,17 @@
     back, peer_halo, out_halo = lax.optimization_barrier((back, peer_halo, out_halo))
     returned = lax.all_to_all(back, SEQ, 0, 0, tiled=True)
     w3 = weight.transpose(1, 0, 2)
-    slope, placed, xt_mine, xt_peer, pick, masks = forward(
+    both, placed, xt_mine, xt_peer, masks = forward(
         place, x, peer_halo, out_halo, ids[None], owners[None], w3
     )
     xt_from = to_peer(xt_peer)
-    g, edge = gradient(place, returned, pick, slope)
+    g, edge = gradient(place, returned, both)
     g_peer = to_peer(g)
     g_out = to_next_chip(edge)
     placed, g = lax.optimization_barrier((placed, g))
     received = lax.all_to_all(placed, SEQ, 0, 0, tiled=True)
     parts = spread(wgrad(xt_mine, xt_from, g, g_peer), "batch")
-    input_grad = dgrad(place, g, g_peer, g_out, masks, pick, returned, w3)
+    input_grad = dgrad(place, g, g_peer, g_out, masks, both, returned, w3)
     pieces = sum_parts(parts)
     pieces, input_grad = lax.optimization_barrier((pieces, input_grad))
     pieces = spread(pieces, "y")
@@ -314,10 +309,10 @@
     by_xy, received = lax.optimization_barrier((by_xy, received))
     owner_rows = jnp.dot(received, proj, preferred_element_type=F32).astype(BF)
     by_z = lax.all_to_all(by_xy, "z", 0, 0, tiled=True)
+    by_z, owner_rows = lax.optimization_barrier((by_z, owner_rows))
     by_z = jnp.sum(by_z.astype(F32), axis=0).astype(BF)
-    copies = jnp.broadcast_to(by_z[None], (NX,) + by_z.shape)
-    every = lax.all_to_all(copies, "batch", 0, 0, tiled=True)
-    conv_grad = every.transpose(0, 2, 1, 3).reshape(OWN, 3, CH).astype(F32)
+    every = jnp.concatenate(gather_x(by_z), axis=1)
+    conv_grad = every.transpose(1, 0, 2).astype(F32)
     return (
         owner_rows.reshape(1, 1, NZ * NY * NC, CAP, WIDE),
         input_grad[None],

time: 123 us -> 121 us (0.984); the launches traced: 120 us -> 120 us
  blocking collectives: 15.8 us -> 0 us
  waiting for transfers between devices: 21.8 us -> 34.5 us
  starting transfers between devices: 36 us -> 40.5 us
    all_to_all x1 -> x0, blocking collectives: 15.8 us -> none  [body(): by_z = lax.all_to_all(by_xy, 'z', 0, 0, tiled=True)]
    ppermute x6 -> x9, waiting for transfers between devices: 17 us -> 23.4 us  [spread(): got.append(lax.ppermute(pieces[d], axis, pairs))]
    all_to_all x1, waiting for transfers between devices: 0.01 us -> 5.59 us  [body(): by_z = lax.all_to_all(by_xy, 'z', 0, 0, tiled=True)]
    all_to_all x1, starting transfers between devices: 12 us -> 15.2 us  [body(): returned = lax.all_to_all(back, SEQ, 0, 0, tiled=True)]
    ppermute x3, starting transfers between devices: 3.08 us -> 0.15 us  [to_peer(): return lax.ppermute(array, 'core', [(0, 1), (1, 0)])]
    all_to_all x1, starting transfers between devices: 4.5 us -> 6.78 us  [body(): by_z = lax.all_to_all(by_xy, 'z', 0, 0, tiled=True)]
    ppermute x6 -> x9, starting transfers between devices: 8.84 us -> 10.8 us  [spread(): got.append(lax.ppermute(pieces[d], axis, pairs))]
    unnamed x28 -> x25, local copies, waits for them, and re-layouts: 11.2 us -> 10.7 us
  transfers between devices with their start and end apart: 14 -> 17, of which waited for: 6 -> 10; matrix products, arithmetic and copies ran while one was open for 6% -> 6% of each run, Pallas kernels for 20% -> 19%
where the time goes in v4:
time: 121 us; the launch traced here: 120 us
  starting transfers between devices  40.5 us (33%)
  waiting for transfers between devices  34.5 us (29%)
  Pallas kernels  23.4 us (19%)
  local copies, waits for them, and re-layouts  12.7 us (10%)
  matrix products  7.37 us (6%)
    ppermute x9, waiting for transfers between devices, spread(): got.append(lax.ppermute(pieces[d], axis, pairs))  23.4 us
    all_to_all x1, starting transfers between devices, body(): returned = lax.all_to_all(back, SEQ, 0, 0, tiled=True)  15.2 us
    pallas_call x1, Pallas kernels, forward(): pl.pallas_call(forward_kernel, grid=(3,), in_specs=[SMEM_SPEC, whole((ROW...  11.5 us
    ppermute x9, starting transfers between devices, spread(): got.append(lax.ppermute(pieces[d], axis, pairs))  10.8 us
    unnamed x25, local copies, waits for them, and re-layouts  10.7 us
    all_to_all x1, starting transfers between devices, body(): by_z = lax.all_to_all(by_xy, 'z', 0, 0, tiled=True)  6.78 us
    all_to_all x1, starting transfers between devices, body(): received = lax.all_to_all(placed, SEQ, 0, 0, tiled=True)  6.06 us
    all_to_all x1, waiting for transfers between devices, body(): by_z = lax.all_to_all(by_xy, 'z', 0, 0, tiled=True)  5.59 us
  transfers between devices with their start and end apart: 17, of which 10 were waited for; matrix products, arithmetic and copies ran while one was open for 6% of the time, Pallas kernels for 19%

profile of v4, /device:TPU:6, one launch (start us, length us, event | category | flops | bytes accessed | tf_op | source)
XLA Modules:
  0.0 120.3 jit_solution(3854282983649787336)
XLA Ops:
  3.4 3.7 %fusion.2 = bf16[512,768]{1,0:T(8,128)(2,1)} fusion(bf16[768,1536]{1,0:T(8,128)(2,1)S(1)} %copy-done, bf16[1,1,64,8,1536]{4,3,2,1,0:T(8,128)(2,1)} %param.11), kind=kOutput, calls=%fused_computation.3 | convolution fusion | flops 1208352768 | bytes 4718592 | tf_op jit(solution)/shard_map/dot_general | solution.py:289
  7.1 15.2 %all-to-all-start = ((bf16[64,8,768]{2,1,0:T(8,128)(2,1)}), bf16[64,8,768]{2,1,0:T(8,128)(2,1)S(1)}, u32[]{:S(2)}, u32[]{:S(2)}) async-start(bf16[64,8,768]{2,1,0:T(8,128)(2,1)} %bitcast.51), calls=%async_computation | async-start | bytes 1572864 | tf_op jit(solution)/shard_map/all_to_all | solution.py:291
  22.4 2.0 %copy-done.1 = bf16[768,3,768]{2,0,1:T(8,128)(2,1)S(1)} copy-done((bf16[768,3,768]{2,0,1:T(8,128)(2,1)S(1)}, bf16[768,3,768]{2,0,1:T(8,128)(2,1)}, u32[]{:S(2)}) %copy-start.1) | copy-done | bytes 3538968
  25.5 11.5 %forward.1 = (bf16[512,1280]{1,0:T(8,128)(2,1)S(1)}, bf16[512,768]{1,0:T(8,128)(2,1)S(1)}, bf16[3,384,512]{2,1,0:T(8,128)(2,1)S(1)}, bf16[3,384,512]{2,1,0:T(8,128)(2,1)}, bf16[2,512,128]{2,1,0:T(8,128)(2,1)S(1)}) custom-call(s32[3]{0:T(128)S(1)} %pad_add_fusion.place_ref, bf16[512,768]{1,0:T(8,128)(2,1)S(1)} %bitcast.47, ...), custom_call_target="tpu_custom_call" | custom-call | tf_op jit(solution)/shard_map/forward/pallas_call | solution.py:133
  40.0 5.5 %all-to-all-done = bf16[64,8,768]{2,1,0:T(8,128)(2,1)S(1)} async-done(((bf16[64,8,768]{2,1,0:T(8,128)(2,1)}), bf16[64,8,768]{2,1,0:T(8,128)(2,1)S(1)}, u32[]{:S(2)}, u32[]{:S(2)}) %all-to-all-start) | async-done | bytes 786464 | tf_op jit(solution)/shard_map/all_to_all | solution.py:291
  45.6 1.3 %copy-done.4 = bf16[512,1280]{1,0:T(8,128)(2,1)S(1)} copy-done((bf16[512,1280]{1,0:T(8,128)(2,1)S(1)}, bf16[512,1280]{1,0:T(8,128)(2,1)}, u32[]{:S(2)}) %copy-start.4) | copy-done | bytes 1310744
  46.9 2.0 %gradient.1 = (bf16[512,768]{1,0:T(8,128)(2,1)}, bf16[32,768]{1,0:T(8,128)(2,1)S(1)}) custom-call(s32[3]{0:T(128)S(1)} %pad_add_fusion.place_ref, bf16[512,768]{1,0:T(8,128)(2,1)S(1)} %bitcast.45, bf16[512,1280]{1,0:T(8,128)(2,1)S(1)} %copy-done.4), custom_call_target="tpu_custom_call" | custom-call | tf_op jit(solution)/shard_map/gradient/pallas_call | solution.py:167
  48.9 6.1 %all-to-all-start.1 = ((bf16[64,8,768]{2,1,0:T(8,128)(2,1)}), bf16[64,8,768]{2,1,0:T(8,128)(2,1)}, u32[]{:S(2)}, u32[]{:S(2)}) async-start(bf16[64,8,768]{2,1,0:T(8,128)(2,1)} %bitcast.48), calls=%async_computation.1 | async-start | bytes 1572864 | tf_op jit(solution)/shard_map/all_to_all | solution.py:301
  56.3 4.3 %wgrad.1 = (bf16[3,96,768]{2,1,0:T(8,128)(2,1)S(1)}, bf16[3,96,768]{2,1,0:T(8,128)(2,1)S(1)}, bf16[3,96,768]{2,1,0:T(8,128)(2,1)S(1)}, bf16[3,96,768]{2,1,0:T(8,128)(2,1)S(1)}) custom-call(bf16[3,384,512]{2,1,0:T(8,128)(2,1)S(1)} %copy-done.7, bf16[3,384,512]{2,1,0:T(8,128)(2,1)} %collective-permute-done.2.xtp_ref, ...), custom_call_target="tpu_custom_call" | custom-call | tf_op jit(solution)/shard_map/wgrad/pallas_call | solution.py:186
  61.1 2.4 %collective-permute-start.5 = (bf16[3,96,768]{2,1,0:T(8,128)(2,1)S(1)}, bf16[3,96,768]{2,1,0:T(8,128)(2,1)S(1)}, u32[]{:S(2)}, u32[]{:S(2)}) collective-permute-start(bf16[3,96,768]{2,1,0:T(8,128)(2,1)S(1)} %get-tuple-element.43), channel_id=1, source_target_pairs={{0,2},{1,3},{2,0},{3,1},{4,6},{5,7},{6,4},{7,5},{8,10},{9,11},{10,... | collective-permute-start | bytes 1327112 | tf_op jit(solution)/shard_map/ppermute | solution.py:267
  65.7 5.4 %dgrad.1 = bf16[512,768]{1,0:T(8,128)(2,1)} custom-call(s32[3]{0:T(128)S(1)} %pad_add_fusion.place_ref, bf16[512,768]{1,0:T(8,128)(2,1)} %get-tuple-element.40.g_ref, bf16[512,768]{1,0:T(8,128)(2,1)} %collective-permute-done.3.gp_ref, bf16[32,768]{1,0:T(8,128)(2,1)S(1)} %collective-permute-done.7.out_ref, ...), custom_call_target="tpu_custom_call" | custom-call | tf_op jit(solution)/shard_map/dgrad/pallas_call | solution.py:236
  71.1 2.6 %collective-permute-done.4.refs_1_ = bf16[3,96,768]{2,1,0:T(8,128)(2,1)S(1)} collective-permute-done((bf16[3,96,768]{2,1,0:T(8,128)(2,1)S(1)}, bf16[3,96,768]{2,1,0:T(8,128)(2,1)S(1)}, u32[]{:S(2)}, u32[]{:S(2)}) %collective-permute-start.4) | collective-permute-done | bytes 442400 | tf_op jit(solution)/shard_map/ppermute | solution.py:267
  73.7 2.1 %collective-permute-done.5.refs_2_ = bf16[3,96,768]{2,1,0:T(8,128)(2,1)S(1)} collective-permute-done((bf16[3,96,768]{2,1,0:T(8,128)(2,1)S(1)}, bf16[3,96,768]{2,1,0:T(8,128)(2,1)S(1)}, u32[]{:S(2)}, u32[]{:S(2)}) %collective-permute-start.5) | collective-permute-done | bytes 442400 | tf_op jit(solution)/shard_map/ppermute | solution.py:267
  75.7 8.1 %collective-permute-done.6.refs_3_ = bf16[3,96,768]{2,1,0:T(8,128)(2,1)S(1)} collective-permute-done((bf16[3,96,768]{2,1,0:T(8,128)(2,1)S(1)}, bf16[3,96,768]{2,1,0:T(8,128)(2,1)S(1)}, u32[]{:S(2)}, u32[]{:S(2)}) %collective-permute-start.6) | collective-permute-done | bytes 442400 | tf_op jit(solution)/shard_map/ppermute | solution.py:267
  84.1 3.0 %collective-permute-start.10 = (bf16[3,24,768]{2,1,0:T(8,128)(2,1)S(1)}, bf16[3,24,768]{2,1,0:T(8,128)(2,1)S(1)}, u32[]{:S(2)}, u32[]{:S(2)}) collective-permute-start(bf16[3,24,768]{2,1,0:T(8,128)(2,1)S(1)} %get-tuple-element.54), channel_id=1, source_target_pairs={{0,24},{8,0},{16,8},{24,16},{1,25},{9,1},{17,9},{25,17},{2,26},{10... | collective-permute-start | bytes 331784 | tf_op jit(solution)/shard_map/ppermute | solution.py:267
  87.1 2.3 %collective-permute-start.9 = (bf16[3,24,768]{2,1,0:T(8,128)(2,1)S(1)}, bf16[3,24,768]{2,1,0:T(8,128)(2,1)S(1)}, u32[]{:S(2)}, u32[]{:S(2)}) collective-permute-start(bf16[3,24,768]{2,1,0:T(8,128)(2,1)S(1)} %get-tuple-element.53), channel_id=1, source_target_pairs={{0,16},{8,24},{16,0},{24,8},{1,17},{9,25},{17,1},{25,9},{2,18},{10... | collective-permute-start | bytes 331784 | tf_op jit(solution)/shard_map/ppermute | solution.py:267
  89.6 5.8 %collective-permute-done.8 = bf16[3,24,768]{2,1,0:T(8,128)(2,1)S(1)} collective-permute-done((bf16[3,24,768]{2,1,0:T(8,128)(2,1)S(1)}, bf16[3,24,768]{2,1,0:T(8,128)(2,1)S(1)}, u32[]{:S(2)}, u32[]{:S(2)}) %collective-permute-start.8) | collective-permute-done | bytes 110624 | tf_op jit(solution)/shard_map/ppermute | solution.py:267
  96.2 6.8 %all-to-all-start.2 = ((bf16[8,3,3,768]{3,2,1,0:T(4,128)(2,1)}), bf16[8,3,3,768]{3,2,1,0:T(4,128)(2,1)S(1)}, u32[]{:S(2)}, u32[]{:S(2)}) async-start(bf16[8,3,3,768]{3,2,1,0:T(4,128)(2,1)} %copy.11), calls=%async_computation.2 | async-start | bytes 294912 | tf_op jit(solution)/shard_map/all_to_all | solution.py:311
  103.0 3.7 %convolution_convert_fusion = bf16[512,1536]{1,0:T(8,128)(2,1)} fusion(bf16[512,768]{1,0:T(8,128)(2,1)} %bitcast.15, bf16[768,1536]{1,0:T(8,128)(2,1)S(1)} %copy-done), kind=kOutput, calls=%fused_computation | convolution fusion | flops 1208745984 | bytes 4718592 | tf_op jit(solution)/shard_map/dot_general | solution.py:310
  106.7 5.6 %all-to-all-done.2 = bf16[8,3,3,768]{3,2,1,0:T(4,128)(2,1)S(1)} async-done(((bf16[8,3,3,768]{3,2,1,0:T(4,128)(2,1)}), bf16[8,3,3,768]{3,2,1,0:T(4,128)(2,1)S(1)}, u32[]{:S(2)}, u32[]{:S(2)}) %all-to-all-start.2) | async-done | bytes 110624 | tf_op jit(solution)/shard_map/all_to_all | solution.py:311
  112.7 1.8 %collective-permute-start.12 = (bf16[3,3,768]{2,1,0:T(4,128)(2,1)S(1)}, bf16[3,3,768]{2,1,0:T(4,128)(2,1)S(1)}, u32[]{:S(2)}, u32[]{:S(2)}) collective-permute-start(bf16[3,3,768]{2,1,0:T(4,128)(2,1)S(1)} %reduce_sum.12), channel_id=1, source_target_pairs={{0,2},{1,3},{2,0},{3,1},{4,6},{5,7},{6,4},{7,5},{8,10},{9,11},{10,... | collective-permute-start | bytes 41480 | tf_op jit(solution)/shard_map/ppermute | solution.py:267
  114.8 1.3 %collective-permute-done.11 = bf16[3,3,768]{2,1,0:T(4,128)(2,1)S(1)} collective-permute-done((bf16[3,3,768]{2,1,0:T(4,128)(2,1)S(1)}, bf16[3,3,768]{2,1,0:T(4,128)(2,1)S(1)}, u32[]{:S(2)}, u32[]{:S(2)}) %collective-permute-start.11) | collective-permute-done | bytes 13856 | tf_op jit(solution)/shard_map/ppermute | solution.py:267
  116.2 1.8 %collective-permute-done.12 = bf16[3,3,768]{2,1,0:T(4,128)(2,1)S(1)} collective-permute-done((bf16[3,3,768]{2,1,0:T(4,128)(2,1)S(1)}, bf16[3,3,768]{2,1,0:T(4,128)(2,1)S(1)}, u32[]{:S(2)}, u32[]{:S(2)}) %collective-permute-start.12) | collective-permute-done | bytes 13856 | tf_op jit(solution)/shard_map/ppermute | solution.py:267
  117.9 1.5 %collective-permute-done.13 = bf16[3,3,768]{2,1,0:T(4,128)(2,1)S(1)} collective-permute-done((bf16[3,3,768]{2,1,0:T(4,128)(2,1)S(1)}, bf16[3,3,768]{2,1,0:T(4,128)(2,1)S(1)}, u32[]{:S(2)}, u32[]{:S(2)}) %collective-permute-start.13) | collective-permute-done | bytes 13856 | tf_op jit(solution)/shard_map/ppermute | solution.py:267
  (56 shorter events, 13.8 us)
Async XLA Ops:
  0.6 2.7 %copy-start = (bf16[768,1536]{1,0:T(8,128)(2,1)S(1)}, bf16[768,1536]{1,0:T(8,128)(2,1)}, u32[]{:S(2)}) copy-start(bf16[768,1536]{1,0:T(8,128)(2,1)} %param.10) | copy-start | bytes 7077892
  2.6 4.5 %collective-permute-start = (bf16[32,896]{1,0:T(8,128)(2,1)S(1)}, bf16[32,896]{1,0:T(8,128)(2,1)S(1)}, u32[]{:S(2)}, u32[]{:S(2)}) collective-permute-start(bf16[32,896]{1,0:T(8,128)(2,1)S(1)} %get-tuple-element.67), channel_id=1, source_target_pairs={{0,4},{4,0},{1,5},{5,1},{2,6},{6,2},{3,7},{7,3},{8,12},{12,8},{9,1... | collective-permute-start | bytes 172040 | tf_op jit(solution)/shard_map/ppermute | solution.py:253
  2.7 4.4 %collective-permute-start.1 = (bf16[32,896]{1,0:T(8,128)(2,1)S(1)}, bf16[32,896]{1,0:T(8,128)(2,1)S(1)}, u32[]{:S(2)}, u32[]{:S(2)}) collective-permute-start(bf16[32,896]{1,0:T(8,128)(2,1)S(1)} %get-tuple-element.66), channel_id=1, source_target_pairs={{8,4},{16,12},{24,20},{32,28},{40,36},{48,44},{56,52},{64,60},{72,... | collective-permute-start | bytes 172040 | tf_op jit(solution)/shard_map/ppermute | solution.py:259
  7.1 15.3 %copy-start.10 = (s32[1,512]{1,0:T(1,128)S(1)}, s32[1,512]{1,0:T(1,128)}, u32[]{:S(2)}) copy-start(s32[1,512]{1,0:T(1,128)} %ids_ref.1) | copy-start | bytes 6148
  7.1 15.3 %copy-start.11 = (s32[1,256,1]{1,2,0:T(1,128)S(1)}, s32[1,256,1]{1,2,0:T(1,128)}, u32[]{:S(2)}) copy-start(s32[1,256,1]{1,2,0:T(1,128)} %param.8) | copy-start | bytes 3076
  7.1 38.5 %all-to-all-start = ((bf16[64,8,768]{2,1,0:T(8,128)(2,1)}), bf16[64,8,768]{2,1,0:T(8,128)(2,1)S(1)}, u32[]{:S(2)}, u32[]{:S(2)}) async-start(bf16[64,8,768]{2,1,0:T(8,128)(2,1)} %bitcast.51), calls=%async_computation | async-start | bytes 1572864 | tf_op jit(solution)/shard_map/all_to_all | solution.py:291
  22.4 2.0 %copy-start.1 = (bf16[768,3,768]{2,0,1:T(8,128)(2,1)S(1)}, bf16[768,3,768]{2,0,1:T(8,128)(2,1)}, u32[]{:S(2)}) copy-start(bf16[768,3,768]{2,0,1:T(8,128)(2,1)} %param.9) | copy-start | bytes 10616836
  40.0 15.0 %collective-permute-start.2 = (bf16[3,384,512]{2,1,0:T(8,128)(2,1)}, bf16[3,384,512]{2,1,0:T(8,128)(2,1)}, u32[]{:S(2)}, u32[]{:S(2)}) collective-permute-start(bf16[3,384,512]{2,1,0:T(8,128)(2,1)} %get-tuple-element.35), channel_id=1, source_target_pairs={{0,4},{4,0},{1,5},{5,1},{2,6},{6,2},{3,7},{7,3},{8,12},{12,8},{9,1... | collective-permute-start | bytes 3538952 | tf_op jit(solution)/shard_map/ppermute | solution.py:253
  45.6 1.3 %copy-start.4 = (bf16[512,1280]{1,0:T(8,128)(2,1)S(1)}, bf16[512,1280]{1,0:T(8,128)(2,1)}, u32[]{:S(2)}) copy-start(bf16[512,1280]{1,0:T(8,128)(2,1)} %copy-done.3) | copy-start | bytes 3932164
  48.9 6.1 %collective-permute-start.3 = (bf16[512,768]{1,0:T(8,128)(2,1)}, bf16[512,768]{1,0:T(8,128)(2,1)}, u32[]{:S(2)}, u32[]{:S(2)}) collective-permute-start(bf16[512,768]{1,0:T(8,128)(2,1)} %get-tuple-element.40.g_ref), channel_id=1, source_target_pairs={{0,4},{4,0},{1,5},{5,1},{2,6},{6,2},{3,7},{7,3},{8,12},{12,8},{9,1... | collective-permute-start | bytes 2359304 | tf_op jit(solution)/shard_map/ppermute | solution.py:253
  48.9 46.6 %all-to-all-start.1 = ((bf16[64,8,768]{2,1,0:T(8,128)(2,1)}), bf16[64,8,768]{2,1,0:T(8,128)(2,1)}, u32[]{:S(2)}, u32[]{:S(2)}) async-start(bf16[64,8,768]{2,1,0:T(8,128)(2,1)} %bitcast.48), calls=%async_computation.1 | async-start | bytes 1572864 | tf_op jit(solution)/shard_map/all_to_all | solution.py:301
  56.3 8.1 %copy-start.2 = (bf16[768,3,768]{2,0,1:T(8,128)(2,1)S(1)}, bf16[768,3,768]{2,0,1:T(8,128)(2,1)}, u32[]{:S(2)}) copy-start(bf16[768,3,768]{2,0,1:T(8,128)(2,1)} %param.9) | copy-start | bytes 10616836
  60.6 13.1 %collective-permute-start.4 = (bf16[3,96,768]{2,1,0:T(8,128)(2,1)S(1)}, bf16[3,96,768]{2,1,0:T(8,128)(2,1)S(1)}, u32[]{:S(2)}, u32[]{:S(2)}) collective-permute-start(bf16[3,96,768]{2,1,0:T(8,128)(2,1)S(1)} %get-tuple-element.42), channel_id=1, source_target_pairs={{0,1},{1,2},{2,3},{3,0},{4,5},{5,6},{6,7},{7,4},{8,9},{9,10},{10,1... | collective-permute-start | bytes 1327112 | tf_op jit(solution)/shard_map/ppermute | solution.py:267
  61.1 14.6 %collective-permute-start.5 = (bf16[3,96,768]{2,1,0:T(8,128)(2,1)S(1)}, bf16[3,96,768]{2,1,0:T(8,128)(2,1)S(1)}, u32[]{:S(2)}, u32[]{:S(2)}) collective-permute-start(bf16[3,96,768]{2,1,0:T(8,128)(2,1)S(1)} %get-tuple-element.43), channel_id=1, source_target_pairs={{0,2},{1,3},{2,0},{3,1},{4,6},{5,7},{6,4},{7,5},{8,10},{9,11},{10,... | collective-permute-start | bytes 1327112 | tf_op jit(solution)/shard_map/ppermute | solution.py:267
  63.5 20.3 %collective-permute-start.6 = (bf16[3,96,768]{2,1,0:T(8,128)(2,1)S(1)}, bf16[3,96,768]{2,1,0:T(8,128)(2,1)S(1)}, u32[]{:S(2)}, u32[]{:S(2)}) collective-permute-start(bf16[3,96,768]{2,1,0:T(8,128)(2,1)S(1)} %get-tuple-element.44), channel_id=1, source_target_pairs={{0,3},{1,0},{2,1},{3,2},{4,7},{5,4},{6,5},{7,6},{8,11},{9,8},{10,9... | collective-permute-start | bytes 1327112 | tf_op jit(solution)/shard_map/ppermute | solution.py:267
  63.5 0.8 collective-permute-start.7
  64.4 1.3 %copy-start.5 = (bf16[512,1280]{1,0:T(8,128)(2,1)S(1)}, bf16[512,1280]{1,0:T(8,128)(2,1)}, u32[]{:S(2)}) copy-start(bf16[512,1280]{1,0:T(8,128)(2,1)} %copy-done.3) | copy-start | bytes 3932164
  84.1 5.5 %collective-permute-start.10 = (bf16[3,24,768]{2,1,0:T(8,128)(2,1)S(1)}, bf16[3,24,768]{2,1,0:T(8,128)(2,1)S(1)}, u32[]{:S(2)}, u32[]{:S(2)}) collective-permute-start(bf16[3,24,768]{2,1,0:T(8,128)(2,1)S(1)} %get-tuple-element.54), channel_id=1, source_target_pairs={{0,24},{8,0},{16,8},{24,16},{1,25},{9,1},{17,9},{25,17},{2,26},{10... | collective-permute-start | bytes 331784 | tf_op jit(solution)/shard_map/ppermute | solution.py:267
  87.1 8.3 %collective-permute-start.8 = (bf16[3,24,768]{2,1,0:T(8,128)(2,1)S(1)}, bf16[3,24,768]{2,1,0:T(8,128)(2,1)S(1)}, u32[]{:S(2)}, u32[]{:S(2)}) collective-permute-start(bf16[3,24,768]{2,1,0:T(8,128)(2,1)S(1)} %get-tuple-element.52), channel_id=1, source_target_pairs={{0,8},{8,16},{16,24},{24,0},{1,9},{9,17},{17,25},{25,1},{2,10},{10... | collective-permute-start | bytes 331784 | tf_op jit(solution)/shard_map/ppermute | solution.py:267
  87.1 8.3 %collective-permute-start.9 = (bf16[3,24,768]{2,1,0:T(8,128)(2,1)S(1)}, bf16[3,24,768]{2,1,0:T(8,128)(2,1)S(1)}, u32[]{:S(2)}, u32[]{:S(2)}) collective-permute-start(bf16[3,24,768]{2,1,0:T(8,128)(2,1)S(1)} %get-tuple-element.53), channel_id=1, source_target_pairs={{0,16},{8,24},{16,0},{24,8},{1,17},{9,25},{17,1},{25,9},{2,18},{10... | collective-permute-start | bytes 331784 | tf_op jit(solution)/shard_map/ppermute | solution.py:267
  96.2 16.0 %all-to-all-start.2 = ((bf16[8,3,3,768]{3,2,1,0:T(4,128)(2,1)}), bf16[8,3,3,768]{3,2,1,0:T(4,128)(2,1)S(1)}, u32[]{:S(2)}, u32[]{:S(2)}) async-start(bf16[8,3,3,768]{3,2,1,0:T(4,128)(2,1)} %copy.11), calls=%async_computation.2 | async-start | bytes 294912 | tf_op jit(solution)/shard_map/all_to_all | solution.py:311
  112.3 3.8 %collective-permute-start.11 = (bf16[3,3,768]{2,1,0:T(4,128)(2,1)S(1)}, bf16[3,3,768]{2,1,0:T(4,128)(2,1)S(1)}, u32[]{:S(2)}, u32[]{:S(2)}) collective-permute-start(bf16[3,3,768]{2,1,0:T(4,128)(2,1)S(1)} %reduce_sum.12), channel_id=1, source_target_pairs={{0,1},{1,2},{2,3},{3,0},{4,5},{5,6},{6,7},{7,4},{8,9},{9,10},{10,1... | collective-permute-start | bytes 41480 | tf_op jit(solution)/shard_map/ppermute | solution.py:267
  112.7 5.3 %collective-permute-start.12 = (bf16[3,3,768]{2,1,0:T(4,128)(2,1)S(1)}, bf16[3,3,768]{2,1,0:T(4,128)(2,1)S(1)}, u32[]{:S(2)}, u32[]{:S(2)}) collective-permute-start(bf16[3,3,768]{2,1,0:T(4,128)(2,1)S(1)} %reduce_sum.12), channel_id=1, source_target_pairs={{0,2},{1,3},{2,0},{3,1},{4,6},{5,7},{6,4},{7,5},{8,10},{9,11},{10,... | collective-permute-start | bytes 41480 | tf_op jit(solution)/shard_map/ppermute | solution.py:267
  114.5 5.0 %collective-permute-start.13 = (bf16[3,3,768]{2,1,0:T(4,128)(2,1)S(1)}, bf16[3,3,768]{2,1,0:T(4,128)(2,1)S(1)}, u32[]{:S(2)}, u32[]{:S(2)}) collective-permute-start(bf16[3,3,768]{2,1,0:T(4,128)(2,1)S(1)} %reduce_sum.12), channel_id=1, source_target_pairs={{0,3},{1,0},{2,1},{3,2},{4,7},{5,4},{6,5},{7,6},{8,11},{9,8},{10,9... | collective-permute-start | bytes 41480 | tf_op jit(solution)/shard_map/ppermute | solution.py:267
  (5 other events, 5.3 us)

commit v5 on v4

--- a/solution.py
+++ b/solution.py
@@ -180,27 +180,30 @@
             outs[d][k] = total[d * PART : (d + 1) * PART].astype(BF)
 
 
-def wgrad(xt, xt_peer, g, gp):
-    cols = pl.BlockSpec((ROWS, CHUNK), lambda j: (0, j))
+def wgrad(xt, xt_peer, g, gp, side):
+    cols = pl.BlockSpec((ROWS, HALF), lambda j: (0, side))
     xts = whole((3, HALF, ROWS))
     return pl.pallas_call(
         wgrad_kernel,
-        grid=(CH // CHUNK,),
+        grid=(1,),
         in_specs=[xts, xts, cols, cols],
-        out_specs=[pl.BlockSpec((3, PART, CHUNK), lambda j: (0, 0, j))] * NX,
-        out_shape=[jax.ShapeDtypeStruct((3, PART, CH), BF)] * NX,
-        compiler_params=pltpu.CompilerParams(vmem_limit_bytes=VMEM),
-        name="wgrad",
+        out_specs=[whole((3, PART, HALF))] * NX,
+        out_shape=[jax.ShapeDtypeStruct((3, PART, HALF), BF)] * NX,
+        compiler_params=pltpu.CompilerParams(vmem_limit_bytes=VMEM),
+        name="wgrad%d" % side,
     )(xt, xt_peer, g, gp)
 
 
 def sum_kernel(*refs):
-    ins, outs = refs[:NX], refs[NX:]
-    total = ins[0][...].astype(F32)
-    for ref in ins[1:]:
-        total += ref[...].astype(F32)
-    for d in range(NY):
-        outs[d][...] = total[:, d * PIECE : (d + 1) * PIECE].astype(BF)
+    outs = refs[2 * NX :]
+    for side in (0, 1):
+        ins = refs[side * NX : side * NX + NX]
+        total = ins[0][...].astype(F32)
+        for ref in ins[1:]:
+            total += ref[...].astype(F32)
+        for d in range(NY):
+            piece = total[:, d * PIECE : (d + 1) * PIECE].astype(BF)
+            outs[d][:, :, side * HALF : (side + 1) * HALF] = piece
 
 
 def sum_parts(parts):
@@ -299,7 +302,9 @@
     g_out = to_next_chip(edge)
     placed, g = lax.optimization_barrier((placed, g))
     received = lax.all_to_all(placed, SEQ, 0, 0, tiled=True)
-    parts = spread(wgrad(xt_mine, xt_from, g, g_peer), "batch")
+    parts = []
+    for side in (0, 1):
+        parts += spread(wgrad(xt_mine, xt_from, g, g_peer, side), "batch")
     input_grad = dgrad(place, g, g_peer, g_out, masks, both, returned, w3)
     pieces = sum_parts(parts)
     pieces, input_grad = lax.optimization_barrier((pieces, input_grad))

time: 121 us -> 122 us (level)
  starting transfers between devices: 40.5 us -> 48 us
  waiting for transfers between devices: 34.5 us -> 27.7 us
  Pallas kernels: 23.4 us -> 25 us
  local copies, waits for them, and re-layouts: 12.7 us -> 11.4 us
    ppermute x9 -> x12, starting transfers between devices: 10.8 us -> 18.7 us  [spread(): got.append(lax.ppermute(pieces[d], axis, pairs))]
    ppermute x9 -> x12, waiting for transfers between devices: 23.4 us -> 16.5 us  [spread(): got.append(lax.ppermute(pieces[d], axis, pairs))]
    pallas_call x1 -> x2, Pallas kernels: 4.3 us -> 5.95 us  [wgrad(): pl.pallas_call(wgrad_kernel, grid=(1,), in_specs=[xts, xts, cols, cols],...]
    unnamed x25, local copies, waits for them, and re-layouts: 10.7 us -> 9.43 us
  transfers between devices with their start and end apart: 17 -> 20, of which waited for: 10 -> 9; matrix products, arithmetic and copies ran while one was open for 6% -> 6% of each run, Pallas kernels for 19% -> 21%
where the time goes in v5:
time: 122 us; the launch traced here: 121 us
  starting transfers between devices  48 us (39%)
  waiting for transfers between devices  27.7 us (23%)
  Pallas kernels  25 us (20%)
  local copies, waits for them, and re-layouts  11.4 us (9%)
  matrix products  7.37 us (6%)
    ppermute x12, starting transfers between devices, spread(): got.append(lax.ppermute(pieces[d], axis, pairs))  18.7 us
    ppermute x12, waiting for transfers between devices, spread(): got.append(lax.ppermute(pieces[d], axis, pairs))  16.5 us
    all_to_all x1, starting transfers between devices, body(): returned = lax.all_to_all(back, SEQ, 0, 0, tiled=True)  15.2 us
    pallas_call x1, Pallas kernels, forward(): pl.pallas_call(forward_kernel, grid=(3,), in_specs=[SMEM_SPEC, whole((ROW...  11.5 us
    unnamed x25, local copies, waits for them, and re-layouts  9.43 us
    all_to_all x1, starting transfers between devices, body(): by_z = lax.all_to_all(by_xy, 'z', 0, 0, tiled=True)  6.54 us
    all_to_all x1, starting transfers between devices, body(): received = lax.all_to_all(placed, SEQ, 0, 0, tiled=True)  6.06 us
    pallas_call x2, Pallas kernels, wgrad(): pl.pallas_call(wgrad_kernel, grid=(1,), in_specs=[xts, xts, cols, cols],...  5.95 us
  transfers between devices with their start and end apart: 20, of which 9 were waited for; matrix products, arithmetic and copies ran while one was open for 6% of the time, Pallas kernels for 21%

profile of v5, /device:TPU:6, one launch (start us, length us, event | category | flops | bytes accessed | tf_op | source)
XLA Modules:
  0.0 121.4 jit_solution(15315982768985062189)
XLA Ops:
  3.4 3.7 %fusion.2 = bf16[512,768]{1,0:T(8,128)(2,1)} fusion(bf16[768,1536]{1,0:T(8,128)(2,1)S(1)} %copy-done, bf16[1,1,64,8,1536]{4,3,2,1,0:T(8,128)(2,1)} %param.11), kind=kOutput, calls=%fused_computation.3 | convolution fusion | flops 1208352768 | bytes 4718592 | tf_op jit(solution)/shard_map/dot_general | solution.py:292
  7.1 15.2 %all-to-all-start = ((bf16[64,8,768]{2,1,0:T(8,128)(2,1)}), bf16[64,8,768]{2,1,0:T(8,128)(2,1)S(1)}, u32[]{:S(2)}, u32[]{:S(2)}) async-start(bf16[64,8,768]{2,1,0:T(8,128)(2,1)} %bitcast.51), calls=%async_computation | async-start | bytes 1572864 | tf_op jit(solution)/shard_map/all_to_all | solution.py:294
  22.4 2.0 %copy-done.1 = bf16[768,3,768]{2,0,1:T(8,128)(2,1)S(1)} copy-done((bf16[768,3,768]{2,0,1:T(8,128)(2,1)S(1)}, bf16[768,3,768]{2,0,1:T(8,128)(2,1)}, u32[]{:S(2)}) %copy-start.1) | copy-done | bytes 3538968
  25.5 11.5 %forward.1 = (bf16[512,1280]{1,0:T(8,128)(2,1)S(1)}, bf16[512,768]{1,0:T(8,128)(2,1)S(1)}, bf16[3,384,512]{2,1,0:T(8,128)(2,1)S(1)}, bf16[3,384,512]{2,1,0:T(8,128)(2,1)}, bf16[2,512,128]{2,1,0:T(8,128)(2,1)S(1)}) custom-call(s32[3]{0:T(128)S(1)} %pad_add_fusion.place_ref, bf16[512,768]{1,0:T(8,128)(2,1)S(1)} %bitcast.47, ...), custom_call_target="tpu_custom_call" | custom-call | tf_op jit(solution)/shard_map/forward/pallas_call | solution.py:133
  40.0 5.6 %all-to-all-done = bf16[64,8,768]{2,1,0:T(8,128)(2,1)S(1)} async-done(((bf16[64,8,768]{2,1,0:T(8,128)(2,1)}), bf16[64,8,768]{2,1,0:T(8,128)(2,1)S(1)}, u32[]{:S(2)}, u32[]{:S(2)}) %all-to-all-start) | async-done | bytes 786464 | tf_op jit(solution)/shard_map/all_to_all | solution.py:294
  46.9 2.0 %gradient.1 = (bf16[512,768]{1,0:T(8,128)(2,1)}, bf16[32,768]{1,0:T(8,128)(2,1)S(1)}) custom-call(s32[3]{0:T(128)S(1)} %pad_add_fusion.place_ref, bf16[512,768]{1,0:T(8,128)(2,1)S(1)} %bitcast.45, bf16[512,1280]{1,0:T(8,128)(2,1)S(1)} %copy-done.4), custom_call_target="tpu_custom_call" | custom-call | tf_op jit(solution)/shard_map/gradient/pallas_call | solution.py:167
  48.9 6.1 %all-to-all-start.1 = ((bf16[64,8,768]{2,1,0:T(8,128)(2,1)}), bf16[64,8,768]{2,1,0:T(8,128)(2,1)}, u32[]{:S(2)}, u32[]{:S(2)}) async-start(bf16[64,8,768]{2,1,0:T(8,128)(2,1)} %bitcast.48), calls=%async_computation.1 | async-start | bytes 1572864 | tf_op jit(solution)/shard_map/all_to_all | solution.py:304
  56.3 3.0 %wgrad1.1 = (bf16[3,96,384]{2,1,0:T(8,128)(2,1)S(1)}, bf16[3,96,384]{2,1,0:T(8,128)(2,1)S(1)}, bf16[3,96,384]{2,1,0:T(8,128)(2,1)S(1)}, bf16[3,96,384]{2,1,0:T(8,128)(2,1)S(1)}) custom-call(bf16[3,384,512]{2,1,0:T(8,128)(2,1)S(1)} %copy-done.7, bf16[3,384,512]{2,1,0:T(8,128)(2,1)} %collective-permute-done.2.xtp_ref, ...), custom_call_target="tpu_custom_call" | custom-call | tf_op jit(solution)/shard_map/wgrad1/pallas_call | solution.py:186
  60.4 2.5 %collective-permute-start.8 = (bf16[3,96,384]{2,1,0:T(8,128)(2,1)S(1)}, bf16[3,96,384]{2,1,0:T(8,128)(2,1)S(1)}, u32[]{:S(2)}, u32[]{:S(2)}) collective-permute-start(bf16[3,96,384]{2,1,0:T(8,128)(2,1)S(1)} %get-tuple-element.51), channel_id=1, source_target_pairs={{0,2},{1,3},{2,0},{3,1},{4,6},{5,7},{6,4},{7,5},{8,10},{9,11},{10,... | collective-permute-start | bytes 663560 | tf_op jit(solution)/shard_map/ppermute | solution.py:270
  63.0 3.0 %wgrad0.1 = (bf16[3,96,384]{2,1,0:T(8,128)(2,1)S(1)}, bf16[3,96,384]{2,1,0:T(8,128)(2,1)S(1)}, bf16[3,96,384]{2,1,0:T(8,128)(2,1)S(1)}, bf16[3,96,384]{2,1,0:T(8,128)(2,1)S(1)}) custom-call(bf16[3,384,512]{2,1,0:T(8,128)(2,1)S(1)} %copy-done.7, bf16[3,384,512]{2,1,0:T(8,128)(2,1)} %collective-permute-done.2.xtp_ref, ...), custom_call_target="tpu_custom_call" | custom-call | tf_op jit(solution)/shard_map/wgrad0/pallas_call | solution.py:186
  66.0 3.3 %collective-permute-start.4 = (bf16[3,96,384]{2,1,0:T(8,128)(2,1)S(1)}, bf16[3,96,384]{2,1,0:T(8,128)(2,1)S(1)}, u32[]{:S(2)}, u32[]{:S(2)}) collective-permute-start(bf16[3,96,384]{2,1,0:T(8,128)(2,1)S(1)} %get-tuple-element.46), channel_id=1, source_target_pairs={{0,1},{1,2},{2,3},{3,0},{4,5},{5,6},{6,7},{7,4},{8,9},{9,10},{10,1... | collective-permute-start | bytes 663560 | tf_op jit(solution)/shard_map/ppermute | solution.py:270
  70.8 5.4 %dgrad.1 = bf16[512,768]{1,0:T(8,128)(2,1)} custom-call(s32[3]{0:T(128)S(1)} %pad_add_fusion.place_ref, bf16[512,768]{1,0:T(8,128)(2,1)} %get-tuple-element.44.g_ref, bf16[512,768]{1,0:T(8,128)(2,1)} %collective-permute-done.3.gp_ref, bf16[32,768]{1,0:T(8,128)(2,1)S(1)} %collective-permute-done.10.out_ref, ...), custom_call_target="tpu_custom_call" | custom-call | tf_op jit(solution)/shard_map/dgrad/pallas_call | solution.py:239
  76.2 3.1 %collective-permute-done.5.refs_2_ = bf16[3,96,384]{2,1,0:T(8,128)(2,1)S(1)} collective-permute-done((bf16[3,96,384]{2,1,0:T(8,128)(2,1)S(1)}, bf16[3,96,384]{2,1,0:T(8,128)(2,1)S(1)}, u32[]{:S(2)}, u32[]{:S(2)}) %collective-permute-start.5) | collective-permute-done | bytes 221216 | tf_op jit(solution)/shard_map/ppermute | solution.py:270
  79.3 4.7 %collective-permute-done.6.refs_3_ = bf16[3,96,384]{2,1,0:T(8,128)(2,1)S(1)} collective-permute-done((bf16[3,96,384]{2,1,0:T(8,128)(2,1)S(1)}, bf16[3,96,384]{2,1,0:T(8,128)(2,1)S(1)}, u32[]{:S(2)}, u32[]{:S(2)}) %collective-permute-start.6) | collective-permute-done | bytes 221216 | tf_op jit(solution)/shard_map/ppermute | solution.py:270
  84.2 3.4 %collective-permute-start.11 = (bf16[3,24,768]{2,1,0:T(8,128)(2,1)S(1)}, bf16[3,24,768]{2,1,0:T(8,128)(2,1)S(1)}, u32[]{:S(2)}, u32[]{:S(2)}) collective-permute-start(bf16[3,24,768]{2,1,0:T(8,128)(2,1)S(1)} %get-tuple-element.60), channel_id=1, source_target_pairs={{0,8},{8,16},{16,24},{24,0},{1,9},{9,17},{17,25},{25,1},{2,10},{10... | collective-permute-start | bytes 331784 | tf_op jit(solution)/shard_map/ppermute | solution.py:270
  87.6 2.7 %collective-permute-start.12 = (bf16[3,24,768]{2,1,0:T(8,128)(2,1)S(1)}, bf16[3,24,768]{2,1,0:T(8,128)(2,1)S(1)}, u32[]{:S(2)}, u32[]{:S(2)}) collective-permute-start(bf16[3,24,768]{2,1,0:T(8,128)(2,1)S(1)} %get-tuple-element.61), channel_id=1, source_target_pairs={{0,16},{8,24},{16,0},{24,8},{1,17},{9,25},{17,1},{25,9},{2,18},{10... | collective-permute-start | bytes 331784 | tf_op jit(solution)/shard_map/ppermute | solution.py:270
  90.3 1.5 %collective-permute-start.13 = (bf16[3,24,768]{2,1,0:T(8,128)(2,1)S(1)}, bf16[3,24,768]{2,1,0:T(8,128)(2,1)S(1)}, u32[]{:S(2)}, u32[]{:S(2)}) collective-permute-start(bf16[3,24,768]{2,1,0:T(8,128)(2,1)S(1)} %get-tuple-element.62), channel_id=1, source_target_pairs={{0,24},{8,0},{16,8},{24,16},{1,25},{9,1},{17,9},{25,17},{2,26},{10... | collective-permute-start | bytes 331784 | tf_op jit(solution)/shard_map/ppermute | solution.py:270
  92.2 3.5 %collective-permute-done.12 = bf16[3,24,768]{2,1,0:T(8,128)(2,1)S(1)} collective-permute-done((bf16[3,24,768]{2,1,0:T(8,128)(2,1)S(1)}, bf16[3,24,768]{2,1,0:T(8,128)(2,1)S(1)}, u32[]{:S(2)}, u32[]{:S(2)}) %collective-permute-start.12) | collective-permute-done | bytes 110624 | tf_op jit(solution)/shard_map/ppermute | solution.py:270
  96.6 6.5 %all-to-all-start.2 = ((bf16[8,3,3,768]{3,2,1,0:T(4,128)(2,1)}), bf16[8,3,3,768]{3,2,1,0:T(4,128)(2,1)S(1)}, u32[]{:S(2)}, u32[]{:S(2)}) async-start(bf16[8,3,3,768]{3,2,1,0:T(4,128)(2,1)} %copy.11), calls=%async_computation.2 | async-start | bytes 294912 | tf_op jit(solution)/shard_map/all_to_all | solution.py:316
  103.2 3.7 %convolution_convert_fusion = bf16[512,1536]{1,0:T(8,128)(2,1)} fusion(bf16[512,768]{1,0:T(8,128)(2,1)} %bitcast.15, bf16[768,1536]{1,0:T(8,128)(2,1)S(1)} %copy-done), kind=kOutput, calls=%fused_computation | convolution fusion | flops 1208745984 | bytes 4718592 | tf_op jit(solution)/shard_map/dot_general | solution.py:315
  106.8 5.6 %all-to-all-done.2 = bf16[8,3,3,768]{3,2,1,0:T(4,128)(2,1)S(1)} async-done(((bf16[8,3,3,768]{3,2,1,0:T(4,128)(2,1)}), bf16[8,3,3,768]{3,2,1,0:T(4,128)(2,1)S(1)}, u32[]{:S(2)}, u32[]{:S(2)}) %all-to-all-start.2) | async-done | bytes 110624 | tf_op jit(solution)/shard_map/all_to_all | solution.py:316
  113.2 2.3 %collective-permute-start.15 = (bf16[3,3,768]{2,1,0:T(4,128)(2,1)S(1)}, bf16[3,3,768]{2,1,0:T(4,128)(2,1)S(1)}, u32[]{:S(2)}, u32[]{:S(2)}) collective-permute-start(bf16[3,3,768]{2,1,0:T(4,128)(2,1)S(1)} %reduce_sum.12), channel_id=1, source_target_pairs={{0,2},{1,3},{2,0},{3,1},{4,6},{5,7},{6,4},{7,5},{8,10},{9,11},{10,... | collective-permute-start | bytes 41480 | tf_op jit(solution)/shard_map/ppermute | solution.py:270
  116.3 2.2 %collective-permute-done.15 = bf16[3,3,768]{2,1,0:T(4,128)(2,1)S(1)} collective-permute-done((bf16[3,3,768]{2,1,0:T(4,128)(2,1)S(1)}, bf16[3,3,768]{2,1,0:T(4,128)(2,1)S(1)}, u32[]{:S(2)}, u32[]{:S(2)}) %collective-permute-start.15) | collective-permute-done | bytes 13856 | tf_op jit(solution)/shard_map/ppermute | solution.py:270
  118.5 2.0 %collective-permute-done.16 = bf16[3,3,768]{2,1,0:T(4,128)(2,1)S(1)} collective-permute-done((bf16[3,3,768]{2,1,0:T(4,128)(2,1)S(1)}, bf16[3,3,768]{2,1,0:T(4,128)(2,1)S(1)}, u32[]{:S(2)}, u32[]{:S(2)}) %collective-permute-start.16) | collective-permute-done | bytes 13856 | tf_op jit(solution)/shard_map/ppermute | solution.py:270
  (63 shorter events, 16.1 us)
Async XLA Ops:
  2.6 4.5 %collective-permute-start = (bf16[32,896]{1,0:T(8,128)(2,1)S(1)}, bf16[32,896]{1,0:T(8,128)(2,1)S(1)}, u32[]{:S(2)}, u32[]{:S(2)}) collective-permute-start(bf16[32,896]{1,0:T(8,128)(2,1)S(1)} %get-tuple-element.75), channel_id=1, source_target_pairs={{0,4},{4,0},{1,5},{5,1},{2,6},{6,2},{3,7},{7,3},{8,12},{12,8},{9,1... | collective-permute-start | bytes 172040 | tf_op jit(solution)/shard_map/ppermute | solution.py:256
  2.7 4.4 %collective-permute-start.1 = (bf16[32,896]{1,0:T(8,128)(2,1)S(1)}, bf16[32,896]{1,0:T(8,128)(2,1)S(1)}, u32[]{:S(2)}, u32[]{:S(2)}) collective-permute-start(bf16[32,896]{1,0:T(8,128)(2,1)S(1)} %get-tuple-element.74), channel_id=1, source_target_pairs={{8,4},{16,12},{24,20},{32,28},{40,36},{48,44},{56,52},{64,60},{72,... | collective-permute-start | bytes 172040 | tf_op jit(solution)/shard_map/ppermute | solution.py:262
  7.1 15.3 %copy-start.10 = (s32[1,512]{1,0:T(1,128)S(1)}, s32[1,512]{1,0:T(1,128)}, u32[]{:S(2)}) copy-start(s32[1,512]{1,0:T(1,128)} %ids_ref.1) | copy-start | bytes 6148
  7.1 15.3 %copy-start.11 = (s32[1,256,1]{1,2,0:T(1,128)S(1)}, s32[1,256,1]{1,2,0:T(1,128)}, u32[]{:S(2)}) copy-start(s32[1,256,1]{1,2,0:T(1,128)} %param.8) | copy-start | bytes 3076
  7.1 38.5 %all-to-all-start = ((bf16[64,8,768]{2,1,0:T(8,128)(2,1)}), bf16[64,8,768]{2,1,0:T(8,128)(2,1)S(1)}, u32[]{:S(2)}, u32[]{:S(2)}) async-start(bf16[64,8,768]{2,1,0:T(8,128)(2,1)} %bitcast.51), calls=%async_computation | async-start | bytes 1572864 | tf_op jit(solution)/shard_map/all_to_all | solution.py:294
  40.0 15.0 %collective-permute-start.2 = (bf16[3,384,512]{2,1,0:T(8,128)(2,1)}, bf16[3,384,512]{2,1,0:T(8,128)(2,1)}, u32[]{:S(2)}, u32[]{:S(2)}) collective-permute-start(bf16[3,384,512]{2,1,0:T(8,128)(2,1)} %get-tuple-element.39), channel_id=1, source_target_pairs={{0,4},{4,0},{1,5},{5,1},{2,6},{6,2},{3,7},{7,3},{8,12},{12,8},{9,1... | collective-permute-start | bytes 3538952 | tf_op jit(solution)/shard_map/ppermute | solution.py:256
  48.9 6.1 %collective-permute-start.3 = (bf16[512,768]{1,0:T(8,128)(2,1)}, bf16[512,768]{1,0:T(8,128)(2,1)}, u32[]{:S(2)}, u32[]{:S(2)}) collective-permute-start(bf16[512,768]{1,0:T(8,128)(2,1)} %get-tuple-element.44.g_ref), channel_id=1, source_target_pairs={{0,4},{4,0},{1,5},{5,1},{2,6},{6,2},{3,7},{7,3},{8,12},{12,8},{9,1... | collective-permute-start | bytes 2359304 | tf_op jit(solution)/shard_map/ppermute | solution.py:256
  48.9 47.0 %all-to-all-start.1 = ((bf16[64,8,768]{2,1,0:T(8,128)(2,1)}), bf16[64,8,768]{2,1,0:T(8,128)(2,1)}, u32[]{:S(2)}, u32[]{:S(2)}) async-start(bf16[64,8,768]{2,1,0:T(8,128)(2,1)} %bitcast.48), calls=%async_computation.1 | async-start | bytes 1572864 | tf_op jit(solution)/shard_map/all_to_all | solution.py:304
  56.3 14.5 %copy-start.5 = (bf16[512,1280]{1,0:T(8,128)(2,1)S(1)}, bf16[512,1280]{1,0:T(8,128)(2,1)}, u32[]{:S(2)}) copy-start(bf16[512,1280]{1,0:T(8,128)(2,1)} %copy-done.3) | copy-start | bytes 3932164
  59.2 10.2 %collective-permute-start.7 = (bf16[3,96,384]{2,1,0:T(8,128)(2,1)S(1)}, bf16[3,96,384]{2,1,0:T(8,128)(2,1)S(1)}, u32[]{:S(2)}, u32[]{:S(2)}) collective-permute-start(bf16[3,96,384]{2,1,0:T(8,128)(2,1)S(1)} %get-tuple-element.50), channel_id=1, source_target_pairs={{0,1},{1,2},{2,3},{3,0},{4,5},{5,6},{6,7},{7,4},{8,9},{9,10},{10,1... | collective-permute-start | bytes 663560 | tf_op jit(solution)/shard_map/ppermute | solution.py:270
  59.8 9.5 %collective-permute-start.10 = (bf16[32,768]{1,0:T(8,128)(2,1)S(1)}, bf16[32,768]{1,0:T(8,128)(2,1)S(1)}, u32[]{:S(2)}, u32[]{:S(2)}) collective-permute-start(bf16[32,768]{1,0:T(8,128)(2,1)S(1)} %get-tuple-element.57), channel_id=1, source_target_pairs={{8,4},{16,12},{24,20},{32,28},{40,36},{48,44},{56,52},{64,60},{72,... | collective-permute-start | bytes 147464 | tf_op jit(solution)/shard_map/ppermute | solution.py:262
  60.4 15.7 %collective-permute-start.8 = (bf16[3,96,384]{2,1,0:T(8,128)(2,1)S(1)}, bf16[3,96,384]{2,1,0:T(8,128)(2,1)S(1)}, u32[]{:S(2)}, u32[]{:S(2)}) collective-permute-start(bf16[3,96,384]{2,1,0:T(8,128)(2,1)S(1)} %get-tuple-element.51), channel_id=1, source_target_pairs={{0,2},{1,3},{2,0},{3,1},{4,6},{5,7},{6,4},{7,5},{8,10},{9,11},{10,... | collective-permute-start | bytes 663560 | tf_op jit(solution)/shard_map/ppermute | solution.py:270
  63.0 7.8 %copy-start.2 = (bf16[768,3,768]{2,0,1:T(8,128)(2,1)S(1)}, bf16[768,3,768]{2,0,1:T(8,128)(2,1)}, u32[]{:S(2)}) copy-start(bf16[768,3,768]{2,0,1:T(8,128)(2,1)} %param.9) | copy-start | bytes 10616836
  63.0 13.2 %collective-permute-start.9 = (bf16[3,96,384]{2,1,0:T(8,128)(2,1)S(1)}, bf16[3,96,384]{2,1,0:T(8,128)(2,1)S(1)}, u32[]{:S(2)}, u32[]{:S(2)}) collective-permute-start(bf16[3,96,384]{2,1,0:T(8,128)(2,1)S(1)} %get-tuple-element.52), channel_id=1, source_target_pairs={{0,3},{1,0},{2,1},{3,2},{4,7},{5,4},{6,5},{7,6},{8,11},{9,8},{10,9... | collective-permute-start | bytes 663560 | tf_op jit(solution)/shard_map/ppermute | solution.py:270
  66.0 10.2 %collective-permute-start.4 = (bf16[3,96,384]{2,1,0:T(8,128)(2,1)S(1)}, bf16[3,96,384]{2,1,0:T(8,128)(2,1)S(1)}, u32[]{:S(2)}, u32[]{:S(2)}) collective-permute-start(bf16[3,96,384]{2,1,0:T(8,128)(2,1)S(1)} %get-tuple-element.46), channel_id=1, source_target_pairs={{0,1},{1,2},{2,3},{3,0},{4,5},{5,6},{6,7},{7,4},{8,9},{9,10},{10,1... | collective-permute-start | bytes 663560 | tf_op jit(solution)/shard_map/ppermute | solution.py:270
  69.3 10.0 %collective-permute-start.5 = (bf16[3,96,384]{2,1,0:T(8,128)(2,1)S(1)}, bf16[3,96,384]{2,1,0:T(8,128)(2,1)S(1)}, u32[]{:S(2)}, u32[]{:S(2)}) collective-permute-start(bf16[3,96,384]{2,1,0:T(8,128)(2,1)S(1)} %get-tuple-element.47), channel_id=1, source_target_pairs={{0,2},{1,3},{2,0},{3,1},{4,6},{5,7},{6,4},{7,5},{8,10},{9,11},{10,... | collective-permute-start | bytes 663560 | tf_op jit(solution)/shard_map/ppermute | solution.py:270
  69.4 14.6 %collective-permute-start.6 = (bf16[3,96,384]{2,1,0:T(8,128)(2,1)S(1)}, bf16[3,96,384]{2,1,0:T(8,128)(2,1)S(1)}, u32[]{:S(2)}, u32[]{:S(2)}) collective-permute-start(bf16[3,96,384]{2,1,0:T(8,128)(2,1)S(1)} %get-tuple-element.48), channel_id=1, source_target_pairs={{0,3},{1,0},{2,1},{3,2},{4,7},{5,4},{6,5},{7,6},{8,11},{9,8},{10,9... | collective-permute-start | bytes 663560 | tf_op jit(solution)/shard_map/ppermute | solution.py:270
  84.2 8.0 %collective-permute-start.11 = (bf16[3,24,768]{2,1,0:T(8,128)(2,1)S(1)}, bf16[3,24,768]{2,1,0:T(8,128)(2,1)S(1)}, u32[]{:S(2)}, u32[]{:S(2)}) collective-permute-start(bf16[3,24,768]{2,1,0:T(8,128)(2,1)S(1)} %get-tuple-element.60), channel_id=1, source_target_pairs={{0,8},{8,16},{16,24},{24,0},{1,9},{9,17},{17,25},{25,1},{2,10},{10... | collective-permute-start | bytes 331784 | tf_op jit(solution)/shard_map/ppermute | solution.py:270
  87.6 8.1 %collective-permute-start.12 = (bf16[3,24,768]{2,1,0:T(8,128)(2,1)S(1)}, bf16[3,24,768]{2,1,0:T(8,128)(2,1)S(1)}, u32[]{:S(2)}, u32[]{:S(2)}) collective-permute-start(bf16[3,24,768]{2,1,0:T(8,128)(2,1)S(1)} %get-tuple-element.61), channel_id=1, source_target_pairs={{0,16},{8,24},{16,0},{24,8},{1,17},{9,25},{17,1},{25,9},{2,18},{10... | collective-permute-start | bytes 331784 | tf_op jit(solution)/shard_map/ppermute | solution.py:270
  90.3 5.5 %collective-permute-start.13 = (bf16[3,24,768]{2,1,0:T(8,128)(2,1)S(1)}, bf16[3,24,768]{2,1,0:T(8,128)(2,1)S(1)}, u32[]{:S(2)}, u32[]{:S(2)}) collective-permute-start(bf16[3,24,768]{2,1,0:T(8,128)(2,1)S(1)} %get-tuple-element.62), channel_id=1, source_target_pairs={{0,24},{8,0},{16,8},{24,16},{1,25},{9,1},{17,9},{25,17},{2,26},{10... | collective-permute-start | bytes 331784 | tf_op jit(solution)/shard_map/ppermute | solution.py:270
  96.6 15.8 %all-to-all-start.2 = ((bf16[8,3,3,768]{3,2,1,0:T(4,128)(2,1)}), bf16[8,3,3,768]{3,2,1,0:T(4,128)(2,1)S(1)}, u32[]{:S(2)}, u32[]{:S(2)}) async-start(bf16[8,3,3,768]{3,2,1,0:T(4,128)(2,1)} %copy.11), calls=%async_computation.2 | async-start | bytes 294912 | tf_op jit(solution)/shard_map/all_to_all | solution.py:316
  112.5 3.8 %collective-permute-start.14 = (bf16[3,3,768]{2,1,0:T(4,128)(2,1)S(1)}, bf16[3,3,768]{2,1,0:T(4,128)(2,1)S(1)}, u32[]{:S(2)}, u32[]{:S(2)}) collective-permute-start(bf16[3,3,768]{2,1,0:T(4,128)(2,1)S(1)} %reduce_sum.12), channel_id=1, source_target_pairs={{0,1},{1,2},{2,3},{3,0},{4,5},{5,6},{6,7},{7,4},{8,9},{9,10},{10,1... | collective-permute-start | bytes 41480 | tf_op jit(solution)/shard_map/ppermute | solution.py:270
  113.2 5.3 %collective-permute-start.15 = (bf16[3,3,768]{2,1,0:T(4,128)(2,1)S(1)}, bf16[3,3,768]{2,1,0:T(4,128)(2,1)S(1)}, u32[]{:S(2)}, u32[]{:S(2)}) collective-permute-start(bf16[3,3,768]{2,1,0:T(4,128)(2,1)S(1)} %reduce_sum.12), channel_id=1, source_target_pairs={{0,2},{1,3},{2,0},{3,1},{4,6},{5,7},{6,4},{7,5},{8,10},{9,11},{10,... | collective-permute-start | bytes 41480 | tf_op jit(solution)/shard_map/ppermute | solution.py:270
  115.6 5.0 %collective-permute-start.16 = (bf16[3,3,768]{2,1,0:T(4,128)(2,1)S(1)}, bf16[3,3,768]{2,1,0:T(4,128)(2,1)S(1)}, u32[]{:S(2)}, u32[]{:S(2)}) collective-permute-start(bf16[3,3,768]{2,1,0:T(4,128)(2,1)S(1)} %reduce_sum.12), channel_id=1, source_target_pairs={{0,3},{1,0},{2,1},{3,2},{4,7},{5,4},{6,5},{7,6},{8,11},{9,8},{10,9... | collective-permute-start | bytes 41480 | tf_op jit(solution)/shard_map/ppermute | solution.py:270
  (8 other events, 11.4 us)
